TPU v7x, 32 devices: a whole 2x2x4 slice. The times are simulated.
32 devices in a mesh: tm: 8 (over y, x, core), space: 4 (over z).
Axes of the slice: x: 2, y: 2, z: 4, core: 2. Of those that a mesh axis runs over, the one named last changes fastest.
Arguments:
- eigen_vectors: bfloat16 [8, 2, 128, 3, 2048], P(None, None, 'tm', None, 'space'), may hold values from -90 to 90
- propagators: bfloat16 [8, 2, 128, 3, 2048], P('tm', None, None, None, 'space'), may hold values from -6 to 6
Outputs:
- perambulator: float32 [8, 128, 8, 2, 128], P(None, 'space', 'tm')
All inputs are finite; a program needn't handle non-finite values.
Results may differ from a plain program's by a relative error of at most 0.0026.
Values may be sent and summed in bfloat16 or wider, within the bound.
No kernel may reach another device: no remote copies, remote signals or barrier semaphores. Data moves between devices by JAX's collectives and lax.ppermute only.
A program may use at most 64 MiB of HBM per device.

v0:
```python
import math

import jax
import jax.numpy as jnp
from jax import lax
from jax.sharding import PartitionSpec as P

LS = 64


momenta_table = (
    (0, 0, 0),
    (1, 0, 0),
    (0, 1, 0),
    (0, 0, 1),
    (1, 1, 0),
    (1, 0, 1),
    (0, 1, 1),
    (1, 1, 1),
)
epsilon_norm = 1e-06


def phase_tables(first_site, count, momentum):
    positions = first_site + jnp.arange(count, dtype=jnp.int32)
    coord_z = positions % LS
    coord_y = positions // LS % LS
    coord_x = positions // (LS * LS)
    wave = (momentum[0] * coord_x + momentum[1] * coord_y + momentum[2] * coord_z) % LS
    phase_angle = wave.astype(jnp.float32) * (2.0 * math.pi / LS)
    return (jnp.cos(phase_angle), jnp.sin(phase_angle))


def project(vectors, columns, cosine, sine):
    slices = vectors.shape[0]
    real_in = vectors[:, 0].astype(jnp.float32)
    imag_in = vectors[:, 1].astype(jnp.float32)
    w_real = (cosine * real_in - sine * imag_in).astype(jnp.bfloat16)
    w_imag = (-(sine * real_in + cosine * imag_in)).astype(jnp.bfloat16)
    left = jnp.stack([w_real, w_imag], 1)
    left = left.reshape(slices, 2, left.shape[2], -1)
    right = columns.reshape(slices, 2, columns.shape[2], -1)
    products = jnp.einsum("tcek,tdak->etcda", left, right, preferred_element_type=jnp.float32)
    real_out = products[:, :, 0, 0] - products[:, :, 1, 1]
    imag_out = products[:, :, 0, 1] + products[:, :, 1, 0]
    return jnp.stack([real_out, imag_out], 2)


def per_device(eigen_vectors, propagators):
    vectors = lax.all_to_all(eigen_vectors, "tm", split_axis=0, concat_axis=2, tiled=True)
    sites_local = vectors.shape[4]
    eigen_total = vectors.shape[2]
    eigen_local = eigen_total // lax.axis_size("space")
    first_site = lax.axis_index("space") * sites_local
    local_squares = jnp.sum(jnp.square(vectors.astype(jnp.float32)), axis=(1, 3, 4))
    squares = lax.psum(local_squares, "space")
    inverse = lax.rsqrt(squares + epsilon_norm)
    my_rows = lax.dynamic_slice_in_dim(
        inverse, lax.axis_index("space") * eigen_local, eigen_local, 1
    )
    row_scale = jnp.transpose(my_rows)[:, :, None, None]
    results = []
    for momentum in momenta_table:
        cosine, sine = phase_tables(first_site, sites_local, momentum)
        summed = lax.psum_scatter(
            project(vectors, propagators, cosine, sine), "space", scatter_dimension=0, tiled=True
        )
        results.append(summed * row_scale)
    return jnp.stack(results, 0)


def solution(mesh):
    placed = (P(None, None, "tm", None, "space"), P("tm", None, None, None, "space"))
    return jax.shard_map(
        per_device,
        mesh=mesh,
        in_specs=placed,
        out_specs=P(None, "space", "tm", None, None),
        check_vma=False,
    )
```

profile of v0, /device:TPU:0, one launch (start us, length us, event | category | flops | bytes accessed | tf_op | source)
XLA Modules:
  0.0 194.0 jit_solution(6654774041449049947)
XLA Ops:
  6.5 5.3 %all-to-all-start = ((bf16[8,2,16,3,512]{4,2,3,1,0:T(8,128)(2,1)}), bf16[8,2,16,3,512]{4,2,3,1,0:T(8,128)(2,1)S(1)}, u32[]{:S(2)}, u32[]{:S(2)}) async-start(bf16[8,2,16,3,512]{4,2,3,1,0:T(8,128)(2,1)} %param.2), calls=%async_computation | async-start | bytes 1572864 | tf_op jit(solution)/shard_map/all_to_all | solution.py:50
  12.0 1.2 copy.52
  15.9 8.6 %all-to-all-done = bf16[8,2,16,3,512]{4,2,3,1,0:T(8,128)(2,1)S(1)} async-done(((bf16[8,2,16,3,512]{4,2,3,1,0:T(8,128)(2,1)}), bf16[8,2,16,3,512]{4,2,3,1,0:T(8,128)(2,1)S(1)}, u32[]{:S(2)}, u32[]{:S(2)}) %all-to-all-start) | async-done | bytes 786464 | tf_op jit(solution)/shard_map/all_to_all | solution.py:50
  27.1 1.5 convolution_bitcast_fusion.7
  32.1 1.5 fusion.17
  33.6 1.9 copy.60
  35.5 1.9 %copy.62 = bf16[1,1,128,1536]{3,2,1,0:T(8,128)(2,1)} copy(bf16[1,1,128,1536]{2,3,1,0:T(8,128)(2,1)} %bitcast.193) | data formatting | bytes 786432 | tf_op jit(solution)/shard_map/stack | solution.py:40
  38.3 2.0 %copy.61 = bf16[1,1,128,1536]{3,2,1,0:T(8,128)(2,1)} copy(bf16[1,1,128,1536]{2,3,1,0:T(8,128)(2,1)} %bitcast.194) | data formatting | bytes 786432 | tf_op jit(solution)/shard_map/stack | solution.py:40
  40.3 2.4 %convolution_bitcast_fusion.5 = f32[128,1,2,2,128]{4,0,3,2,1:T(8,128)} fusion(bf16[2,128,1536,1]{1,2,0,3:T(8,128)(2,1)} %bitcast.206, bf16[1,1,128,1536]{3,2,1,0:T(8,128)(2,1)S(1)} %copy-done.6, bf16[1,1,128,1536]{3,2,1,0:T(8,128)(2,1)} %copy.61), kind=kOutput, calls=%fused_computation.38 | convolution fusion | flops 202899456 | bytes 1835008 | tf_op jit(solution)/shard_map/tcek,tdak->etcda/dot_general | solution.py:43
  46.0 2.2 %convolution_bitcast_fusion.4 = f32[128,1,2,2,128]{4,0,3,2,1:T(8,128)} fusion(bf16[2,128,1536,1]{1,2,0,3:T(8,128)(2,1)} %bitcast.207, bf16[1,1,128,1536]{3,2,1,0:T(8,128)(2,1)S(1)} %copy-done.4, bf16[1,1,128,1536]{3,2,1,0:T(8,128)(2,1)S(1)} %copy.66), kind=kOutput, calls=%fused_computation.37 | convolution fusion | flops 202899456 | bytes 1835008 | tf_op jit(solution)/shard_map/tcek,tdak->etcda/dot_general | solution.py:43
  49.7 1.6 fusion.63
  51.4 1.1 convolution_bitcast_fusion.3
  52.5 1.5 fusion.32
  54.7 1.2 copy.75
  57.5 2.2 %convolution_bitcast_fusion.2 = f32[128,1,2,2,128]{4,0,3,2,1:T(8,128)} fusion(bf16[2,128,1536,1]{1,2,0,3:T(8,128)(2,1)} %bitcast.208, bf16[1,1,128,1536]{3,2,1,0:T(8,128)(2,1)S(1)} %copy.77, bf16[1,1,128,1536]{3,2,1,0:T(8,128)(2,1)S(1)} %copy.76), kind=kOutput, calls=%fused_computation.35 | convolution fusion | flops 202899456 | bytes 1835008 | tf_op jit(solution)/shard_map/tcek,tdak->etcda/dot_general | solution.py:43
  61.3 1.0 fusion.59
  62.3 1.1 convolution_bitcast_fusion.1
  66.9 11.9 %psum.7 = f32[1,128]{1,0:T(1,128)S(1)} all-reduce(f32[1,128]{1,0:T(1,128)S(1)} %reduce_sum.12), channel_id=1, replica_groups=mesh['tm'=8,'space'=4] {'space'}, use_global_device_ids=true, to_apply=%region_2.3 | all-reduce | flops 128 | bytes 1024 | tf_op jit(solution)/shard_map/psum | solution.py:56
  81.4 6.0 %reduce-scatter.13.cloned.1.call-done = f32[32,1,2,128]{3,0,2,1:T(8,128)} async-done(((f32[128,1,2,128]{3,0,2,1:T(8,128)}), f32[32,1,2,128]{3,0,2,1:T(8,128)}) %reduce-scatter.13.cloned.1.call-update) | async-done | bytes 32784 | tf_op jit(solution)/shard_map/reduce_scatter | solution.py:65
  88.3 18.8 %reduce-scatter.15.cloned.1.call-done = f32[32,1,2,128]{3,0,2,1:T(8,128)} async-done(((f32[128,1,2,128]{3,0,2,1:T(8,128)}), f32[32,1,2,128]{3,0,2,1:T(8,128)}) %reduce-scatter.15.cloned.1.call-update) | async-done | bytes 32784 | tf_op jit(solution)/shard_map/reduce_scatter | solution.py:65
  107.9 18.6 %reduce-scatter.17.cloned.1.call-done = f32[32,1,2,128]{3,0,2,1:T(8,128)} async-done(((f32[128,1,2,128]{3,0,2,1:T(8,128)}), f32[32,1,2,128]{3,0,2,1:T(8,128)}) %reduce-scatter.17.cloned.1.call-update) | async-done | bytes 32784 | tf_op jit(solution)/shard_map/reduce_scatter | solution.py:65
  127.3 18.8 %reduce-scatter.19.cloned.1.call-done = f32[32,1,2,128]{3,0,2,1:T(8,128)} async-done(((f32[128,1,2,128]{3,0,2,1:T(8,128)}), f32[32,1,2,128]{3,0,2,1:T(8,128)}) %reduce-scatter.19.cloned.1.call-update) | async-done | bytes 32784 | tf_op jit(solution)/shard_map/reduce_scatter | solution.py:65
  146.9 18.8 %reduce-scatter.21.cloned.1.call-done = f32[32,1,2,128]{3,0,2,1:T(8,128)} async-done(((f32[128,1,2,128]{3,0,2,1:T(8,128)}), f32[32,1,2,128]{3,0,2,1:T(8,128)}) %reduce-scatter.21.cloned.1.call-update) | async-done | bytes 32784 | tf_op jit(solution)/shard_map/reduce_scatter | solution.py:65
  166.5 18.9 %reduce-scatter.23.cloned.1.call-done = f32[32,1,2,128]{3,0,2,1:T(8,128)} async-done(((f32[128,1,2,128]{3,0,2,1:T(8,128)}), f32[32,1,2,128]{3,0,2,1:T(8,128)}) %reduce-scatter.23.cloned.1.call-update) | async-done | bytes 32784 | tf_op jit(solution)/shard_map/reduce_scatter | solution.py:65
  (124 shorter events, 30.1 us)
Async XLA Ops:
  6.5 5.4 %copy-start = (bf16[1,2,128,3,512]{4,2,3,1,0:T(8,128)(2,1)S(1)}, bf16[1,2,128,3,512]{4,2,3,1,0:T(8,128)(2,1)}, u32[]{:S(2)}) copy-start(bf16[1,2,128,3,512]{4,2,3,1,0:T(8,128)(2,1)} %param.3) | copy-start | bytes 2359300
  6.5 17.9 %all-to-all-start = ((bf16[8,2,16,3,512]{4,2,3,1,0:T(8,128)(2,1)}), bf16[8,2,16,3,512]{4,2,3,1,0:T(8,128)(2,1)S(1)}, u32[]{:S(2)}, u32[]{:S(2)}) async-start(bf16[8,2,16,3,512]{4,2,3,1,0:T(8,128)(2,1)} %param.2), calls=%async_computation | async-start | bytes 1572864 | tf_op jit(solution)/shard_map/all_to_all | solution.py:50
  11.8 67.9 %reduce-scatter.9.cloned.1.call-start = ((), (), s32[]{:S(2)}) async-start(), calls=%async_computation.9 | async-start | bytes 163840 | tf_op jit(solution)/shard_map/reduce_scatter | solution.py:65
  29.4 51.2 %reduce-scatter.11.cloned.1.call-start = ((), (), s32[]{:S(2)}) async-start(), calls=%async_computation.10 | async-start | bytes 163840 | tf_op jit(solution)/shard_map/reduce_scatter | solution.py:65
  29.8 1.1 copy-start.1
  31.0 1.1 copy-start.17
  31.0 1.1 copy-start.18
  31.0 1.1 copy-start.19
  38.3 2.0 %copy-start.6 = (bf16[1,1,128,1536]{3,2,1,0:T(8,128)(2,1)S(1)}, bf16[1,1,128,1536]{3,2,1,0:T(8,128)(2,1)}, u32[]{:S(2)}) copy-start(bf16[1,1,128,1536]{3,2,1,0:T(8,128)(2,1)} %copy.62) | copy-start | bytes 1179652
  40.3 2.4 %copy-start.10 = (f32[128,1,1,128]{3,0,2,1:T(8,128)S(1)}, f32[128,1,1,128]{3,0,2,1:T(8,128)}, u32[]{:S(2)}) copy-start(f32[128,1,1,128]{3,0,2,1:T(8,128)} %get-tuple-element.41) | copy-start | bytes 196612
  40.3 2.4 %copy-start.11 = (f32[128,1,1,128]{3,0,2,1:T(8,128)S(1)}, f32[128,1,1,128]{3,0,2,1:T(8,128)}, u32[]{:S(2)}) copy-start(f32[128,1,1,128]{3,0,2,1:T(8,128)} %get-tuple-element.42) | copy-start | bytes 196612
  44.8 1.2 copy-start.4
  45.9 41.5 %reduce-scatter.13.cloned.1.call-start = ((), (), s32[]{:S(2)}) async-start(), calls=%async_computation.11 | async-start | bytes 163840 | tf_op jit(solution)/shard_map/reduce_scatter | solution.py:65
  49.5 1.9 copy-start.2
  51.4 55.7 %reduce-scatter.15.cloned.1.call-start = ((), (), s32[]{:S(2)}) async-start(), calls=%async_computation.12 | async-start | bytes 163840 | tf_op jit(solution)/shard_map/reduce_scatter | solution.py:65
  51.4 1.1 copy-start.12
  51.4 1.1 copy-start.13
  52.5 1.5 copy-start.8
  52.5 1.5 copy-start.9
  57.5 69.0 %reduce-scatter.17.cloned.1.call-start = ((), (), s32[]{:S(2)}) async-start(), calls=%async_computation.13 | async-start | bytes 163840 | tf_op jit(solution)/shard_map/reduce_scatter | solution.py:65
  61.1 1.3 copy-start.3
  62.3 83.8 %reduce-scatter.19.cloned.1.call-start = ((), (), s32[]{:S(2)}) async-start(), calls=%async_computation.14 | async-start | bytes 163840 | tf_op jit(solution)/shard_map/reduce_scatter | solution.py:65
  65.5 100.2 %reduce-scatter.21.cloned.1.call-start = ((), (), s32[]{:S(2)}) async-start(), calls=%async_computation.15 | async-start | bytes 163840 | tf_op jit(solution)/shard_map/reduce_scatter | solution.py:65
  78.9 106.6 %reduce-scatter.23.cloned.1.call-start = ((), (), s32[]{:S(2)}) async-start(), calls=%async_computation.16 | async-start | bytes 163840 | tf_op jit(solution)/shard_map/reduce_scatter | solution.py:65
  (5 other events, 5.2 us)
Sparse Core Ops, SparseCore 0:
  29.5 18.5 reduce-scatter.8
  50.4 17.3 reduce-scatter.10
  70.0 17.3 reduce-scatter.12
  89.6 17.3 reduce-scatter.14
  109.1 17.3 reduce-scatter.16
  128.7 17.3 reduce-scatter.18
  148.3 17.3 reduce-scatter.20
  168.0 17.3 reduce-scatter.22
where the time goes:
time: 195 us; the launch traced here: 194 us
  waiting for transfers between devices  109 us (56%)
  other arithmetic  23.6 us (12%)
  local copies, waits for them, and re-layouts  19.1 us (10%)
  between operations  13.9 us (7%)
  blocking collectives  11.9 us (6%)
  matrix products  11.2 us (6%)
  starting transfers between devices  5.63 us (3%)
    reduce_scatter x8, waiting for transfers between devices, per_device(): lax.psum_scatter(project(vectors, propagators, cosine, sine), 'space', sc...  99.9 us
    psum x1, blocking collectives, per_device(): squares = lax.psum(local_squares, 'space')  11.9 us
    dot_general x8, matrix products, project(): jnp.einsum('tcek,tdak->etcda', left, right, preferred_element_type=jnp.fl...  11.2 us
    all_to_all x1, waiting for transfers between devices, per_device(): lax.all_to_all(eigen_vectors, 'tm', split_axis=0, concat_axis=2, tiled=True)  8.55 us
    another operation x16, local copies, waits for them, and re-layouts, project(): left = jnp.stack([w_real, w_imag], 1)  8.03 us
    unnamed x7, other arithmetic  5.81 us
    another operation x8, other arithmetic, project(): return jnp.stack([real_out, imag_out], 2)  5.31 us
    all_to_all x1, starting transfers between devices, per_device(): lax.all_to_all(eigen_vectors, 'tm', split_axis=0, concat_axis=2, tiled=True)  5.3 us
  transfers between devices with their start and end apart: 9, of which 7 were waited for; matrix products, arithmetic and copies ran while one was open for 24% of the time, Pallas kernels for 0%

commit v1 on v0

v1 whole, which is shorter than its diff:
```python
import functools
import math

import jax
import jax.numpy as jnp
import numpy as np
from jax import lax
from jax.experimental import pallas as pl
from jax.experimental.pallas import tpu as pltpu
from jax.sharding import PartitionSpec as P

LS = 64
LANES = 128

momenta_table = (
    (0, 0, 0),
    (1, 0, 0),
    (0, 1, 0),
    (0, 0, 1),
    (1, 1, 0),
    (1, 0, 1),
    (0, 1, 1),
    (1, 1, 1),
)
epsilon_norm = 1e-06


def window_waves(sites):
    positions = np.arange(sites)
    coords = np.stack([positions // (LS * LS), positions // LS % LS, positions % LS])
    return (np.asarray(momenta_table) @ coords) % LS


def distinct_rows(waves):
    rows, group = [], []
    for wave in waves:
        for known, row in enumerate(rows):
            if np.array_equal(row, wave):
                group.append(known)
                break
        else:
            group.append(len(rows))
            rows.append(wave)
    return np.stack(rows), tuple(group)


def trig_tables(waves):
    angle = waves.astype(np.float32) * np.float32(2.0 * math.pi / LS)
    return np.cos(angle).astype(np.float32), np.sin(angle).astype(np.float32)


def columns_kernel(p_ref, r_ref):
    cols, sites = p_ref.shape[2], p_ref.shape[3]
    for colour in range(p_ref.shape[1]):
        real = p_ref[0, colour].T
        imag = p_ref[1, colour].T
        r_ref[colour, :sites, :cols] = real
        r_ref[colour, :sites, cols:] = imag
        r_ref[colour, sites:, :cols] = -imag
        r_ref[colour, sites:, cols:] = real


def half_kernel(trivial, where_ref, tab_ref, r_ref, *refs):
    pieces = len(trivial[1])
    groups = len(trivial[0])
    v_refs, out_refs = refs[:pieces], refs[pieces : 2 * pieces]
    acc_ref, w_refs = refs[2 * pieces], refs[2 * pieces + 1 :]
    colours, rows, sites = v_refs[0].shape[1:]
    cols = r_ref.shape[2] // 2
    squares = [None] * pieces
    total = None
    for colour in range(colours):
        w_ref = w_refs[colour]
        for k, v_ref in enumerate(v_refs):
            real = v_ref[0, colour].astype(jnp.float32)
            imag = v_ref[1, colour].astype(jnp.float32)
            square = real * real + imag * imag
            square = sum(square[:, at : at + LANES] for at in range(0, sites, LANES))
            squares[k] = square if squares[k] is None else squares[k] + square
            for g in range(groups):
                at = (g * pieces + k) * rows
                if trivial[0][g]:
                    w_real, w_imag = real, -imag
                else:
                    cosine = tab_ref[2 * g : 2 * g + 1, :]
                    sine = tab_ref[2 * g + 1 : 2 * g + 2, :]
                    w_real = cosine * real - sine * imag
                    w_imag = -(sine * real + cosine * imag)
                w_ref[at : at + rows, :sites] = w_real.astype(jnp.bfloat16)
                w_ref[at : at + rows, sites:] = w_imag.astype(jnp.bfloat16)
        part = jnp.dot(w_ref[...], r_ref[colour], preferred_element_type=jnp.float32)
        total = part if total is None else total + part
    acc_ref[: groups * pieces * rows, :cols] = total[:, :cols]
    acc_ref[: groups * pieces * rows, cols:] = total[:, cols:]
    lane = lax.broadcasted_iota(jnp.int32, (rows, LANES), 1)
    for k in range(pieces):
        whole = jnp.broadcast_to(jnp.sum(squares[k], axis=1, keepdims=True), (rows, LANES))
        high = whole.astype(jnp.bfloat16).astype(jnp.float32)
        at = (groups * pieces + k) * rows
        acc_ref[at : at + rows, :LANES] = jnp.where(lane < LANES // 2, high, whole - high)
    for q in range(pieces):
        k = jnp.bitwise_xor(where_ref[0], q)
        out_ref = out_refs[q]
        for g in range(groups):
            at = pl.multiple_of((g * pieces + k) * rows, rows)
            for part in range(2):
                out_ref[2 * g + part] = acc_ref[
                    pl.ds(at, rows), part * cols : (part + 1) * cols
                ].astype(out_ref.dtype)
        at = pl.multiple_of((groups * pieces + k) * rows, rows)
        out_ref[2 * groups] = acc_ref[pl.ds(at, rows), :LANES].astype(out_ref.dtype)


def finish_kernel(group, core_ref, *refs):
    out_ref = refs[-1]
    per_half = (len(refs) - 1) // 2
    tiles, rows, cols = refs[0].shape
    for half in range(2):
        parts = refs[half * per_half : (half + 1) * per_half]
        first = pl.multiple_of(jnp.bitwise_xor(core_ref[0], half) * (2 * rows), 2 * rows)

        def summed(tile):
            value = parts[0][tile].astype(jnp.float32)
            for ref in parts[1:]:
                value = value + ref[tile].astype(jnp.float32)
            return value

        both = summed(tiles - 1)
        squares = both[:, :1] + both[:, LANES // 2 : LANES // 2 + 1]
        inverse = lax.rsqrt(squares + epsilon_norm)
        for g in range((tiles - 1) // 2):
            for part in range(2):
                value = summed(2 * g + part) * inverse
                for m, mine in enumerate(group):
                    if mine == g:
                        at = m * 4 * rows + first + part
                        out_ref[pl.ds(at, rows, stride=2), :] = value


def in_vmem(count):
    return [pl.BlockSpec(memory_space=pltpu.VMEM)] * count


def scalar():
    return [pl.BlockSpec(memory_space=pltpu.SMEM)]


def per_device_permutes(eigen_vectors, propagators):
    tm, space = lax.axis_size("tm"), lax.axis_size("space")
    me, z = lax.axis_index("tm"), lax.axis_index("space")
    rows, sites = eigen_vectors.shape[2], eigen_vectors.shape[4]
    cols = propagators.shape[2]
    waves, group = distinct_rows(window_waves(sites * space))
    groups = len(waves)
    trivial = tuple(not wave.any() for wave in waves)
    cosine, sine = trig_tables(waves)
    tables = np.stack([cosine, sine], 1).reshape(2 * groups, space, sites).transpose(1, 0, 2)
    table = lax.dynamic_index_in_dim(jnp.asarray(tables), z, 0, keepdims=False)

    vectors = jnp.transpose(eigen_vectors, (0, 1, 3, 2, 4))
    columns = jnp.transpose(propagators[0], (0, 2, 1, 3))
    colours = vectors.shape[2]

    def piece(r):
        mine = lax.dynamic_index_in_dim(vectors, jnp.bitwise_xor(me, r), 0, keepdims=False)
        if r == 0:
            return mine
        return lax.ppermute(mine, "tm", [(i, i ^ r) for i in range(tm)])

    right = pl.pallas_call(
        columns_kernel,
        out_shape=jax.ShapeDtypeStruct((colours, 2 * sites, 2 * cols), jnp.bfloat16),
        in_specs=in_vmem(1),
        out_specs=in_vmem(1)[0],
        cost_estimate=pl.CostEstimate(flops=0, bytes_accessed=3 * 2**20, transcendentals=0),
        compiler_params=pltpu.CompilerParams(vmem_limit_bytes=16 * 2**20),
    )(columns)

    where = jnp.bitwise_xor(me // 2, z).astype(jnp.int32).reshape(1)
    core = (me % 2).astype(jnp.int32).reshape(1)
    tiles = 2 * groups + 1
    out_tile = lambda dtype: jax.ShapeDtypeStruct((tiles, rows, cols), dtype)
    half = pl.pallas_call(
        functools.partial(half_kernel, (trivial, (None,) * space)),
        out_shape=[out_tile(jnp.float32)] + [out_tile(jnp.bfloat16)] * (space - 1),
        in_specs=scalar() + in_vmem(2 + space),
        out_specs=in_vmem(space),
        scratch_shapes=[pltpu.VMEM(((groups + 1) * space * rows, 2 * cols), jnp.float32)]
        + [pltpu.VMEM((groups * space * rows, 2 * sites), jnp.bfloat16)] * colours,
        cost_estimate=pl.CostEstimate(
            flops=2 * groups * space * rows * colours * 2 * sites * 2 * cols,
            bytes_accessed=2 * 2**20,
            transcendentals=0,
        ),
        compiler_params=pltpu.CompilerParams(vmem_limit_bytes=24 * 2**20),
    )
    sent = [[piece(r) for r in range(first, tm, 2)] for first in range(2)]
    parts = []
    for pieces in sent:
        own, *others = half(where, table, right, *pieces)
        parts.append(own)
        for q, other in enumerate(others, 1):
            parts.append(lax.ppermute(other, "space", [(i, i ^ q) for i in range(space)]))
    out = pl.pallas_call(
        functools.partial(finish_kernel, group),
        out_shape=jax.ShapeDtypeStruct((len(group) * 2 * rows * 2, cols), jnp.float32),
        in_specs=scalar() + in_vmem(len(parts)),
        out_specs=in_vmem(1)[0],
        cost_estimate=pl.CostEstimate(flops=2**20, bytes_accessed=2**20, transcendentals=0),
        compiler_params=pltpu.CompilerParams(vmem_limit_bytes=16 * 2**20),
    )(core, *parts)
    return out.reshape(len(group), 2 * rows, 1, 2, cols)


def project(vectors, columns, cosine, sine):
    slices = vectors.shape[0]
    real_in = vectors[:, 0].astype(jnp.float32)
    imag_in = vectors[:, 1].astype(jnp.float32)
    w_real = (cosine * real_in - sine * imag_in).astype(jnp.bfloat16)
    w_imag = (-(sine * real_in + cosine * imag_in)).astype(jnp.bfloat16)
    left = jnp.stack([w_real, w_imag], 1)
    left = left.reshape(slices, 2, left.shape[2], -1)
    right = columns.reshape(slices, 2, columns.shape[2], -1)
    products = jnp.einsum("tcek,tdak->etcda", left, right, preferred_element_type=jnp.float32)
    real_out = products[:, :, 0, 0] - products[:, :, 1, 1]
    imag_out = products[:, :, 0, 1] + products[:, :, 1, 0]
    return jnp.stack([real_out, imag_out], 2)


def per_device_general(eigen_vectors, propagators):
    vectors = lax.all_to_all(eigen_vectors, "tm", split_axis=0, concat_axis=2, tiled=True)
    sites = vectors.shape[4]
    space = lax.axis_size("space")
    rows = vectors.shape[2] // space
    z = lax.axis_index("space")
    squares = lax.psum(jnp.sum(jnp.square(vectors.astype(jnp.float32)), axis=(1, 3, 4)), "space")
    inverse = lax.rsqrt(squares + epsilon_norm)
    mine = lax.dynamic_slice_in_dim(inverse, z * rows, rows, 1)
    row_scale = jnp.transpose(mine)[:, :, None, None]
    waves, group = distinct_rows(window_waves(sites * space))
    positions = z * sites + jnp.arange(sites, dtype=jnp.int32)
    coords = (positions // (LS * LS), positions // LS % LS, positions % LS)
    results = []
    for g in range(len(waves)):
        momentum = momenta_table[group.index(g)]
        wave = sum(n * x for n, x in zip(momentum, coords)) % LS
        angle = wave.astype(jnp.float32) * (2.0 * math.pi / LS)
        sums = project(vectors, propagators, jnp.cos(angle), jnp.sin(angle))
        sums = lax.psum_scatter(sums, "space", scatter_dimension=0, tiled=True)
        results.append(sums * row_scale)
    return jnp.stack([results[g] for g in group], 0)


def solution(mesh):
    tm, space = mesh.shape["tm"], mesh.shape["space"]

    def per_device(eigen_vectors, propagators):
        rows, sites = eigen_vectors.shape[2], eigen_vectors.shape[4]
        fits = (
            tm == 2 * space
            and space & (space - 1) == 0
            and eigen_vectors.shape[0] == tm
            and rows % 16 == 0
            and sites % LANES == 0
            and propagators.shape[2] == LANES
        )
        form = per_device_permutes if fits else per_device_general
        return form(eigen_vectors, propagators)

    placed = (P(None, None, "tm", None, "space"), P("tm", None, None, None, "space"))
    return jax.shard_map(
        per_device,
        mesh=mesh,
        in_specs=placed,
        out_specs=P(None, "space", "tm", None, None),
        check_vma=False,
    )
```

time: 195 us -> 33.4 us (0.17)
  waiting for transfers between devices: 109 us -> 9.94 us
  other arithmetic: 23.6 us -> 0 us
  local copies, waits for them, and re-layouts: 19.1 us -> 2.72 us
  between operations: 13.9 us -> 0.05 us
  starting transfers between devices: 5.63 us -> 18.1 us
  blocking collectives: 11.9 us -> 0 us
  matrix products: 11.2 us -> 0 us
  Pallas kernels: 0 us -> 2.37 us
    reduce_scatter x8 -> x0, waiting for transfers between devices: 99.9 us -> none  [per_device(): lax.psum_scatter(project(vectors, propagators, cosine, sine), 'space', sc...]
    ppermute x0 -> x13, starting transfers between devices: none -> 18.1 us  [the longest x7 9.18 us: piece(): return lax.ppermute(mine, 'tm', [(i, i ^ r) for i in range(tm)])]
    psum x1 -> x0, blocking collectives: 11.9 us -> none  [per_device(): squares = lax.psum(local_squares, 'space')]
    dot_general x8 -> x0, matrix products: 11.2 us -> none  [project(): jnp.einsum('tcek,tdak->etcda', left, right, preferred_element_type=jnp.fl...]
    ppermute x0 -> x13, waiting for transfers between devices: none -> 9.94 us  [the longest x6 5.54 us: per_device_permutes(): lax.ppermute(other, 'space', [(i, i ^ q) for i in range(space)])]
    another operation x17 -> x0, local copies, waits for them, and re-layouts: 8.94 us -> none  [the longest x16 8.03 us: project(): left = jnp.stack([w_real, w_imag], 1)]
    all_to_all x1 -> x0, waiting for transfers between devices: 8.55 us -> none  [per_device(): lax.all_to_all(eigen_vectors, 'tm', split_axis=0, concat_axis=2, tiled=True)]
    convert_element_type x16 -> x0, local copies, waits for them, and re-layouts: 6.88 us -> none  [the longest x8 4.43 us: project(): w_imag = (-(sine * real_in + cosine * imag_in)).astype(jnp.bfloat16)]
  transfers between devices with their start and end apart: 9 -> 13, of which waited for: 7 -> 5; matrix products, arithmetic and copies ran while one was open for 24% -> 2% of each run, Pallas kernels for 0% -> 5%
where the time goes in v1:
time: 33.4 us; the launch traced here: 33.2 us
  starting transfers between devices  18.1 us (54%)
  waiting for transfers between devices  9.94 us (30%)
  local copies, waits for them, and re-layouts  2.72 us (8%)
  Pallas kernels  2.37 us (7%)
    ppermute x7, starting transfers between devices, piece(): return lax.ppermute(mine, 'tm', [(i, i ^ r) for i in range(tm)])  9.18 us
    ppermute x6, starting transfers between devices, per_device_permutes(): lax.ppermute(other, 'space', [(i, i ^ q) for i in range(space)])  8.91 us
    ppermute x6, waiting for transfers between devices, per_device_permutes(): lax.ppermute(other, 'space', [(i, i ^ q) for i in range(space)])  5.54 us
    ppermute x7, waiting for transfers between devices, piece(): return lax.ppermute(mine, 'tm', [(i, i ^ r) for i in range(tm)])  4.4 us
    squeeze x1, local copies, waits for them, and re-layouts, piece(): lax.dynamic_index_in_dim(vectors, jnp.bitwise_xor(me, r), 0, keepdims=False)  2 us
    pallas_call x2, Pallas kernels, per_device_permutes(): own, *others = half(where, table, right, *pieces)  1.24 us
    pallas_call x1, Pallas kernels, per_device_permutes(): pl.pallas_call(functools.partial(finish_kernel, group), out_shape=jax.Sha...  0.87 us
    squeeze x1, local copies, waits for them, and re-layouts, per_device_permutes(): table = lax.dynamic_index_in_dim(jnp.asarray(tables), z, 0, keepdims=False)  0.72 us
  transfers between devices with their start and end apart: 13, of which 5 were waited for; matrix products, arithmetic and copies ran while one was open for 2% of the time, Pallas kernels for 5%

profile of v1, /device:TPU:0, one launch (start us, length us, event | category | flops | bytes accessed | tf_op | source)
XLA Modules:
  0.0 33.2 jit_solution(13050599247545068962)
XLA Ops:
  0.0 2.0 %dynamic-slice_bitcast_fusion = (bf16[2,3,16,512]{3,2,1,0:T(8,128)(2,1)}, bf16[2,3,16,512]{3,2,1,0:T(8,128)(2,1)S(1)}, bf16[2,3,16,512]{3,2,1,0:T(8,128)(2,1)S(1...) fusion(bf16[8,2,16,3,512]{4,2,3,1,0:T(8,128)(2,1)} %param.3, ...), kind=kLoop, calls=%fused_computation | loop fusion | bytes 1572896 | tf_op jit(solution)/shard_map/jit(dynamic_index_in_dim)/squeeze | solution.py:165
  2.0 3.3 %collective-permute-start.9 = (bf16[2,3,16,512]{3,2,1,0:T(8,128)(2,1)}, bf16[2,3,16,512]{3,2,1,0:T(8,128)(2,1)S(1)}, u32[]{:S(2)}, u32[]{:S(2)}) collective-permute-start(bf16[2,3,16,512]{3,2,1,0:T(8,128)(2,1)} %get-tuple-element.21), channel_id=1, source_target_pairs={{0,28},{4,24},{8,20},{12,16},{16,12},{20,8},{24,4},{28,0},{1,29},{... | collective-permute-start | bytes 294920 | tf_op jit(solution)/shard_map/ppermute | solution.py:168
  5.3 0.8 %collective-permute-start.7 = (bf16[2,3,16,512]{3,2,1,0:T(8,128)(2,1)S(1)}, bf16[2,3,16,512]{3,2,1,0:T(8,128)(2,1)S(1)}, u32[]{:S(2)}, u32[]{:S(2)}) collective-permute-start(bf16[2,3,16,512]{3,2,1,0:T(8,128)(2,1)S(1)} %get-tuple-element.22), channel_id=1, source_target_pairs={{0,12},{4,8},{8,4},{12,0},{16,28},{20,24},{24,20},{28,16},{1,13},{... | collective-permute-start | bytes 294920 | tf_op jit(solution)/shard_map/ppermute | solution.py:168
  6.2 0.0 collective-permute-start.6
  6.2 1.4 %collective-permute-start.2 = (bf16[2,3,16,512]{3,2,1,0:T(8,128)(2,1)S(1)}, bf16[2,3,16,512]{3,2,1,0:T(8,128)(2,1)S(1)}, u32[]{:S(2)}, u32[]{:S(2)}) collective-permute-start(bf16[2,3,16,512]{3,2,1,0:T(8,128)(2,1)S(1)} %get-tuple-element.24), channel_id=1, source_target_pairs={{0,24},{4,28},{8,16},{12,20},{16,8},{20,12},{24,0},{28,4},{1,25},{... | collective-permute-start | bytes 294920 | tf_op jit(solution)/shard_map/ppermute | solution.py:168
  7.6 1.5 %collective-permute-start.1 = (bf16[2,3,16,512]{3,2,1,0:T(8,128)(2,1)S(1)}, bf16[2,3,16,512]{3,2,1,0:T(8,128)(2,1)S(1)}, u32[]{:S(2)}, u32[]{:S(2)}) collective-permute-start(bf16[2,3,16,512]{3,2,1,0:T(8,128)(2,1)S(1)} %get-tuple-element.25), channel_id=1, source_target_pairs={{0,16},{4,20},{8,24},{12,28},{16,0},{20,4},{24,8},{28,12},{1,17},{... | collective-permute-start | bytes 294920 | tf_op jit(solution)/shard_map/ppermute | solution.py:168
  9.1 0.3 shard_map.37.r_ref
  9.4 1.8 %collective-permute-start = (bf16[2,3,16,512]{3,2,1,0:T(8,128)(2,1)S(1)}, bf16[2,3,16,512]{3,2,1,0:T(8,128)(2,1)S(1)}, u32[]{:S(2)}, u32[]{:S(2)}) collective-permute-start(bf16[2,3,16,512]{3,2,1,0:T(8,128)(2,1)S(1)} %get-tuple-element.26), channel_id=1, source_target_pairs={{0,8},{4,12},{8,0},{12,4},{16,24},{20,28},{24,16},{28,20},{1,9},{5... | collective-permute-start | bytes 294920 | tf_op jit(solution)/shard_map/ppermute | solution.py:168
  11.2 0.6 %collective-permute-done.7.refs_1_ = bf16[2,3,16,512]{3,2,1,0:T(8,128)(2,1)S(1)} collective-permute-done((bf16[2,3,16,512]{3,2,1,0:T(8,128)(2,1)S(1)}, bf16[2,3,16,512]{3,2,1,0:T(8,128)(2,1)S(1)}, u32[]{:S(2)}, u32[]{:S(2)}) %collective-permute-start.7) | collective-permute-done | bytes 98336 | tf_op jit(solution)/shard_map/ppermute | solution.py:168
  11.8 0.3 collective-permute-start.8
  12.1 0.7 %dynamic-slice_bitcast_fusion.8.tab_ref = f32[8,512]{1,0:T(8,128)S(1)} fusion(f32[4,8,512]{2,1,0:T(8,128)} %constant.69.clone, s32[]{:T(128)S(6)} %select_n.42), kind=kLoop, calls=%fused_computation.8 | loop fusion | bytes 32772 | tf_op jit(solution)/shard_map/jit(dynamic_index_in_dim)/squeeze | solution.py:158
  12.8 3.8 %collective-permute-done.8.refs_2_ = bf16[2,3,16,512]{3,2,1,0:T(8,128)(2,1)S(1)} collective-permute-done((bf16[2,3,16,512]{3,2,1,0:T(8,128)(2,1)S(1)}, bf16[2,3,16,512]{3,2,1,0:T(8,128)(2,1)S(1)}, u32[]{:S(2)}, u32[]{:S(2)}) %collective-permute-start.8) | collective-permute-done | bytes 98336 | tf_op jit(solution)/shard_map/ppermute | solution.py:168
  16.6 0.6 %shard_map.39 = (f32[9,16,128]{2,1,0:T(8,128)S(1)}, bf16[9,16,128]{2,1,0:T(8,128)(2,1)S(1)}, bf16[9,16,128]{2,1,0:T(8,128)(2,1)S(1)}, bf16[9,16,128]{2,1,0:T(8,128)(2,1)S(1)}) custom-call(s32[1]{0:T(128)} %bitcast.1.where_ref, f32[8,512]{1,0:T(8,128)S(1)} %dynamic-slice_bitcast_fusion.8.tab_ref, bf16[3,1024,256]{2,1,0:T(8,128)(2,1)S(1)} %shard_map.37.r_ref, ...), custom_call_target="tpu_custom_call" | custom-call | flops 402653184 | bytes 2097152 | tf_op jit(solution)/shard_map/pallas_call | solution.py:200
  17.2 1.6 %collective-permute-start.10 = (bf16[9,16,128]{2,1,0:T(8,128)(2,1)S(1)}, bf16[9,16,128]{2,1,0:T(8,128)(2,1)S(1)}, u32[]{:S(2)}, u32[]{:S(2)}) collective-permute-start(bf16[9,16,128]{2,1,0:T(8,128)(2,1)S(1)} %get-tuple-element.18), channel_id=1, source_target_pairs={{0,1},{1,0},{2,3},{3,2},{4,5},{5,4},{6,7},{7,6},{8,9},{9,8},{10,11... | collective-permute-start | bytes 110600 | tf_op jit(solution)/shard_map/ppermute | solution.py:203
  18.9 2.6 %collective-permute-start.11 = (bf16[9,16,128]{2,1,0:T(8,128)(2,1)S(1)}, bf16[9,16,128]{2,1,0:T(8,128)(2,1)S(1)}, u32[]{:S(2)}, u32[]{:S(2)}) collective-permute-start(bf16[9,16,128]{2,1,0:T(8,128)(2,1)S(1)} %get-tuple-element.19), channel_id=1, source_target_pairs={{0,2},{1,3},{2,0},{3,1},{4,6},{5,7},{6,4},{7,5},{8,10},{9,11},{10,... | collective-permute-start | bytes 110600 | tf_op jit(solution)/shard_map/ppermute | solution.py:203
  21.4 0.2 collective-permute-start.12
  21.7 0.6 %shard_map.38 = (f32[9,16,128]{2,1,0:T(8,128)S(1)}, bf16[9,16,128]{2,1,0:T(8,128)(2,1)S(1)}, bf16[9,16,128]{2,1,0:T(8,128)(2,1)S(1)}, bf16[9,16,128]{2,1,0:T(8,128)(2,1)S(1)}) custom-call(s32[1]{0:T(128)} %bitcast.1.where_ref, f32[8,512]{1,0:T(8,128)S(1)} %dynamic-slice_bitcast_fusion.8.tab_ref, bf16[3,1024,256]{2,1,0:T(8,128)(2,1)S(1)} %shard_map.37.r_ref, ...), custom_call_target="tpu_custom_call" | custom-call | flops 402653184 | bytes 2097152 | tf_op jit(solution)/shard_map/pallas_call | solution.py:200
  22.3 0.8 %collective-permute-start.3 = (bf16[9,16,128]{2,1,0:T(8,128)(2,1)S(1)}, bf16[9,16,128]{2,1,0:T(8,128)(2,1)S(1)}, u32[]{:S(2)}, u32[]{:S(2)}) collective-permute-start(bf16[9,16,128]{2,1,0:T(8,128)(2,1)S(1)} %get-tuple-element.14), channel_id=1, source_target_pairs={{0,1},{1,0},{2,3},{3,2},{4,5},{5,4},{6,7},{7,6},{8,9},{9,8},{10,11... | collective-permute-start | bytes 110600 | tf_op jit(solution)/shard_map/ppermute | solution.py:203
  23.1 3.5 %collective-permute-start.4 = (bf16[9,16,128]{2,1,0:T(8,128)(2,1)S(1)}, bf16[9,16,128]{2,1,0:T(8,128)(2,1)S(1)}, u32[]{:S(2)}, u32[]{:S(2)}) collective-permute-start(bf16[9,16,128]{2,1,0:T(8,128)(2,1)S(1)} %get-tuple-element.15), channel_id=1, source_target_pairs={{0,2},{1,3},{2,0},{3,1},{4,6},{5,7},{6,4},{7,5},{8,10},{9,11},{10,... | collective-permute-start | bytes 110600 | tf_op jit(solution)/shard_map/ppermute | solution.py:203
  26.5 0.2 collective-permute-start.5
  26.8 0.7 %collective-permute-done.12.refs_7_ = bf16[9,16,128]{2,1,0:T(8,128)(2,1)S(1)} collective-permute-done((bf16[9,16,128]{2,1,0:T(8,128)(2,1)S(1)}, bf16[9,16,128]{2,1,0:T(8,128)(2,1)S(1)}, u32[]{:S(2)}, u32[]{:S(2)}) %collective-permute-start.12) | collective-permute-done | bytes 36896 | tf_op jit(solution)/shard_map/ppermute | solution.py:203
  27.4 1.4 %collective-permute-done.4.refs_2_ = bf16[9,16,128]{2,1,0:T(8,128)(2,1)S(1)} collective-permute-done((bf16[9,16,128]{2,1,0:T(8,128)(2,1)S(1)}, bf16[9,16,128]{2,1,0:T(8,128)(2,1)S(1)}, u32[]{:S(2)}, u32[]{:S(2)}) %collective-permute-start.4) | collective-permute-done | bytes 36896 | tf_op jit(solution)/shard_map/ppermute | solution.py:203
  28.9 3.4 %collective-permute-done.5.refs_3_ = bf16[9,16,128]{2,1,0:T(8,128)(2,1)S(1)} collective-permute-done((bf16[9,16,128]{2,1,0:T(8,128)(2,1)S(1)}, bf16[9,16,128]{2,1,0:T(8,128)(2,1)S(1)}, u32[]{:S(2)}, u32[]{:S(2)}) %collective-permute-start.5) | collective-permute-done | bytes 36896 | tf_op jit(solution)/shard_map/ppermute | solution.py:203
  32.3 0.9 %shard_map.40 = f32[512,128]{1,0:T(8,128)} custom-call(s32[1]{0:T(128)} %bitcast.core_ref, f32[9,16,128]{2,1,0:T(8,128)S(1)} %get-tuple-element.13.refs_0_, bf16[9,16,128]{2,1,0:T(8,128)(2,1)S(1)} %collective-permute-done.3.refs_1_, bf16[9,16,128]{2,1,0:T(8,128)(2,1)S(1)} %collective-permute-done.4.refs_2_, ...), custom_call_target="tpu_custom_call" | custom-call | flops 1048576 | bytes 1048576 | tf_op jit(solution)/shard_map/pallas_call | solution.py:204
  (10 shorter events, 0.0 us)
Async XLA Ops:
  0.0 9.1 %copy-start = (bf16[1,2,128,3,512]{4,2,3,1,0:T(8,128)(2,1)S(1)}, bf16[1,2,128,3,512]{4,2,3,1,0:T(8,128)(2,1)}, u32[]{:S(2)}) copy-start(bf16[1,2,128,3,512]{4,2,3,1,0:T(8,128)(2,1)} %param.4) | copy-start | bytes 2359300
  2.0 7.4 %collective-permute-start.9 = (bf16[2,3,16,512]{3,2,1,0:T(8,128)(2,1)}, bf16[2,3,16,512]{3,2,1,0:T(8,128)(2,1)S(1)}, u32[]{:S(2)}, u32[]{:S(2)}) collective-permute-start(bf16[2,3,16,512]{3,2,1,0:T(8,128)(2,1)} %get-tuple-element.21), channel_id=1, source_target_pairs={{0,28},{4,24},{8,20},{12,16},{16,12},{20,8},{24,4},{28,0},{1,29},{... | collective-permute-start | bytes 294920 | tf_op jit(solution)/shard_map/ppermute | solution.py:168
  5.3 6.5 %collective-permute-start.7 = (bf16[2,3,16,512]{3,2,1,0:T(8,128)(2,1)S(1)}, bf16[2,3,16,512]{3,2,1,0:T(8,128)(2,1)S(1)}, u32[]{:S(2)}, u32[]{:S(2)}) collective-permute-start(bf16[2,3,16,512]{3,2,1,0:T(8,128)(2,1)S(1)} %get-tuple-element.22), channel_id=1, source_target_pairs={{0,12},{4,8},{8,4},{12,0},{16,28},{20,24},{24,20},{28,16},{1,13},{... | collective-permute-start | bytes 294920 | tf_op jit(solution)/shard_map/ppermute | solution.py:168
  6.2 6.7 %collective-permute-start.6 = (bf16[2,3,16,512]{3,2,1,0:T(8,128)(2,1)S(1)}, bf16[2,3,16,512]{3,2,1,0:T(8,128)(2,1)S(1)}, u32[]{:S(2)}, u32[]{:S(2)}) collective-permute-start(bf16[2,3,16,512]{3,2,1,0:T(8,128)(2,1)S(1)} %get-tuple-element.23), channel_id=1, source_target_pairs={{0,4},{4,0},{8,12},{12,8},{16,20},{20,16},{24,28},{28,24},{1,5},{5... | collective-permute-start | bytes 294920 | tf_op jit(solution)/shard_map/ppermute | solution.py:168
  6.2 15.3 %collective-permute-start.2 = (bf16[2,3,16,512]{3,2,1,0:T(8,128)(2,1)S(1)}, bf16[2,3,16,512]{3,2,1,0:T(8,128)(2,1)S(1)}, u32[]{:S(2)}, u32[]{:S(2)}) collective-permute-start(bf16[2,3,16,512]{3,2,1,0:T(8,128)(2,1)S(1)} %get-tuple-element.24), channel_id=1, source_target_pairs={{0,24},{4,28},{8,16},{12,20},{16,8},{20,12},{24,0},{28,4},{1,25},{... | collective-permute-start | bytes 294920 | tf_op jit(solution)/shard_map/ppermute | solution.py:168
  7.6 14.1 %collective-permute-start.1 = (bf16[2,3,16,512]{3,2,1,0:T(8,128)(2,1)S(1)}, bf16[2,3,16,512]{3,2,1,0:T(8,128)(2,1)S(1)}, u32[]{:S(2)}, u32[]{:S(2)}) collective-permute-start(bf16[2,3,16,512]{3,2,1,0:T(8,128)(2,1)S(1)} %get-tuple-element.25), channel_id=1, source_target_pairs={{0,16},{4,20},{8,24},{12,28},{16,0},{20,4},{24,8},{28,12},{1,17},{... | collective-permute-start | bytes 294920 | tf_op jit(solution)/shard_map/ppermute | solution.py:168
  9.4 12.3 %collective-permute-start = (bf16[2,3,16,512]{3,2,1,0:T(8,128)(2,1)S(1)}, bf16[2,3,16,512]{3,2,1,0:T(8,128)(2,1)S(1)}, u32[]{:S(2)}, u32[]{:S(2)}) collective-permute-start(bf16[2,3,16,512]{3,2,1,0:T(8,128)(2,1)S(1)} %get-tuple-element.26), channel_id=1, source_target_pairs={{0,8},{4,12},{8,0},{12,4},{16,24},{20,28},{24,16},{28,20},{1,9},{5... | collective-permute-start | bytes 294920 | tf_op jit(solution)/shard_map/ppermute | solution.py:168
  11.8 4.8 %collective-permute-start.8 = (bf16[2,3,16,512]{3,2,1,0:T(8,128)(2,1)S(1)}, bf16[2,3,16,512]{3,2,1,0:T(8,128)(2,1)S(1)}, u32[]{:S(2)}, u32[]{:S(2)}) collective-permute-start(bf16[2,3,16,512]{3,2,1,0:T(8,128)(2,1)S(1)} %get-tuple-element.28), channel_id=1, source_target_pairs={{0,20},{4,16},{8,28},{12,24},{16,4},{20,0},{24,12},{28,8},{1,21},{... | collective-permute-start | bytes 294920 | tf_op jit(solution)/shard_map/ppermute | solution.py:168
  17.2 9.3 %collective-permute-start.10 = (bf16[9,16,128]{2,1,0:T(8,128)(2,1)S(1)}, bf16[9,16,128]{2,1,0:T(8,128)(2,1)S(1)}, u32[]{:S(2)}, u32[]{:S(2)}) collective-permute-start(bf16[9,16,128]{2,1,0:T(8,128)(2,1)S(1)} %get-tuple-element.18), channel_id=1, source_target_pairs={{0,1},{1,0},{2,3},{3,2},{4,5},{5,4},{6,7},{7,6},{8,9},{9,8},{10,11... | collective-permute-start | bytes 110600 | tf_op jit(solution)/shard_map/ppermute | solution.py:203
  18.9 7.9 %collective-permute-start.11 = (bf16[9,16,128]{2,1,0:T(8,128)(2,1)S(1)}, bf16[9,16,128]{2,1,0:T(8,128)(2,1)S(1)}, u32[]{:S(2)}, u32[]{:S(2)}) collective-permute-start(bf16[9,16,128]{2,1,0:T(8,128)(2,1)S(1)} %get-tuple-element.19), channel_id=1, source_target_pairs={{0,2},{1,3},{2,0},{3,1},{4,6},{5,7},{6,4},{7,5},{8,10},{9,11},{10,... | collective-permute-start | bytes 110600 | tf_op jit(solution)/shard_map/ppermute | solution.py:203
  21.4 6.0 %collective-permute-start.12 = (bf16[9,16,128]{2,1,0:T(8,128)(2,1)S(1)}, bf16[9,16,128]{2,1,0:T(8,128)(2,1)S(1)}, u32[]{:S(2)}, u32[]{:S(2)}) collective-permute-start(bf16[9,16,128]{2,1,0:T(8,128)(2,1)S(1)} %get-tuple-element.20), channel_id=1, source_target_pairs={{0,3},{1,2},{2,1},{3,0},{4,7},{5,6},{6,5},{7,4},{8,11},{9,10},{10,... | collective-permute-start | bytes 110600 | tf_op jit(solution)/shard_map/ppermute | solution.py:203
  22.3 5.1 %collective-permute-start.3 = (bf16[9,16,128]{2,1,0:T(8,128)(2,1)S(1)}, bf16[9,16,128]{2,1,0:T(8,128)(2,1)S(1)}, u32[]{:S(2)}, u32[]{:S(2)}) collective-permute-start(bf16[9,16,128]{2,1,0:T(8,128)(2,1)S(1)} %get-tuple-element.14), channel_id=1, source_target_pairs={{0,1},{1,0},{2,3},{3,2},{4,5},{5,4},{6,7},{7,6},{8,9},{9,8},{10,11... | collective-permute-start | bytes 110600 | tf_op jit(solution)/shard_map/ppermute | solution.py:203
  23.1 5.8 %collective-permute-start.4 = (bf16[9,16,128]{2,1,0:T(8,128)(2,1)S(1)}, bf16[9,16,128]{2,1,0:T(8,128)(2,1)S(1)}, u32[]{:S(2)}, u32[]{:S(2)}) collective-permute-start(bf16[9,16,128]{2,1,0:T(8,128)(2,1)S(1)} %get-tuple-element.15), channel_id=1, source_target_pairs={{0,2},{1,3},{2,0},{3,1},{4,6},{5,7},{6,4},{7,5},{8,10},{9,11},{10,... | collective-permute-start | bytes 110600 | tf_op jit(solution)/shard_map/ppermute | solution.py:203
  26.5 5.8 %collective-permute-start.5 = (bf16[9,16,128]{2,1,0:T(8,128)(2,1)S(1)}, bf16[9,16,128]{2,1,0:T(8,128)(2,1)S(1)}, u32[]{:S(2)}, u32[]{:S(2)}) collective-permute-start(bf16[9,16,128]{2,1,0:T(8,128)(2,1)S(1)} %get-tuple-element.16), channel_id=1, source_target_pairs={{0,3},{1,2},{2,1},{3,0},{4,7},{5,6},{6,5},{7,4},{8,11},{9,10},{10,... | collective-permute-start | bytes 110600 | tf_op jit(solution)/shard_map/ppermute | solution.py:203

commit v2 on v1

--- a/solution.py
+++ b/solution.py
@@ -49,24 +49,9 @@
     return np.cos(angle).astype(np.float32), np.sin(angle).astype(np.float32)
 
 
-def columns_kernel(p_ref, r_ref):
-    cols, sites = p_ref.shape[2], p_ref.shape[3]
-    for colour in range(p_ref.shape[1]):
-        real = p_ref[0, colour].T
-        imag = p_ref[1, colour].T
-        r_ref[colour, :sites, :cols] = real
-        r_ref[colour, :sites, cols:] = imag
-        r_ref[colour, sites:, :cols] = -imag
-        r_ref[colour, sites:, cols:] = real
-
-
-def half_kernel(trivial, where_ref, tab_ref, r_ref, *refs):
-    pieces = len(trivial[1])
-    groups = len(trivial[0])
-    v_refs, out_refs = refs[:pieces], refs[pieces : 2 * pieces]
-    acc_ref, w_refs = refs[2 * pieces], refs[2 * pieces + 1 :]
+def project_rows(trivial, v_refs, tab_ref, right, w_refs):
+    pieces, groups = len(v_refs), len(trivial)
     colours, rows, sites = v_refs[0].shape[1:]
-    cols = r_ref.shape[2] // 2
     squares = [None] * pieces
     total = None
     for colour in range(colours):
@@ -79,7 +64,7 @@
             squares[k] = square if squares[k] is None else squares[k] + square
             for g in range(groups):
                 at = (g * pieces + k) * rows
-                if trivial[0][g]:
+                if trivial[g]:
                     w_real, w_imag = real, -imag
                 else:
                     cosine = tab_ref[2 * g : 2 * g + 1, :]
@@ -88,49 +73,78 @@
                     w_imag = -(sine * real + cosine * imag)
                 w_ref[at : at + rows, :sites] = w_real.astype(jnp.bfloat16)
                 w_ref[at : at + rows, sites:] = w_imag.astype(jnp.bfloat16)
-        part = jnp.dot(w_ref[...], r_ref[colour], preferred_element_type=jnp.float32)
+        part = jnp.dot(w_ref[...], right(colour), preferred_element_type=jnp.float32)
         total = part if total is None else total + part
-    acc_ref[: groups * pieces * rows, :cols] = total[:, :cols]
-    acc_ref[: groups * pieces * rows, cols:] = total[:, cols:]
-    lane = lax.broadcasted_iota(jnp.int32, (rows, LANES), 1)
-    for k in range(pieces):
-        whole = jnp.broadcast_to(jnp.sum(squares[k], axis=1, keepdims=True), (rows, LANES))
-        high = whole.astype(jnp.bfloat16).astype(jnp.float32)
-        at = (groups * pieces + k) * rows
-        acc_ref[at : at + rows, :LANES] = jnp.where(lane < LANES // 2, high, whole - high)
-    for q in range(pieces):
-        k = jnp.bitwise_xor(where_ref[0], q)
-        out_ref = out_refs[q]
-        for g in range(groups):
-            at = pl.multiple_of((g * pieces + k) * rows, rows)
+    return total, squares
+
+
+def square_tile(square):
+    whole = jnp.broadcast_to(jnp.sum(square, axis=1, keepdims=True), square.shape)
+    high = whole.astype(jnp.bfloat16).astype(jnp.float32)
+    lane = lax.broadcasted_iota(jnp.int32, square.shape, 1)
+    return jnp.where(lane < LANES // 2, high, whole - high)
+
+
+def first_kernel(trivial, tab_ref, p_ref, *refs):
+    v_refs, r_ref, out_refs, w_refs = refs[:2], refs[2], refs[3:5], refs[5:]
+    cols, sites = p_ref.shape[2], p_ref.shape[3]
+    rows = v_refs[0].shape[2]
+    for colour in range(p_ref.shape[1]):
+        real = p_ref[0, colour].T
+        imag = p_ref[1, colour].T
+        r_ref[colour, :sites, :cols] = real
+        r_ref[colour, :sites, cols:] = imag
+        r_ref[colour, sites:, :cols] = -imag
+        r_ref[colour, sites:, cols:] = real
+    total, squares = project_rows(trivial, v_refs, tab_ref, lambda colour: r_ref[colour], w_refs)
+    for k, out_ref in enumerate(out_refs):
+        for g in range(len(trivial)):
+            at = (2 * g + k) * rows
             for part in range(2):
-                out_ref[2 * g + part] = acc_ref[
-                    pl.ds(at, rows), part * cols : (part + 1) * cols
-                ].astype(out_ref.dtype)
-        at = pl.multiple_of((groups * pieces + k) * rows, rows)
-        out_ref[2 * groups] = acc_ref[pl.ds(at, rows), :LANES].astype(out_ref.dtype)
+                out_ref[2 * g + part] = total[at : at + rows, part * cols : (part + 1) * cols]
+        out_ref[2 * len(trivial)] = square_tile(squares[k])
+
+
+def rows_kernel(trivial, where_ref, tab_ref, r_ref, own_ref, sibling_ref, *refs):
+    owners = 4
+    v_refs, refs = refs[: 2 * (owners - 1)], refs[2 * (owners - 1) :]
+    out_refs, acc_ref, w_refs = refs[:owners], refs[owners], refs[owners + 1 :]
+    tiles, rows, cols = own_ref.shape
+    total, squares = project_rows(trivial, v_refs, tab_ref, lambda colour: r_ref[colour], w_refs)
+    acc_ref[0, :, :rows] = own_ref[...]
+    acc_ref[0, :, rows:] = sibling_ref[...]
+    for n in range(len(v_refs)):
+        owner, at = divmod(n + 2, 2)
+        for g in range(len(trivial)):
+            low = (g * len(v_refs) + n) * rows
+            for part in range(2):
+                acc_ref[owner, 2 * g + part, at * rows : (at + 1) * rows] = total[
+                    low : low + rows, part * cols : (part + 1) * cols
+                ]
+        acc_ref[owner, tiles - 1, at * rows : (at + 1) * rows] = square_tile(squares[n])
+    for q, out_ref in enumerate(out_refs):
+        out_ref[...] = acc_ref[jnp.bitwise_xor(where_ref[0], q)].astype(out_ref.dtype)
 
 
 def finish_kernel(group, core_ref, *refs):
-    out_ref = refs[-1]
-    per_half = (len(refs) - 1) // 2
+    parts, out_ref = refs[:-1], refs[-1]
     tiles, rows, cols = refs[0].shape
-    for half in range(2):
-        parts = refs[half * per_half : (half + 1) * per_half]
-        first = pl.multiple_of(jnp.bitwise_xor(core_ref[0], half) * (2 * rows), 2 * rows)
-
-        def summed(tile):
-            value = parts[0][tile].astype(jnp.float32)
-            for ref in parts[1:]:
-                value = value + ref[tile].astype(jnp.float32)
-            return value
-
-        both = summed(tiles - 1)
+    rows //= 2
+
+    def summed(tile, at):
+        value = parts[0][tile, at : at + rows].astype(jnp.float32)
+        for ref in parts[1:]:
+            value = value + ref[tile, at : at + rows].astype(jnp.float32)
+        return value
+
+    for other in range(2):
+        first = pl.multiple_of(jnp.bitwise_xor(core_ref[0], other) * (2 * rows), 2 * rows)
+        both = summed(tiles - 1, other * rows)
         squares = both[:, :1] + both[:, LANES // 2 : LANES // 2 + 1]
         inverse = lax.rsqrt(squares + epsilon_norm)
         for g in range((tiles - 1) // 2):
             for part in range(2):
-                value = summed(2 * g + part) * inverse
+                value = summed(2 * g + part, other * rows) * inverse
                 for m, mine in enumerate(group):
                     if mine == g:
                         at = m * 4 * rows + first + part
@@ -161,53 +175,58 @@
     columns = jnp.transpose(propagators[0], (0, 2, 1, 3))
     colours = vectors.shape[2]
 
-    def piece(r):
-        mine = lax.dynamic_index_in_dim(vectors, jnp.bitwise_xor(me, r), 0, keepdims=False)
-        if r == 0:
-            return mine
+    def piece(source, r):
+        return lax.dynamic_index_in_dim(source, jnp.bitwise_xor(me, r), 0, keepdims=False)
+
+    def swapped(mine, r):
         return lax.ppermute(mine, "tm", [(i, i ^ r) for i in range(tm)])
 
-    right = pl.pallas_call(
-        columns_kernel,
-        out_shape=jax.ShapeDtypeStruct((colours, 2 * sites, 2 * cols), jnp.bfloat16),
-        in_specs=in_vmem(1),
-        out_specs=in_vmem(1)[0],
-        cost_estimate=pl.CostEstimate(flops=0, bytes_accessed=3 * 2**20, transcendentals=0),
-        compiler_params=pltpu.CompilerParams(vmem_limit_bytes=16 * 2**20),
-    )(columns)
+    tiles = 2 * groups + 1
+    tile = lambda dtype, count: jax.ShapeDtypeStruct((tiles, count * rows, cols), dtype)
+    w_scratch = lambda count: [pltpu.VMEM((groups * count * rows, 2 * sites), jnp.bfloat16)] * colours
+    small = pl.CostEstimate(flops=2**20, bytes_accessed=2**20, transcendentals=0)
+    params = pltpu.CompilerParams(vmem_limit_bytes=24 * 2**20)
+
+    order = (2, 4, 6, 3, 5, 7)
+    far = {r: piece(vectors, r) for r in order[:3]}
+    vectors, far = lax.optimization_barrier((vectors, far))
+    own, sibling = piece(vectors, 0), piece(vectors, 1)
+    far.update({r: piece(vectors, r) for r in order[3:]})
+    far = {r: swapped(far[r], r) for r in order}
+    sibling = swapped(sibling, 1)
+
+    right, own_sums, sibling_sums = pl.pallas_call(
+        functools.partial(first_kernel, trivial),
+        out_shape=[jax.ShapeDtypeStruct((colours, 2 * sites, 2 * cols), jnp.bfloat16)]
+        + [tile(jnp.float32, 1)] * 2,
+        in_specs=in_vmem(4),
+        out_specs=in_vmem(3),
+        scratch_shapes=w_scratch(2),
+        cost_estimate=small,
+        compiler_params=params,
+    )(table, columns, own, sibling)
 
     where = jnp.bitwise_xor(me // 2, z).astype(jnp.int32).reshape(1)
     core = (me % 2).astype(jnp.int32).reshape(1)
-    tiles = 2 * groups + 1
-    out_tile = lambda dtype: jax.ShapeDtypeStruct((tiles, rows, cols), dtype)
-    half = pl.pallas_call(
-        functools.partial(half_kernel, (trivial, (None,) * space)),
-        out_shape=[out_tile(jnp.float32)] + [out_tile(jnp.bfloat16)] * (space - 1),
-        in_specs=scalar() + in_vmem(2 + space),
+    own, *others = pl.pallas_call(
+        functools.partial(rows_kernel, trivial),
+        out_shape=[tile(jnp.float32, 2)] + [tile(jnp.bfloat16, 2)] * (space - 1),
+        in_specs=scalar() + in_vmem(4 + len(far)),
         out_specs=in_vmem(space),
-        scratch_shapes=[pltpu.VMEM(((groups + 1) * space * rows, 2 * cols), jnp.float32)]
-        + [pltpu.VMEM((groups * space * rows, 2 * sites), jnp.bfloat16)] * colours,
-        cost_estimate=pl.CostEstimate(
-            flops=2 * groups * space * rows * colours * 2 * sites * 2 * cols,
-            bytes_accessed=2 * 2**20,
-            transcendentals=0,
-        ),
-        compiler_params=pltpu.CompilerParams(vmem_limit_bytes=24 * 2**20),
-    )
-    sent = [[piece(r) for r in range(first, tm, 2)] for first in range(2)]
-    parts = []
-    for pieces in sent:
-        own, *others = half(where, table, right, *pieces)
-        parts.append(own)
-        for q, other in enumerate(others, 1):
-            parts.append(lax.ppermute(other, "space", [(i, i ^ q) for i in range(space)]))
+        scratch_shapes=[pltpu.VMEM((space, tiles, 2 * rows, cols), jnp.float32)] + w_scratch(len(far)),
+        cost_estimate=small,
+        compiler_params=params,
+    )(where, table, right, own_sums, sibling_sums, *[far[r] for r in range(2, tm)])
+    parts = [own]
+    for q in (2, 3, 1):
+        parts.append(lax.ppermute(others[q - 1], "space", [(i, i ^ q) for i in range(space)]))
     out = pl.pallas_call(
         functools.partial(finish_kernel, group),
         out_shape=jax.ShapeDtypeStruct((len(group) * 2 * rows * 2, cols), jnp.float32),
         in_specs=scalar() + in_vmem(len(parts)),
         out_specs=in_vmem(1)[0],
-        cost_estimate=pl.CostEstimate(flops=2**20, bytes_accessed=2**20, transcendentals=0),
-        compiler_params=pltpu.CompilerParams(vmem_limit_bytes=16 * 2**20),
+        cost_estimate=small,
+        compiler_params=params,
     )(core, *parts)
     return out.reshape(len(group), 2 * rows, 1, 2, cols)
 
@@ -257,8 +276,8 @@
     def per_device(eigen_vectors, propagators):
         rows, sites = eigen_vectors.shape[2], eigen_vectors.shape[4]
         fits = (
-            tm == 2 * space
-            and space & (space - 1) == 0
+            tm == 8
+            and space == 4
             and eigen_vectors.shape[0] == tm
             and rows % 16 == 0
             and sites % LANES == 0

time: 33.4 us -> 28.6 us (0.86)
  starting transfers between devices: 18.1 us -> 12.2 us
  waiting for transfers between devices: 9.94 us -> 10.9 us
    ppermute x13 -> x10, starting transfers between devices: 18.1 us -> 12.2 us  [the longest x7 7.91 us: swapped(): return lax.ppermute(mine, 'tm', [(i, i ^ r) for i in range(tm)])]
    ppermute x13 -> x10, waiting for transfers between devices: 9.94 us -> 10.9 us  [the longest x3 5.62 us: per_device_permutes(): lax.ppermute(others[q - 1], 'space', [(i, i ^ q) for i in range(space)])]
    squeeze x1 -> x2, local copies, waits for them, and re-layouts: 2 us -> 2.2 us  [piece(): lax.dynamic_index_in_dim(source, jnp.bitwise_xor(me, r), 0, keepdims=False)]
    pallas_call x3 -> x2, Pallas kernels: 1.5 us -> 1.43 us  [the longest x1 0.83 us: per_device_permutes(): pl.pallas_call(functools.partial(rows_kernel, trivial), out_shape=[tile(j...]
  transfers between devices with their start and end apart: 13 -> 10, of which waited for: 5 -> 5; matrix products, arithmetic and copies ran while one was open for 2% -> 6% of each run, Pallas kernels for 5% -> 2%
where the time goes in v2:
time: 28.6 us; the launch traced here: 28.4 us
  starting transfers between devices  12.2 us (43%)
  waiting for transfers between devices  10.9 us (38%)
  local copies, waits for them, and re-layouts  2.92 us (10%)
  Pallas kernels  2.3 us (8%)
    ppermute x7, starting transfers between devices, swapped(): return lax.ppermute(mine, 'tm', [(i, i ^ r) for i in range(tm)])  7.91 us
    ppermute x3, waiting for transfers between devices, per_device_permutes(): lax.ppermute(others[q - 1], 'space', [(i, i ^ q) for i in range(space)])  5.62 us
    ppermute x7, waiting for transfers between devices, swapped(): return lax.ppermute(mine, 'tm', [(i, i ^ r) for i in range(tm)])  5.32 us
    ppermute x3, starting transfers between devices, per_device_permutes(): lax.ppermute(others[q - 1], 'space', [(i, i ^ q) for i in range(space)])  4.24 us
    squeeze x2, local copies, waits for them, and re-layouts, piece(): lax.dynamic_index_in_dim(source, jnp.bitwise_xor(me, r), 0, keepdims=False)  2.2 us
    pallas_call x1, Pallas kernels, per_device_permutes(): pl.pallas_call(functools.partial(finish_kernel, group), out_shape=jax.Sha...  0.87 us
    pallas_call x1, Pallas kernels, per_device_permutes(): pl.pallas_call(functools.partial(rows_kernel, trivial), out_shape=[tile(j...  0.83 us
    squeeze x1, local copies, waits for them, and re-layouts, per_device_permutes(): table = lax.dynamic_index_in_dim(jnp.asarray(tables), z, 0, keepdims=False)  0.72 us
  transfers between devices with their start and end apart: 10, of which 5 were waited for; matrix products, arithmetic and copies ran while one was open for 6% of the time, Pallas kernels for 2%

profile of v2, /device:TPU:0, one launch (start us, length us, event | category | flops | bytes accessed | tf_op | source)
XLA Modules:
  0.0 28.4 jit_solution(1727488328915964614)
XLA Ops:
  0.0 1.1 %dynamic-slice_bitcast_fusion.5 = (bf16[2,3,16,512]{3,2,1,0:T(8,128)(2,1)S(1)}, bf16[2,3,16,512]{3,2,1,0:T(8,128)(2,1)S(1)}, bf16[2,3,16,512]{3,2,1,0:T(8,128)(2,1)S(1)}) fusion(bf16[8,2,16,3,512]{4,2,3,1,0:T(8,128)(2,1)} %param.3, s32[]{:T(128)S(6)} %select_n.45, s32[]{:T(128)S(6)} %select_n.43, s32[]{:T(128)S(6)} %select_n.44), kind=kLoop, calls=%fused_computation.5 | loop fusion | bytes 589836 | tf_op jit(solution)/shard_map/jit(dynamic_index_in_dim)/squeeze | solution.py:179
  1.1 3.0 %collective-permute-start.1 = (bf16[2,3,16,512]{3,2,1,0:T(8,128)(2,1)S(1)}, bf16[2,3,16,512]{3,2,1,0:T(8,128)(2,1)S(1)}, u32[]{:S(2)}, u32[]{:S(2)}) collective-permute-start(bf16[2,3,16,512]{3,2,1,0:T(8,128)(2,1)S(1)} %get-tuple-element.20), channel_id=1, source_target_pairs={{0,8},{4,12},{8,0},{12,4},{16,24},{20,28},{24,16},{28,20},{1,9},{5... | collective-permute-start | bytes 294920 | tf_op jit(solution)/shard_map/ppermute | solution.py:182
  4.1 1.1 %dynamic-slice_bitcast_fusion = (bf16[2,3,16,512]{3,2,1,0:T(8,128)(2,1)S(1)}, bf16[2,3,16,512]{3,2,1,0:T(8,128)(2,1)S(1)}, bf16[2,3,16,512]{3,2,1,0:T(8,128)(2,1...) fusion(bf16[8,2,3,16,512]{4,3,2,1,0:T(8,128)(2,1)} %bitcast.34, s32[]{:T(128)S(6)} %select_n.50, ...), kind=kLoop, calls=%fused_computation | loop fusion | bytes 983060 | tf_op jit(solution)/shard_map/jit(dynamic_index_in_dim)/squeeze | solution.py:179
  5.2 0.1 collective-permute-start
  5.3 1.6 %collective-permute-start.3 = (bf16[2,3,16,512]{3,2,1,0:T(8,128)(2,1)S(1)}, bf16[2,3,16,512]{3,2,1,0:T(8,128)(2,1)S(1)}, u32[]{:S(2)}, u32[]{:S(2)}) collective-permute-start(bf16[2,3,16,512]{3,2,1,0:T(8,128)(2,1)S(1)} %get-tuple-element.21), channel_id=1, source_target_pairs={{0,16},{4,20},{8,24},{12,28},{16,0},{20,4},{24,8},{28,12},{1,17},{... | collective-permute-start | bytes 294920 | tf_op jit(solution)/shard_map/ppermute | solution.py:182
  6.9 0.0 collective-permute-start.5
  6.9 2.4 %collective-permute-start.6 = (bf16[2,3,16,512]{3,2,1,0:T(8,128)(2,1)S(1)}, bf16[2,3,16,512]{3,2,1,0:T(8,128)(2,1)S(1)}, u32[]{:S(2)}, u32[]{:S(2)}) collective-permute-start(bf16[2,3,16,512]{3,2,1,0:T(8,128)(2,1)S(1)} %get-tuple-element.27), channel_id=1, source_target_pairs={{0,28},{4,24},{8,20},{12,16},{16,12},{20,8},{24,4},{28,0},{1,29},{... | collective-permute-start | bytes 294920 | tf_op jit(solution)/shard_map/ppermute | solution.py:182
  9.3 0.0 collective-permute-done.1.refs_0_
  9.3 0.7 %collective-permute-start.4 = (bf16[2,3,16,512]{3,2,1,0:T(8,128)(2,1)S(1)}, bf16[2,3,16,512]{3,2,1,0:T(8,128)(2,1)S(1)}, u32[]{:S(2)}, u32[]{:S(2)}) collective-permute-start(bf16[2,3,16,512]{3,2,1,0:T(8,128)(2,1)S(1)} %get-tuple-element.28), channel_id=1, source_target_pairs={{0,20},{4,16},{8,28},{12,24},{16,4},{20,0},{24,12},{28,8},{1,21},{... | collective-permute-start | bytes 294920 | tf_op jit(solution)/shard_map/ppermute | solution.py:182
  10.0 0.0 collective-permute-done.refs_1_
  10.0 0.1 collective-permute-start.2
  10.1 0.7 %dynamic-slice_bitcast_fusion.8.tab_ref = f32[8,512]{1,0:T(8,128)S(1)} fusion(f32[4,8,512]{2,1,0:T(8,128)} %constant.69.clone, s32[]{:T(128)S(6)} %select_n.42), kind=kLoop, calls=%fused_computation.8 | loop fusion | bytes 32772 | tf_op jit(solution)/shard_map/jit(dynamic_index_in_dim)/squeeze | solution.py:172
  10.9 0.6 %shard_map.37 = (bf16[3,1024,256]{2,1,0:T(8,128)(2,1)S(1)}, f32[9,16,128]{2,1,0:T(8,128)S(1)}, f32[9,16,128]{2,1,0:T(8,128)S(1)}) custom-call(f32[8,512]{1,0:T(8,128)S(1)} %dynamic-slice_bitcast_fusion.8.tab_ref, bf16[2,3,128,512]{3,2,1,0:T(8,128)(2,1)S(1)} %bitcast.33, bf16[2,3,16,512]{3,2,1,0:T(8,128)(2,1)S(1)} %get-tuple-element.31.refs_0_, ...), custom_call_target="tpu_custom_call" | custom-call | flops 1048576 | bytes 1048576 | tf_op jit(solution)/shard_map/pallas_call | solution.py:198
  11.5 2.7 %collective-permute-done.3.refs_2_ = bf16[2,3,16,512]{3,2,1,0:T(8,128)(2,1)S(1)} collective-permute-done((bf16[2,3,16,512]{3,2,1,0:T(8,128)(2,1)S(1)}, bf16[2,3,16,512]{3,2,1,0:T(8,128)(2,1)S(1)}, u32[]{:S(2)}, u32[]{:S(2)}) %collective-permute-start.3) | collective-permute-done | bytes 98336 | tf_op jit(solution)/shard_map/ppermute | solution.py:182
  14.2 0.0 collective-permute-done.5.refs_4_
  14.2 2.6 %collective-permute-done.4.refs_3_ = bf16[2,3,16,512]{3,2,1,0:T(8,128)(2,1)S(1)} collective-permute-done((bf16[2,3,16,512]{3,2,1,0:T(8,128)(2,1)S(1)}, bf16[2,3,16,512]{3,2,1,0:T(8,128)(2,1)S(1)}, u32[]{:S(2)}, u32[]{:S(2)}) %collective-permute-start.4) | collective-permute-done | bytes 98336 | tf_op jit(solution)/shard_map/ppermute | solution.py:182
  16.8 0.8 %shard_map.38 = (f32[9,32,128]{2,1,0:T(8,128)S(1)}, bf16[9,32,128]{2,1,0:T(8,128)(2,1)S(1)}, bf16[9,32,128]{2,1,0:T(8,128)(2,1)S(1)}, bf16[9,32,128]{2,1,0:T(8,128)(2,1)S(1)}) custom-call(s32[1]{0:T(128)} %bitcast.1.where_ref, f32[8,512]{1,0:T(8,128)S(1)} %dynamic-slice_bitcast_fusion.8.tab_ref, bf16[3,1024,256]{2,1,0:T(8,128)(2,1)S(1)} %get-tuple-element.17.r_ref, ...), custom_call_target="tpu_custom_call" | custom-call | flops 1048576 | bytes 1048576 | tf_op jit(solution)/shard_map/pallas_call | solution.py:211
  17.6 2.7 %collective-permute-start.7 = (bf16[9,32,128]{2,1,0:T(8,128)(2,1)S(1)}, bf16[9,32,128]{2,1,0:T(8,128)(2,1)S(1)}, u32[]{:S(2)}, u32[]{:S(2)}) collective-permute-start(bf16[9,32,128]{2,1,0:T(8,128)(2,1)S(1)} %get-tuple-element.24), channel_id=1, source_target_pairs={{0,2},{1,3},{2,0},{3,1},{4,6},{5,7},{6,4},{7,5},{8,10},{9,11},{10,... | collective-permute-start | bytes 221192 | tf_op jit(solution)/shard_map/ppermute | solution.py:222
  20.3 1.3 %collective-permute-start.8 = (bf16[9,32,128]{2,1,0:T(8,128)(2,1)S(1)}, bf16[9,32,128]{2,1,0:T(8,128)(2,1)S(1)}, u32[]{:S(2)}, u32[]{:S(2)}) collective-permute-start(bf16[9,32,128]{2,1,0:T(8,128)(2,1)S(1)} %get-tuple-element.25), channel_id=1, source_target_pairs={{0,3},{1,2},{2,1},{3,0},{4,7},{5,6},{6,5},{7,4},{8,11},{9,10},{10,... | collective-permute-start | bytes 221192 | tf_op jit(solution)/shard_map/ppermute | solution.py:222
  21.6 0.2 collective-permute-start.9
  21.9 4.2 %collective-permute-done.7.refs_1_ = bf16[9,32,128]{2,1,0:T(8,128)(2,1)S(1)} collective-permute-done((bf16[9,32,128]{2,1,0:T(8,128)(2,1)S(1)}, bf16[9,32,128]{2,1,0:T(8,128)(2,1)S(1)}, u32[]{:S(2)}, u32[]{:S(2)}) %collective-permute-start.7) | collective-permute-done | bytes 73760 | tf_op jit(solution)/shard_map/ppermute | solution.py:222
  26.0 0.9 %collective-permute-done.8.refs_2_ = bf16[9,32,128]{2,1,0:T(8,128)(2,1)S(1)} collective-permute-done((bf16[9,32,128]{2,1,0:T(8,128)(2,1)S(1)}, bf16[9,32,128]{2,1,0:T(8,128)(2,1)S(1)}, u32[]{:S(2)}, u32[]{:S(2)}) %collective-permute-start.8) | collective-permute-done | bytes 73760 | tf_op jit(solution)/shard_map/ppermute | solution.py:222
  26.9 0.6 %collective-permute-done.9.refs_3_ = bf16[9,32,128]{2,1,0:T(8,128)(2,1)S(1)} collective-permute-done((bf16[9,32,128]{2,1,0:T(8,128)(2,1)S(1)}, bf16[9,32,128]{2,1,0:T(8,128)(2,1)S(1)}, u32[]{:S(2)}, u32[]{:S(2)}) %collective-permute-start.9) | collective-permute-done | bytes 73760 | tf_op jit(solution)/shard_map/ppermute | solution.py:222
  27.5 0.9 %shard_map.39 = f32[512,128]{1,0:T(8,128)} custom-call(s32[1]{0:T(128)} %bitcast.core_ref, f32[9,32,128]{2,1,0:T(8,128)S(1)} %get-tuple-element.23.refs_0_, bf16[9,32,128]{2,1,0:T(8,128)(2,1)S(1)} %collective-permute-done.7.refs_1_, bf16[9,32,128]{2,1,0:T(8,128)(2,1)S(1)} %collective-permute-done.8.refs_2_, ...), custom_call_target="tpu_custom_call" | custom-call | flops 1048576 | bytes 1048576 | tf_op jit(solution)/shard_map/pallas_call | solution.py:223
  (4 shorter events, 0.0 us)
Async XLA Ops:
  0.0 10.9 %copy-start = (bf16[1,2,128,3,512]{4,2,3,1,0:T(8,128)(2,1)S(1)}, bf16[1,2,128,3,512]{4,2,3,1,0:T(8,128)(2,1)}, u32[]{:S(2)}) copy-start(bf16[1,2,128,3,512]{4,2,3,1,0:T(8,128)(2,1)} %param.4) | copy-start | bytes 2359300
  1.1 8.2 %collective-permute-start.1 = (bf16[2,3,16,512]{3,2,1,0:T(8,128)(2,1)S(1)}, bf16[2,3,16,512]{3,2,1,0:T(8,128)(2,1)S(1)}, u32[]{:S(2)}, u32[]{:S(2)}) collective-permute-start(bf16[2,3,16,512]{3,2,1,0:T(8,128)(2,1)S(1)} %get-tuple-element.20), channel_id=1, source_target_pairs={{0,8},{4,12},{8,0},{12,4},{16,24},{20,28},{24,16},{28,20},{1,9},{5... | collective-permute-start | bytes 294920 | tf_op jit(solution)/shard_map/ppermute | solution.py:182
  5.2 4.8 %collective-permute-start = (bf16[2,3,16,512]{3,2,1,0:T(8,128)(2,1)S(1)}, bf16[2,3,16,512]{3,2,1,0:T(8,128)(2,1)S(1)}, u32[]{:S(2)}, u32[]{:S(2)}) collective-permute-start(bf16[2,3,16,512]{3,2,1,0:T(8,128)(2,1)S(1)} %get-tuple-element.30), channel_id=1, source_target_pairs={{0,4},{4,0},{8,12},{12,8},{16,20},{20,16},{24,28},{28,24},{1,5},{5... | collective-permute-start | bytes 294920 | tf_op jit(solution)/shard_map/ppermute | solution.py:182
  5.3 8.9 %collective-permute-start.3 = (bf16[2,3,16,512]{3,2,1,0:T(8,128)(2,1)S(1)}, bf16[2,3,16,512]{3,2,1,0:T(8,128)(2,1)S(1)}, u32[]{:S(2)}, u32[]{:S(2)}) collective-permute-start(bf16[2,3,16,512]{3,2,1,0:T(8,128)(2,1)S(1)} %get-tuple-element.21), channel_id=1, source_target_pairs={{0,16},{4,20},{8,24},{12,28},{16,0},{20,4},{24,8},{28,12},{1,17},{... | collective-permute-start | bytes 294920 | tf_op jit(solution)/shard_map/ppermute | solution.py:182
  6.9 7.3 %collective-permute-start.5 = (bf16[2,3,16,512]{3,2,1,0:T(8,128)(2,1)S(1)}, bf16[2,3,16,512]{3,2,1,0:T(8,128)(2,1)S(1)}, u32[]{:S(2)}, u32[]{:S(2)}) collective-permute-start(bf16[2,3,16,512]{3,2,1,0:T(8,128)(2,1)S(1)} %get-tuple-element.22), channel_id=1, source_target_pairs={{0,24},{4,28},{8,16},{12,20},{16,8},{20,12},{24,0},{28,4},{1,25},{... | collective-permute-start | bytes 294920 | tf_op jit(solution)/shard_map/ppermute | solution.py:182
  6.9 7.3 %collective-permute-start.6 = (bf16[2,3,16,512]{3,2,1,0:T(8,128)(2,1)S(1)}, bf16[2,3,16,512]{3,2,1,0:T(8,128)(2,1)S(1)}, u32[]{:S(2)}, u32[]{:S(2)}) collective-permute-start(bf16[2,3,16,512]{3,2,1,0:T(8,128)(2,1)S(1)} %get-tuple-element.27), channel_id=1, source_target_pairs={{0,28},{4,24},{8,20},{12,16},{16,12},{20,8},{24,4},{28,0},{1,29},{... | collective-permute-start | bytes 294920 | tf_op jit(solution)/shard_map/ppermute | solution.py:182
  9.3 7.5 %collective-permute-start.4 = (bf16[2,3,16,512]{3,2,1,0:T(8,128)(2,1)S(1)}, bf16[2,3,16,512]{3,2,1,0:T(8,128)(2,1)S(1)}, u32[]{:S(2)}, u32[]{:S(2)}) collective-permute-start(bf16[2,3,16,512]{3,2,1,0:T(8,128)(2,1)S(1)} %get-tuple-element.28), channel_id=1, source_target_pairs={{0,20},{4,16},{8,28},{12,24},{16,4},{20,0},{24,12},{28,8},{1,21},{... | collective-permute-start | bytes 294920 | tf_op jit(solution)/shard_map/ppermute | solution.py:182
  10.0 6.7 %collective-permute-start.2 = (bf16[2,3,16,512]{3,2,1,0:T(8,128)(2,1)S(1)}, bf16[2,3,16,512]{3,2,1,0:T(8,128)(2,1)S(1)}, u32[]{:S(2)}, u32[]{:S(2)}) collective-permute-start(bf16[2,3,16,512]{3,2,1,0:T(8,128)(2,1)S(1)} %get-tuple-element.29), channel_id=1, source_target_pairs={{0,12},{4,8},{8,4},{12,0},{16,28},{20,24},{24,20},{28,16},{1,13},{... | collective-permute-start | bytes 294920 | tf_op jit(solution)/shard_map/ppermute | solution.py:182
  17.6 8.4 %collective-permute-start.7 = (bf16[9,32,128]{2,1,0:T(8,128)(2,1)S(1)}, bf16[9,32,128]{2,1,0:T(8,128)(2,1)S(1)}, u32[]{:S(2)}, u32[]{:S(2)}) collective-permute-start(bf16[9,32,128]{2,1,0:T(8,128)(2,1)S(1)} %get-tuple-element.24), channel_id=1, source_target_pairs={{0,2},{1,3},{2,0},{3,1},{4,6},{5,7},{6,4},{7,5},{8,10},{9,11},{10,... | collective-permute-start | bytes 221192 | tf_op jit(solution)/shard_map/ppermute | solution.py:222
  20.3 6.6 %collective-permute-start.8 = (bf16[9,32,128]{2,1,0:T(8,128)(2,1)S(1)}, bf16[9,32,128]{2,1,0:T(8,128)(2,1)S(1)}, u32[]{:S(2)}, u32[]{:S(2)}) collective-permute-start(bf16[9,32,128]{2,1,0:T(8,128)(2,1)S(1)} %get-tuple-element.25), channel_id=1, source_target_pairs={{0,3},{1,2},{2,1},{3,0},{4,7},{5,6},{6,5},{7,4},{8,11},{9,10},{10,... | collective-permute-start | bytes 221192 | tf_op jit(solution)/shard_map/ppermute | solution.py:222
  21.6 5.9 %collective-permute-start.9 = (bf16[9,32,128]{2,1,0:T(8,128)(2,1)S(1)}, bf16[9,32,128]{2,1,0:T(8,128)(2,1)S(1)}, u32[]{:S(2)}, u32[]{:S(2)}) collective-permute-start(bf16[9,32,128]{2,1,0:T(8,128)(2,1)S(1)} %get-tuple-element.26), channel_id=1, source_target_pairs={{0,1},{1,0},{2,3},{3,2},{4,5},{5,4},{6,7},{7,6},{8,9},{9,8},{10,11... | collective-permute-start | bytes 221192 | tf_op jit(solution)/shard_map/ppermute | solution.py:222

commit v3 on v2

--- a/solution.py
+++ b/solution.py
@@ -51,7 +51,7 @@
 
 def project_rows(trivial, v_refs, tab_ref, right, w_refs):
     pieces, groups = len(v_refs), len(trivial)
-    colours, rows, sites = v_refs[0].shape[1:]
+    colours, rows, sites = v_refs[0].shape[-3:]
     squares = [None] * pieces
     total = None
     for colour in range(colours):
@@ -78,11 +78,14 @@
     return total, squares
 
 
-def square_tile(square):
+def square_tile(square, half):
+    rows = square.shape[0]
     whole = jnp.broadcast_to(jnp.sum(square, axis=1, keepdims=True), square.shape)
     high = whole.astype(jnp.bfloat16).astype(jnp.float32)
     lane = lax.broadcasted_iota(jnp.int32, square.shape, 1)
-    return jnp.where(lane < LANES // 2, high, whole - high)
+    place = lax.broadcasted_iota(jnp.int32, square.shape, 0) + rows * half
+    spread = jnp.where(lane == place, high, jnp.where(lane == place + 2 * rows, whole - high, 0.0))
+    return jnp.broadcast_to(jnp.sum(spread, axis=0, keepdims=True), square.shape)
 
 
 def first_kernel(trivial, tab_ref, p_ref, *refs):
@@ -102,57 +105,104 @@
             at = (2 * g + k) * rows
             for part in range(2):
                 out_ref[2 * g + part] = total[at : at + rows, part * cols : (part + 1) * cols]
-        out_ref[2 * len(trivial)] = square_tile(squares[k])
-
-
-def rows_kernel(trivial, where_ref, tab_ref, r_ref, own_ref, sibling_ref, *refs):
-    owners = 4
-    v_refs, refs = refs[: 2 * (owners - 1)], refs[2 * (owners - 1) :]
+        out_ref[2 * len(trivial)] = square_tile(squares[k], k)
+
+
+def slab_kernel(v_ref, *refs):
+    slab_refs, own_refs = refs[:-2], refs[-2:]
+    me = lax.axis_index("tm")
+    for k, ref in enumerate(slab_refs, 1):
+        ref[...] = v_ref[pl.ds(2 * jnp.bitwise_xor(lax.div(me, 2), k), 2)]
+    for k, ref in enumerate(own_refs):
+        ref[...] = v_ref[jnp.bitwise_xor(me, k)]
+
+
+def part_kernel(core_ref, *refs):
+    slab_refs, out_ref = refs[:-1], refs[-1]
+    for n, slab_ref in enumerate(slab_refs):
+        out_ref[n] = slab_ref[1 - core_ref[0]]
+
+
+def stay_kernel(trivial, core_ref, tab_ref, r_ref, *refs):
+    slabs = len(refs) - 4
+    slab_refs, out_ref, w_refs = refs[:slabs], refs[slabs], refs[slabs + 1 :]
+    tiles, rows, cols = out_ref.shape[1:]
+    v_refs = [slab_ref.at[core_ref[0]] for slab_ref in slab_refs]
+    total, squares = project_rows(trivial, v_refs, tab_ref, lambda colour: r_ref[colour], w_refs)
+    for n in range(slabs):
+        for g in range(len(trivial)):
+            low = (g * slabs + n) * rows
+            for part in range(2):
+                out_ref[n, 2 * g + part] = total[low : low + rows, part * cols : (part + 1) * cols]
+        out_ref[n, tiles - 1] = square_tile(squares[n], 0)
+
+
+def rows_kernel(trivial, where_ref, tab_ref, r_ref, own_ref, sibling_ref, stay_ref, swapped_ref, *refs):
+    owners = stay_ref.shape[0] + 1
     out_refs, acc_ref, w_refs = refs[:owners], refs[owners], refs[owners + 1 :]
     tiles, rows, cols = own_ref.shape
+    v_refs = [swapped_ref.at[n] for n in range(owners - 1)]
     total, squares = project_rows(trivial, v_refs, tab_ref, lambda colour: r_ref[colour], w_refs)
-    acc_ref[0, :, :rows] = own_ref[...]
-    acc_ref[0, :, rows:] = sibling_ref[...]
-    for n in range(len(v_refs)):
-        owner, at = divmod(n + 2, 2)
+    last = 2 * rows * (tiles - 1)
+    for tile in range(tiles - 1):
+        at = 2 * rows * tile
+        acc_ref[0, at : at + rows] = own_ref[tile]
+        acc_ref[0, at + rows : at + 2 * rows] = sibling_ref[tile]
+    acc_ref[0, last:] = own_ref[tiles - 1] + sibling_ref[tiles - 1]
+    for n in range(owners - 1):
         for g in range(len(trivial)):
-            low = (g * len(v_refs) + n) * rows
+            low = (g * (owners - 1) + n) * rows
             for part in range(2):
-                acc_ref[owner, 2 * g + part, at * rows : (at + 1) * rows] = total[
+                at = 2 * rows * (2 * g + part)
+                acc_ref[n + 1, at : at + rows] = stay_ref[n, 2 * g + part]
+                acc_ref[n + 1, at + rows : at + 2 * rows] = total[
                     low : low + rows, part * cols : (part + 1) * cols
                 ]
-        acc_ref[owner, tiles - 1, at * rows : (at + 1) * rows] = square_tile(squares[n])
+        acc_ref[n + 1, last:] = stay_ref[n, tiles - 1] + square_tile(squares[n], 1)
     for q, out_ref in enumerate(out_refs):
         out_ref[...] = acc_ref[jnp.bitwise_xor(where_ref[0], q)].astype(out_ref.dtype)
 
 
 def finish_kernel(group, core_ref, *refs):
-    parts, out_ref = refs[:-1], refs[-1]
-    tiles, rows, cols = refs[0].shape
-    rows //= 2
-
-    def summed(tile, at):
-        value = parts[0][tile, at : at + rows].astype(jnp.float32)
+    count = len(group)
+    parts, out_ref, done_ref, sems = refs[:-3], refs[-3], refs[-2], refs[-1]
+    groups = max(group) + 1
+    rows = done_ref.shape[1] // 4
+    last = 4 * rows * groups
+
+    def summed(at, size):
+        value = parts[0][at : at + size].astype(jnp.float32)
         for ref in parts[1:]:
-            value = value + ref[tile, at : at + rows].astype(jnp.float32)
+            value = value + ref[at : at + size].astype(jnp.float32)
         return value
 
-    for other in range(2):
-        first = pl.multiple_of(jnp.bitwise_xor(core_ref[0], other) * (2 * rows), 2 * rows)
-        both = summed(tiles - 1, other * rows)
-        squares = both[:, :1] + both[:, LANES // 2 : LANES // 2 + 1]
-        inverse = lax.rsqrt(squares + epsilon_norm)
-        for g in range((tiles - 1) // 2):
-            for part in range(2):
-                value = summed(2 * g + part, other * rows) * inverse
-                for m, mine in enumerate(group):
-                    if mine == g:
-                        at = m * 4 * rows + first + part
-                        out_ref[pl.ds(at, rows, stride=2), :] = value
+    both = jnp.broadcast_to(summed(last, rows)[:1], (2 * rows, LANES))
+    lane = lax.broadcasted_iota(jnp.int32, both.shape, 1)
+    place = lax.broadcasted_iota(jnp.int32, both.shape, 0)
+    mine = (lane == place) | (lane == place + 2 * rows)
+    squares = jnp.sum(jnp.where(mine, both, 0.0), axis=1, keepdims=True)
+    inverse = lax.rsqrt(squares + epsilon_norm)
+    copies = []
+    for g in range(groups):
+        for part in range(2):
+            value = summed(2 * rows * (2 * g + part), 2 * rows) * inverse
+            for other in range(2):
+                first = pl.multiple_of(jnp.bitwise_xor(core_ref[0], other) * (2 * rows), 2 * rows)
+                done_ref[g, pl.ds(first + part, rows, stride=2), :] = value[other * rows : (other + 1) * rows]
+        for m in range(count):
+            if group[m] == g:
+                copies.append(pltpu.make_async_copy(done_ref.at[g], out_ref.at[m], sems.at[m]))
+                copies[-1].start()
+    for copy in copies:
+        copy.wait()
 
 
 def in_vmem(count):
     return [pl.BlockSpec(memory_space=pltpu.VMEM)] * count
+
+
+def anywhere(count):
+    return [pl.BlockSpec(memory_space=pl.ANY)] * count
 
 
 def scalar():
@@ -175,30 +225,32 @@
     columns = jnp.transpose(propagators[0], (0, 2, 1, 3))
     colours = vectors.shape[2]
 
-    def piece(source, r):
-        return lax.dynamic_index_in_dim(source, jnp.bitwise_xor(me, r), 0, keepdims=False)
-
     def swapped(mine, r):
         return lax.ppermute(mine, "tm", [(i, i ^ r) for i in range(tm)])
 
     tiles = 2 * groups + 1
-    tile = lambda dtype, count: jax.ShapeDtypeStruct((tiles, count * rows, cols), dtype)
+    tile = lambda dtype: jax.ShapeDtypeStruct((tiles, rows, cols), dtype)
+    payload = lambda dtype: jax.ShapeDtypeStruct((2 * rows * (tiles - 1) + rows, cols), dtype)
     w_scratch = lambda count: [pltpu.VMEM((groups * count * rows, 2 * sites), jnp.bfloat16)] * colours
     small = pl.CostEstimate(flops=2**20, bytes_accessed=2**20, transcendentals=0)
-    params = pltpu.CompilerParams(vmem_limit_bytes=24 * 2**20)
-
-    order = (2, 4, 6, 3, 5, 7)
-    far = {r: piece(vectors, r) for r in order[:3]}
-    vectors, far = lax.optimization_barrier((vectors, far))
-    own, sibling = piece(vectors, 0), piece(vectors, 1)
-    far.update({r: piece(vectors, r) for r in order[3:]})
-    far = {r: swapped(far[r], r) for r in order}
+    params = pltpu.CompilerParams(vmem_limit_bytes=12 * 2**20)
+
+    one = lambda *lead: jax.ShapeDtypeStruct(lead + vectors.shape[1:], vectors.dtype)
+    *slabs, own, sibling = pl.pallas_call(
+        slab_kernel,
+        out_shape=[one(2)] * (space - 1) + [one()] * 2,
+        in_specs=in_vmem(1),
+        out_specs=in_vmem(space + 1),
+        cost_estimate=small,
+        compiler_params=params,
+    )(vectors)
+    slabs = [swapped(slab, 2 * k) for k, slab in enumerate(slabs, 1)]
     sibling = swapped(sibling, 1)
 
     right, own_sums, sibling_sums = pl.pallas_call(
         functools.partial(first_kernel, trivial),
         out_shape=[jax.ShapeDtypeStruct((colours, 2 * sites, 2 * cols), jnp.bfloat16)]
-        + [tile(jnp.float32, 1)] * 2,
+        + [tile(jnp.float32)] * 2,
         in_specs=in_vmem(4),
         out_specs=in_vmem(3),
         scratch_shapes=w_scratch(2),
@@ -208,23 +260,47 @@
 
     where = jnp.bitwise_xor(me // 2, z).astype(jnp.int32).reshape(1)
     core = (me % 2).astype(jnp.int32).reshape(1)
+    own_sums, slabs = lax.optimization_barrier((own_sums, slabs))
+    part = jax.ShapeDtypeStruct((space - 1,) + slabs[0].shape[1:], slabs[0].dtype)
+    leaving = pl.pallas_call(
+        part_kernel,
+        out_shape=part,
+        in_specs=scalar() + in_vmem(len(slabs)),
+        out_specs=in_vmem(1)[0],
+        cost_estimate=small,
+        compiler_params=params,
+    )(core, *slabs)
+    came = swapped(leaving, 1)
+    stay_sums = pl.pallas_call(
+        functools.partial(stay_kernel, trivial),
+        out_shape=jax.ShapeDtypeStruct((space - 1, tiles, rows, cols), jnp.float32),
+        in_specs=scalar() + in_vmem(2 + len(slabs)),
+        out_specs=in_vmem(1)[0],
+        scratch_shapes=w_scratch(len(slabs)),
+        cost_estimate=small,
+        compiler_params=params,
+    )(core, table, right, *slabs)
     own, *others = pl.pallas_call(
         functools.partial(rows_kernel, trivial),
-        out_shape=[tile(jnp.float32, 2)] + [tile(jnp.bfloat16, 2)] * (space - 1),
-        in_specs=scalar() + in_vmem(4 + len(far)),
+        out_shape=[payload(jnp.float32)] + [payload(jnp.bfloat16)] * (space - 1),
+        in_specs=scalar() + in_vmem(6),
         out_specs=in_vmem(space),
-        scratch_shapes=[pltpu.VMEM((space, tiles, 2 * rows, cols), jnp.float32)] + w_scratch(len(far)),
-        cost_estimate=small,
-        compiler_params=params,
-    )(where, table, right, own_sums, sibling_sums, *[far[r] for r in range(2, tm)])
+        scratch_shapes=[pltpu.VMEM((space,) + payload(jnp.float32).shape, jnp.float32)] + w_scratch(space - 1),
+        cost_estimate=small,
+        compiler_params=params,
+    )(where, table, right, own_sums, sibling_sums, stay_sums, came)
     parts = [own]
     for q in (2, 3, 1):
         parts.append(lax.ppermute(others[q - 1], "space", [(i, i ^ q) for i in range(space)]))
     out = pl.pallas_call(
         functools.partial(finish_kernel, group),
-        out_shape=jax.ShapeDtypeStruct((len(group) * 2 * rows * 2, cols), jnp.float32),
+        out_shape=jax.ShapeDtypeStruct((len(group), 2 * rows * 2, cols), jnp.float32),
         in_specs=scalar() + in_vmem(len(parts)),
-        out_specs=in_vmem(1)[0],
+        out_specs=anywhere(1)[0],
+        scratch_shapes=[
+            pltpu.VMEM((groups, 2 * rows * 2, cols), jnp.float32),
+            pltpu.SemaphoreType.DMA((len(group),)),
+        ],
         cost_estimate=small,
         compiler_params=params,
     )(core, *parts)

time: 28.6 us -> 27.7 us (0.969)
  starting transfers between devices: 12.2 us -> 8.85 us
  waiting for transfers between devices: 10.9 us -> 13 us
    ppermute x7 -> x5, starting transfers between devices: 7.91 us -> 4.62 us  [swapped(): return lax.ppermute(mine, 'tm', [(i, i ^ r) for i in range(tm)])]
    ppermute x7 -> x5, waiting for transfers between devices: 5.32 us -> 7.63 us  [swapped(): return lax.ppermute(mine, 'tm', [(i, i ^ r) for i in range(tm)])]
    unnamed x2 -> x4, local copies, waits for them, and re-layouts: 0.01 us -> 2.27 us
    squeeze x2 -> x0, local copies, waits for them, and re-layouts: 2.2 us -> none  [piece(): lax.dynamic_index_in_dim(source, jnp.bitwise_xor(me, r), 0, keepdims=False)]
    pallas_call x1 -> x4, Pallas kernels: 0.83 us -> 1.08 us  [the longest x1 0.52 us: per_device_permutes(): pl.pallas_call(functools.partial(rows_kernel, trivial), out_shape=[payloa...]
  transfers between devices with their start and end apart: 10 -> 8, of which waited for: 5 -> 7; matrix products, arithmetic and copies ran while one was open for 6% -> 3% of each run, Pallas kernels for 2% -> 4%
where the time goes in v3:
time: 27.7 us; the launch traced here: 27.5 us
  waiting for transfers between devices  13 us (47%)
  starting transfers between devices  8.85 us (32%)
  local copies, waits for them, and re-layouts  2.98 us (11%)
  Pallas kernels  2.54 us (9%)
    ppermute x5, waiting for transfers between devices, swapped(): return lax.ppermute(mine, 'tm', [(i, i ^ r) for i in range(tm)])  7.63 us
    ppermute x3, waiting for transfers between devices, per_device_permutes(): lax.ppermute(others[q - 1], 'space', [(i, i ^ q) for i in range(space)])  5.41 us
    ppermute x5, starting transfers between devices, swapped(): return lax.ppermute(mine, 'tm', [(i, i ^ r) for i in range(tm)])  4.62 us
    ppermute x3, starting transfers between devices, per_device_permutes(): lax.ppermute(others[q - 1], 'space', [(i, i ^ q) for i in range(space)])  4.23 us
    unnamed x4, local copies, waits for them, and re-layouts  2.27 us
    pallas_call x1, Pallas kernels, per_device_permutes(): pl.pallas_call(functools.partial(finish_kernel, group), out_shape=jax.Sha...  0.86 us
    squeeze x1, local copies, waits for them, and re-layouts, per_device_permutes(): table = lax.dynamic_index_in_dim(jnp.asarray(tables), z, 0, keepdims=False)  0.72 us
    pallas_call x1, Pallas kernels, per_device_permutes(): pl.pallas_call(functools.partial(first_kernel, trivial), out_shape=[jax.S...  0.6 us
  transfers between devices with their start and end apart: 8, of which 7 were waited for; matrix products, arithmetic and copies ran while one was open for 3% of the time, Pallas kernels for 4%

profile of v3, /device:TPU:0, one launch (start us, length us, event | category | flops | bytes accessed | tf_op | source)
XLA Modules:
  0.0 27.5 jit_solution(3076388451153329215)
XLA Ops:
  0.0 1.1 %copy-done = bf16[8,2,16,3,512]{4,2,3,1,0:T(8,128)(2,1)S(1)} copy-done((bf16[8,2,16,3,512]{4,2,3,1,0:T(8,128)(2,1)S(1)}, bf16[8,2,16,3,512]{4,2,3,1,0:T(8,128)(2,1)}, u32[]{:S(2)}) %copy-start) | copy-done | bytes 786456
  1.1 0.1 shard_map.37
  1.2 3.0 %collective-permute-start.1 = (bf16[2,2,3,16,512]{4,3,2,1,0:T(8,128)(2,1)S(1)}, bf16[2,2,3,16,512]{4,3,2,1,0:T(8,128)(2,1)S(1)}, u32[]{:S(2)}, u32[]{:S(2)}) collective-permute-start(bf16[2,2,3,16,512]{4,3,2,1,0:T(8,128)(2,1)S(1)} %get-tuple-element.25), channel_id=1, source_target_pairs={{0,8},{4,12},{8,0},{12,4},{16,24},{20,28},{24,16},{28,20},{1,9},{5... | collective-permute-start | bytes 589832 | tf_op jit(solution)/shard_map/ppermute | solution.py:229
  4.2 1.5 %collective-permute-start.2 = (bf16[2,2,3,16,512]{4,3,2,1,0:T(8,128)(2,1)S(1)}, bf16[2,2,3,16,512]{4,3,2,1,0:T(8,128)(2,1)S(1)}, u32[]{:S(2)}, u32[]{:S(2)}) collective-permute-start(bf16[2,2,3,16,512]{4,3,2,1,0:T(8,128)(2,1)S(1)} %get-tuple-element.26), channel_id=1, source_target_pairs={{0,16},{4,20},{8,24},{12,28},{16,0},{20,4},{24,8},{28,12},{1,17},{... | collective-permute-start | bytes 589832 | tf_op jit(solution)/shard_map/ppermute | solution.py:229
  5.7 0.0 collective-permute-start.3
  5.7 0.0 collective-permute-start
  5.7 0.7 %dynamic-slice_bitcast_fusion.tab_ref = f32[8,512]{1,0:T(8,128)S(1)} fusion(f32[4,8,512]{2,1,0:T(8,128)} %constant.40.clone, s32[]{:T(128)S(6)} %select_n.17), kind=kLoop, calls=%fused_computation | loop fusion | bytes 32772 | tf_op jit(solution)/shard_map/jit(dynamic_index_in_dim)/squeeze | solution.py:222
  6.5 0.6 %collective-permute-done.refs_1_ = bf16[2,3,16,512]{3,2,1,0:T(8,128)(2,1)S(1)} collective-permute-done((bf16[2,3,16,512]{3,2,1,0:T(8,128)(2,1)S(1)}, bf16[2,3,16,512]{3,2,1,0:T(8,128)(2,1)S(1)}, u32[]{:S(2)}, u32[]{:S(2)}) %collective-permute-start) | collective-permute-done | bytes 98336 | tf_op jit(solution)/shard_map/ppermute | solution.py:229
  7.0 1.1 %copy-done.1 = bf16[1,2,128,3,512]{4,2,3,1,0:T(8,128)(2,1)S(1)} copy-done((bf16[1,2,128,3,512]{4,2,3,1,0:T(8,128)(2,1)S(1)}, bf16[1,2,128,3,512]{4,2,3,1,0:T(8,128)(2,1)}, u32[]{:S(2)}) %copy-start.1) | copy-done | bytes 786456
  8.2 0.6 %shard_map.38 = (bf16[3,1024,256]{2,1,0:T(8,128)(2,1)S(1)}, f32[9,16,128]{2,1,0:T(8,128)S(1)}, f32[9,16,128]{2,1,0:T(8,128)S(1)}) custom-call(f32[8,512]{1,0:T(8,128)S(1)} %dynamic-slice_bitcast_fusion.tab_ref, bf16[2,3,128,512]{3,2,1,0:T(8,128)(2,1)S(1)} %bitcast.12, bf16[2,3,16,512]{3,2,1,0:T(8,128)(2,1)S(1)} %get-tuple-element.21.refs_0_, ...), custom_call_target="tpu_custom_call" | custom-call | flops 1048576 | bytes 1048576 | tf_op jit(solution)/shard_map/pallas_call | solution.py:250
  8.8 1.1 %collective-permute-done.1.refs_0_ = bf16[2,2,3,16,512]{4,3,2,1,0:T(8,128)(2,1)S(1)} collective-permute-done((bf16[2,2,3,16,512]{4,3,2,1,0:T(8,128)(2,1)S(1)}, bf16[2,2,3,16,512]{4,3,2,1,0:T(8,128)(2,1)S(1)}, u32[]{:S(2)}, u32[]{:S(2)}) %collective-permute-start.1) | collective-permute-done | bytes 196640 | tf_op jit(solution)/shard_map/ppermute | solution.py:229
  9.9 4.8 %collective-permute-done.2.refs_1_ = bf16[2,2,3,16,512]{4,3,2,1,0:T(8,128)(2,1)S(1)} collective-permute-done((bf16[2,2,3,16,512]{4,3,2,1,0:T(8,128)(2,1)S(1)}, bf16[2,2,3,16,512]{4,3,2,1,0:T(8,128)(2,1)S(1)}, u32[]{:S(2)}, u32[]{:S(2)}) %collective-permute-start.2) | collective-permute-done | bytes 196640 | tf_op jit(solution)/shard_map/ppermute | solution.py:229
  14.8 0.0 collective-permute-done.3.refs_2_
  14.8 0.1 collective-permute-start.4
  14.9 0.5 %shard_map.39.stay_ref = f32[3,9,16,128]{3,2,1,0:T(8,128)S(1)} custom-call(s32[1]{0:T(128)} %bitcast.core_ref, f32[8,512]{1,0:T(8,128)S(1)} %dynamic-slice_bitcast_fusion.tab_ref, bf16[3,1024,256]{2,1,0:T(8,128)(2,1)S(1)} %get-tuple-element.23.r_ref, bf16[2,2,3,16,512]{4,3,2,1,0:T(8,128)(2,1)S(1)} %collective-permute-done.1.refs_0_, ...), custom_call_target="tpu_custom_call" | custom-call | flops 1048576 | bytes 1048576 | tf_op jit(solution)/shard_map/pallas_call | solution.py:274
  15.4 1.1 %collective-permute-done.4.swapped_ref = bf16[3,2,3,16,512]{4,3,2,1,0:T(8,128)(2,1)S(1)} collective-permute-done((bf16[3,2,3,16,512]{4,3,2,1,0:T(8,128)(2,1)S(1)}, bf16[3,2,3,16,512]{4,3,2,1,0:T(8,128)(2,1)S(1)}, u32[]{:S(2)}, u32[]{:S(2)}) %collective-permute-start.4) | collective-permute-done | bytes 294944 | tf_op jit(solution)/shard_map/ppermute | solution.py:229
  16.4 0.5 %shard_map.41 = (f32[272,128]{1,0:T(8,128)S(1)}, bf16[272,128]{1,0:T(8,128)(2,1)S(1)}, bf16[272,128]{1,0:T(8,128)(2,1)S(1)}, bf16[272,128]{1,0:T(8,128)(2,1)S(1)}) custom-call(s32[1]{0:T(128)} %bitcast.1.where_ref, f32[8,512]{1,0:T(8,128)S(1)} %dynamic-slice_bitcast_fusion.tab_ref, bf16[3,1024,256]{2,1,0:T(8,128)(2,1)S(1)} %get-tuple-element.23.r_ref, ...), custom_call_target="tpu_custom_call" | custom-call | flops 1048576 | bytes 1048576 | tf_op jit(solution)/shard_map/pallas_call | solution.py:283
  17.0 2.7 %collective-permute-start.5 = (bf16[272,128]{1,0:T(8,128)(2,1)S(1)}, bf16[272,128]{1,0:T(8,128)(2,1)S(1)}, u32[]{:S(2)}, u32[]{:S(2)}) collective-permute-start(bf16[272,128]{1,0:T(8,128)(2,1)S(1)} %get-tuple-element.34), channel_id=1, source_target_pairs={{0,2},{1,3},{2,0},{3,1},{4,6},{5,7},{6,4},{7,5},{8,10},{9,11},{10,... | collective-permute-start | bytes 208904 | tf_op jit(solution)/shard_map/ppermute | solution.py:294
  19.6 1.3 %collective-permute-start.6 = (bf16[272,128]{1,0:T(8,128)(2,1)S(1)}, bf16[272,128]{1,0:T(8,128)(2,1)S(1)}, u32[]{:S(2)}, u32[]{:S(2)}) collective-permute-start(bf16[272,128]{1,0:T(8,128)(2,1)S(1)} %get-tuple-element.35), channel_id=1, source_target_pairs={{0,3},{1,2},{2,1},{3,0},{4,7},{5,6},{6,5},{7,4},{8,11},{9,10},{10,... | collective-permute-start | bytes 208904 | tf_op jit(solution)/shard_map/ppermute | solution.py:294
  21.0 0.2 collective-permute-start.7
  21.2 3.7 %collective-permute-done.5.refs_1_ = bf16[272,128]{1,0:T(8,128)(2,1)S(1)} collective-permute-done((bf16[272,128]{1,0:T(8,128)(2,1)S(1)}, bf16[272,128]{1,0:T(8,128)(2,1)S(1)}, u32[]{:S(2)}, u32[]{:S(2)}) %collective-permute-start.5) | collective-permute-done | bytes 69664 | tf_op jit(solution)/shard_map/ppermute | solution.py:294
  25.0 1.2 %collective-permute-done.6.refs_2_ = bf16[272,128]{1,0:T(8,128)(2,1)S(1)} collective-permute-done((bf16[272,128]{1,0:T(8,128)(2,1)S(1)}, bf16[272,128]{1,0:T(8,128)(2,1)S(1)}, u32[]{:S(2)}, u32[]{:S(2)}) %collective-permute-start.6) | collective-permute-done | bytes 69664 | tf_op jit(solution)/shard_map/ppermute | solution.py:294
  26.2 0.5 %collective-permute-done.7.refs_3_ = bf16[272,128]{1,0:T(8,128)(2,1)S(1)} collective-permute-done((bf16[272,128]{1,0:T(8,128)(2,1)S(1)}, bf16[272,128]{1,0:T(8,128)(2,1)S(1)}, u32[]{:S(2)}, u32[]{:S(2)}) %collective-permute-start.7) | collective-permute-done | bytes 69664 | tf_op jit(solution)/shard_map/ppermute | solution.py:294
  26.6 0.9 %shard_map.42 = f32[8,64,128]{2,1,0:T(8,128)} custom-call(s32[1]{0:T(128)} %bitcast.core_ref, f32[272,128]{1,0:T(8,128)S(1)} %get-tuple-element.33.refs_0_, bf16[272,128]{1,0:T(8,128)(2,1)S(1)} %collective-permute-done.5.refs_1_, bf16[272,128]{1,0:T(8,128)(2,1)S(1)} %collective-permute-done.6.refs_2_, bf16[272,128]{1,0:T(8,128)(2,1)S(1)} %collective-permute-done.7.refs_3_), custom_call_target="tpu_custom_call" | custom-call | flops 1048576 | bytes 1048576 | tf_op jit(solution)/shard_map/pallas_call | solution.py:295
  (3 shorter events, 0.0 us)
Async XLA Ops:
  0.0 1.1 %copy-start = (bf16[8,2,16,3,512]{4,2,3,1,0:T(8,128)(2,1)S(1)}, bf16[8,2,16,3,512]{4,2,3,1,0:T(8,128)(2,1)}, u32[]{:S(2)}) copy-start(bf16[8,2,16,3,512]{4,2,3,1,0:T(8,128)(2,1)} %param.3) | copy-start | bytes 2359300
  1.2 8.7 %collective-permute-start.1 = (bf16[2,2,3,16,512]{4,3,2,1,0:T(8,128)(2,1)S(1)}, bf16[2,2,3,16,512]{4,3,2,1,0:T(8,128)(2,1)S(1)}, u32[]{:S(2)}, u32[]{:S(2)}) collective-permute-start(bf16[2,2,3,16,512]{4,3,2,1,0:T(8,128)(2,1)S(1)} %get-tuple-element.25), channel_id=1, source_target_pairs={{0,8},{4,12},{8,0},{12,4},{16,24},{20,28},{24,16},{28,20},{1,9},{5... | collective-permute-start | bytes 589832 | tf_op jit(solution)/shard_map/ppermute | solution.py:229
  4.2 10.6 %collective-permute-start.2 = (bf16[2,2,3,16,512]{4,3,2,1,0:T(8,128)(2,1)S(1)}, bf16[2,2,3,16,512]{4,3,2,1,0:T(8,128)(2,1)S(1)}, u32[]{:S(2)}, u32[]{:S(2)}) collective-permute-start(bf16[2,2,3,16,512]{4,3,2,1,0:T(8,128)(2,1)S(1)} %get-tuple-element.26), channel_id=1, source_target_pairs={{0,16},{4,20},{8,24},{12,28},{16,0},{20,4},{24,8},{28,12},{1,17},{... | collective-permute-start | bytes 589832 | tf_op jit(solution)/shard_map/ppermute | solution.py:229
  5.7 9.1 %collective-permute-start.3 = (bf16[2,2,3,16,512]{4,3,2,1,0:T(8,128)(2,1)S(1)}, bf16[2,2,3,16,512]{4,3,2,1,0:T(8,128)(2,1)S(1)}, u32[]{:S(2)}, u32[]{:S(2)}) collective-permute-start(bf16[2,2,3,16,512]{4,3,2,1,0:T(8,128)(2,1)S(1)} %get-tuple-element.27), channel_id=1, source_target_pairs={{0,24},{4,28},{8,16},{12,20},{16,8},{20,12},{24,0},{28,4},{1,25},{... | collective-permute-start | bytes 589832 | tf_op jit(solution)/shard_map/ppermute | solution.py:229
  5.7 1.3 %collective-permute-start = (bf16[2,3,16,512]{3,2,1,0:T(8,128)(2,1)S(1)}, bf16[2,3,16,512]{3,2,1,0:T(8,128)(2,1)S(1)}, u32[]{:S(2)}, u32[]{:S(2)}) collective-permute-start(bf16[2,3,16,512]{3,2,1,0:T(8,128)(2,1)S(1)} %get-tuple-element.22), channel_id=1, source_target_pairs={{0,4},{4,0},{8,12},{12,8},{16,20},{20,16},{24,28},{28,24},{1,5},{5... | collective-permute-start | bytes 294920 | tf_op jit(solution)/shard_map/ppermute | solution.py:229
  7.0 1.1 %copy-start.1 = (bf16[1,2,128,3,512]{4,2,3,1,0:T(8,128)(2,1)S(1)}, bf16[1,2,128,3,512]{4,2,3,1,0:T(8,128)(2,1)}, u32[]{:S(2)}) copy-start(bf16[1,2,128,3,512]{4,2,3,1,0:T(8,128)(2,1)} %param.4) | copy-start | bytes 2359300
  14.8 1.6 %collective-permute-start.4 = (bf16[3,2,3,16,512]{4,3,2,1,0:T(8,128)(2,1)S(1)}, bf16[3,2,3,16,512]{4,3,2,1,0:T(8,128)(2,1)S(1)}, u32[]{:S(2)}, u32[]{:S(2)}) collective-permute-start(bf16[3,2,3,16,512]{4,3,2,1,0:T(8,128)(2,1)S(1)} %shard_map.40), channel_id=1, source_target_pairs={{0,4},{4,0},{8,12},{12,8},{16,20},{20,16},{24,28},{28,24},{1,5},{5... | collective-permute-start | bytes 884744 | tf_op jit(solution)/shard_map/ppermute | solution.py:229
  17.0 8.0 %collective-permute-start.5 = (bf16[272,128]{1,0:T(8,128)(2,1)S(1)}, bf16[272,128]{1,0:T(8,128)(2,1)S(1)}, u32[]{:S(2)}, u32[]{:S(2)}) collective-permute-start(bf16[272,128]{1,0:T(8,128)(2,1)S(1)} %get-tuple-element.34), channel_id=1, source_target_pairs={{0,2},{1,3},{2,0},{3,1},{4,6},{5,7},{6,4},{7,5},{8,10},{9,11},{10,... | collective-permute-start | bytes 208904 | tf_op jit(solution)/shard_map/ppermute | solution.py:294
  19.6 6.5 %collective-permute-start.6 = (bf16[272,128]{1,0:T(8,128)(2,1)S(1)}, bf16[272,128]{1,0:T(8,128)(2,1)S(1)}, u32[]{:S(2)}, u32[]{:S(2)}) collective-permute-start(bf16[272,128]{1,0:T(8,128)(2,1)S(1)} %get-tuple-element.35), channel_id=1, source_target_pairs={{0,3},{1,2},{2,1},{3,0},{4,7},{5,6},{6,5},{7,4},{8,11},{9,10},{10,... | collective-permute-start | bytes 208904 | tf_op jit(solution)/shard_map/ppermute | solution.py:294
  21.0 5.6 %collective-permute-start.7 = (bf16[272,128]{1,0:T(8,128)(2,1)S(1)}, bf16[272,128]{1,0:T(8,128)(2,1)S(1)}, u32[]{:S(2)}, u32[]{:S(2)}) collective-permute-start(bf16[272,128]{1,0:T(8,128)(2,1)S(1)} %get-tuple-element.36), channel_id=1, source_target_pairs={{0,1},{1,0},{2,3},{3,2},{4,5},{5,4},{6,7},{7,6},{8,9},{9,8},{10,11... | collective-permute-start | bytes 208904 | tf_op jit(solution)/shard_map/ppermute | solution.py:294

commit v4 on v3

--- a/solution.py
+++ b/solution.py
@@ -137,7 +137,7 @@
         out_ref[n, tiles - 1] = square_tile(squares[n], 0)
 
 
-def rows_kernel(trivial, where_ref, tab_ref, r_ref, own_ref, sibling_ref, stay_ref, swapped_ref, *refs):
+def rows_kernel(trivial, order, where_ref, tab_ref, r_ref, own_ref, sibling_ref, stay_ref, swapped_ref, *refs):
     owners = stay_ref.shape[0] + 1
     out_refs, acc_ref, w_refs = refs[:owners], refs[owners], refs[owners + 1 :]
     tiles, rows, cols = own_ref.shape
@@ -149,16 +149,16 @@
         acc_ref[0, at : at + rows] = own_ref[tile]
         acc_ref[0, at + rows : at + 2 * rows] = sibling_ref[tile]
     acc_ref[0, last:] = own_ref[tiles - 1] + sibling_ref[tiles - 1]
-    for n in range(owners - 1):
+    for n, k in enumerate(order):
         for g in range(len(trivial)):
             low = (g * (owners - 1) + n) * rows
             for part in range(2):
                 at = 2 * rows * (2 * g + part)
-                acc_ref[n + 1, at : at + rows] = stay_ref[n, 2 * g + part]
-                acc_ref[n + 1, at + rows : at + 2 * rows] = total[
+                acc_ref[k, at : at + rows] = stay_ref[n, 2 * g + part]
+                acc_ref[k, at + rows : at + 2 * rows] = total[
                     low : low + rows, part * cols : (part + 1) * cols
                 ]
-        acc_ref[n + 1, last:] = stay_ref[n, tiles - 1] + square_tile(squares[n], 1)
+        acc_ref[k, last:] = stay_ref[n, tiles - 1] + square_tile(squares[n], 1)
     for q, out_ref in enumerate(out_refs):
         out_ref[...] = acc_ref[jnp.bitwise_xor(where_ref[0], q)].astype(out_ref.dtype)
 
@@ -232,7 +232,7 @@
     tile = lambda dtype: jax.ShapeDtypeStruct((tiles, rows, cols), dtype)
     payload = lambda dtype: jax.ShapeDtypeStruct((2 * rows * (tiles - 1) + rows, cols), dtype)
     w_scratch = lambda count: [pltpu.VMEM((groups * count * rows, 2 * sites), jnp.bfloat16)] * colours
-    small = pl.CostEstimate(flops=2**20, bytes_accessed=2**20, transcendentals=0)
+    small = pl.CostEstimate(flops=0, bytes_accessed=0, transcendentals=0)
     params = pltpu.CompilerParams(vmem_limit_bytes=12 * 2**20)
 
     one = lambda *lead: jax.ShapeDtypeStruct(lead + vectors.shape[1:], vectors.dtype)
@@ -244,7 +244,8 @@
         cost_estimate=small,
         compiler_params=params,
     )(vectors)
-    slabs = [swapped(slab, 2 * k) for k, slab in enumerate(slabs, 1)]
+    order = (3, 2, 1)
+    slabs = [swapped(slabs[k - 1], 2 * k) for k in order]
     sibling = swapped(sibling, 1)
 
     right, own_sums, sibling_sums = pl.pallas_call(
@@ -281,7 +282,7 @@
         compiler_params=params,
     )(core, table, right, *slabs)
     own, *others = pl.pallas_call(
-        functools.partial(rows_kernel, trivial),
+        functools.partial(rows_kernel, trivial, order),
         out_shape=[payload(jnp.float32)] + [payload(jnp.bfloat16)] * (space - 1),
         in_specs=scalar() + in_vmem(6),
         out_specs=in_vmem(space),

time: 27.7 us -> 27.5 us (level)
    ppermute x5, waiting for transfers between devices: 7.63 us -> 7.35 us  [swapped(): return lax.ppermute(mine, 'tm', [(i, i ^ r) for i in range(tm)])]
  transfers between devices with their start and end apart: 8 -> 8, of which waited for: 7 -> 8; matrix products, arithmetic and copies ran while one was open for 3% -> 3% of each run, Pallas kernels for 4% -> 4%
where the time goes in v4:
time: 27.5 us; the launch traced here: 27.3 us
  waiting for transfers between devices  12.8 us (47%)
  starting transfers between devices  8.91 us (32%)
  local copies, waits for them, and re-layouts  2.98 us (11%)
  Pallas kernels  2.55 us (9%)
    ppermute x5, waiting for transfers between devices, swapped(): return lax.ppermute(mine, 'tm', [(i, i ^ r) for i in range(tm)])  7.35 us
    ppermute x3, waiting for transfers between devices, per_device_permutes(): lax.ppermute(others[q - 1], 'space', [(i, i ^ q) for i in range(space)])  5.41 us
    ppermute x5, starting transfers between devices, swapped(): return lax.ppermute(mine, 'tm', [(i, i ^ r) for i in range(tm)])  4.68 us
    ppermute x3, starting transfers between devices, per_device_permutes(): lax.ppermute(others[q - 1], 'space', [(i, i ^ q) for i in range(space)])  4.23 us
    unnamed x4, local copies, waits for them, and re-layouts  2.27 us
    pallas_call x1, Pallas kernels, per_device_permutes(): pl.pallas_call(functools.partial(finish_kernel, group), out_shape=jax.Sha...  0.86 us
    squeeze x1, local copies, waits for them, and re-layouts, per_device_permutes(): table = lax.dynamic_index_in_dim(jnp.asarray(tables), z, 0, keepdims=False)  0.72 us
    pallas_call x1, Pallas kernels, per_device_permutes(): pl.pallas_call(functools.partial(first_kernel, trivial), out_shape=[jax.S...  0.6 us
  transfers between devices with their start and end apart: 8, of which 8 were waited for; matrix products, arithmetic and copies ran while one was open for 3% of the time, Pallas kernels for 4%

profile of v4, /device:TPU:0, one launch (start us, length us, event | category | flops | bytes accessed | tf_op | source)
XLA Modules:
  0.0 27.3 jit_solution(2133321605077850941)
XLA Ops:
  0.0 1.1 %copy-done = bf16[8,2,16,3,512]{4,2,3,1,0:T(8,128)(2,1)S(1)} copy-done((bf16[8,2,16,3,512]{4,2,3,1,0:T(8,128)(2,1)S(1)}, bf16[8,2,16,3,512]{4,2,3,1,0:T(8,128)(2,1)}, u32[]{:S(2)}) %copy-start) | copy-done | bytes 786456
  1.1 0.1 shard_map.37
  1.2 4.0 %collective-permute-start.1 = (bf16[2,2,3,16,512]{4,3,2,1,0:T(8,128)(2,1)S(1)}, bf16[2,2,3,16,512]{4,3,2,1,0:T(8,128)(2,1)S(1)}, u32[]{:S(2)}, u32[]{:S(2)}) collective-permute-start(bf16[2,2,3,16,512]{4,3,2,1,0:T(8,128)(2,1)S(1)} %get-tuple-element.25), channel_id=1, source_target_pairs={{0,24},{4,28},{8,16},{12,20},{16,8},{20,12},{24,0},{28,4},{1,25},{... | collective-permute-start | bytes 589832 | tf_op jit(solution)/shard_map/ppermute | solution.py:229
  5.1 0.5 %collective-permute-start.2 = (bf16[2,2,3,16,512]{4,3,2,1,0:T(8,128)(2,1)S(1)}, bf16[2,2,3,16,512]{4,3,2,1,0:T(8,128)(2,1)S(1)}, u32[]{:S(2)}, u32[]{:S(2)}) collective-permute-start(bf16[2,2,3,16,512]{4,3,2,1,0:T(8,128)(2,1)S(1)} %get-tuple-element.26), channel_id=1, source_target_pairs={{0,16},{4,20},{8,24},{12,28},{16,0},{20,4},{24,8},{28,12},{1,17},{... | collective-permute-start | bytes 589832 | tf_op jit(solution)/shard_map/ppermute | solution.py:229
  5.7 0.1 collective-permute-start.3
  5.8 0.0 collective-permute-start
  5.8 0.7 %dynamic-slice_bitcast_fusion.tab_ref = f32[8,512]{1,0:T(8,128)S(1)} fusion(f32[4,8,512]{2,1,0:T(8,128)} %constant.40.clone, s32[]{:T(128)S(6)} %select_n.17), kind=kLoop, calls=%fused_computation | loop fusion | bytes 32772 | tf_op jit(solution)/shard_map/jit(dynamic_index_in_dim)/squeeze | solution.py:222
  6.5 0.6 %collective-permute-done.refs_1_ = bf16[2,3,16,512]{3,2,1,0:T(8,128)(2,1)S(1)} collective-permute-done((bf16[2,3,16,512]{3,2,1,0:T(8,128)(2,1)S(1)}, bf16[2,3,16,512]{3,2,1,0:T(8,128)(2,1)S(1)}, u32[]{:S(2)}, u32[]{:S(2)}) %collective-permute-start) | collective-permute-done | bytes 98336 | tf_op jit(solution)/shard_map/ppermute | solution.py:229
  7.1 1.1 %copy-done.1 = bf16[1,2,128,3,512]{4,2,3,1,0:T(8,128)(2,1)S(1)} copy-done((bf16[1,2,128,3,512]{4,2,3,1,0:T(8,128)(2,1)S(1)}, bf16[1,2,128,3,512]{4,2,3,1,0:T(8,128)(2,1)}, u32[]{:S(2)}) %copy-start.1) | copy-done | bytes 786456
  8.2 0.6 %shard_map.38 = (bf16[3,1024,256]{2,1,0:T(8,128)(2,1)S(1)}, f32[9,16,128]{2,1,0:T(8,128)S(1)}, f32[9,16,128]{2,1,0:T(8,128)S(1)}) custom-call(f32[8,512]{1,0:T(8,128)S(1)} %dynamic-slice_bitcast_fusion.tab_ref, bf16[2,3,128,512]{3,2,1,0:T(8,128)(2,1)S(1)} %bitcast.12, bf16[2,3,16,512]{3,2,1,0:T(8,128)(2,1)S(1)} %get-tuple-element.21.refs_0_, ...), custom_call_target="tpu_custom_call" | custom-call | tf_op jit(solution)/shard_map/pallas_call | solution.py:251
  8.8 2.1 %collective-permute-done.1.refs_0_ = bf16[2,2,3,16,512]{4,3,2,1,0:T(8,128)(2,1)S(1)} collective-permute-done((bf16[2,2,3,16,512]{4,3,2,1,0:T(8,128)(2,1)S(1)}, bf16[2,2,3,16,512]{4,3,2,1,0:T(8,128)(2,1)S(1)}, u32[]{:S(2)}, u32[]{:S(2)}) %collective-permute-start.1) | collective-permute-done | bytes 196640 | tf_op jit(solution)/shard_map/ppermute | solution.py:229
  10.9 3.3 %collective-permute-done.2.refs_1_ = bf16[2,2,3,16,512]{4,3,2,1,0:T(8,128)(2,1)S(1)} collective-permute-done((bf16[2,2,3,16,512]{4,3,2,1,0:T(8,128)(2,1)S(1)}, bf16[2,2,3,16,512]{4,3,2,1,0:T(8,128)(2,1)S(1)}, u32[]{:S(2)}, u32[]{:S(2)}) %collective-permute-start.2) | collective-permute-done | bytes 196640 | tf_op jit(solution)/shard_map/ppermute | solution.py:229
  14.3 0.3 %collective-permute-done.3.refs_2_ = bf16[2,2,3,16,512]{4,3,2,1,0:T(8,128)(2,1)S(1)} collective-permute-done((bf16[2,2,3,16,512]{4,3,2,1,0:T(8,128)(2,1)S(1)}, bf16[2,2,3,16,512]{4,3,2,1,0:T(8,128)(2,1)S(1)}, u32[]{:S(2)}, u32[]{:S(2)}) %collective-permute-start.3) | collective-permute-done | bytes 196640 | tf_op jit(solution)/shard_map/ppermute | solution.py:229
  14.6 0.1 collective-permute-start.4
  14.7 0.5 %shard_map.39.stay_ref = f32[3,9,16,128]{3,2,1,0:T(8,128)S(1)} custom-call(s32[1]{0:T(128)} %bitcast.core_ref, f32[8,512]{1,0:T(8,128)S(1)} %dynamic-slice_bitcast_fusion.tab_ref, bf16[3,1024,256]{2,1,0:T(8,128)(2,1)S(1)} %get-tuple-element.23.r_ref, bf16[2,2,3,16,512]{4,3,2,1,0:T(8,128)(2,1)S(1)} %collective-permute-done.1.refs_0_, ...), custom_call_target="tpu_custom_call" | custom-call | tf_op jit(solution)/shard_map/pallas_call | solution.py:275
  15.2 1.0 %collective-permute-done.4.swapped_ref = bf16[3,2,3,16,512]{4,3,2,1,0:T(8,128)(2,1)S(1)} collective-permute-done((bf16[3,2,3,16,512]{4,3,2,1,0:T(8,128)(2,1)S(1)}, bf16[3,2,3,16,512]{4,3,2,1,0:T(8,128)(2,1)S(1)}, u32[]{:S(2)}, u32[]{:S(2)}) %collective-permute-start.4) | collective-permute-done | bytes 294944 | tf_op jit(solution)/shard_map/ppermute | solution.py:229
  16.2 0.5 %shard_map.41 = (f32[272,128]{1,0:T(8,128)S(1)}, bf16[272,128]{1,0:T(8,128)(2,1)S(1)}, bf16[272,128]{1,0:T(8,128)(2,1)S(1)}, bf16[272,128]{1,0:T(8,128)(2,1)S(1)}) custom-call(s32[1]{0:T(128)} %bitcast.1.where_ref, f32[8,512]{1,0:T(8,128)S(1)} %dynamic-slice_bitcast_fusion.tab_ref, bf16[3,1024,256]{2,1,0:T(8,128)(2,1)S(1)} %get-tuple-element.23.r_ref, ...), custom_call_target="tpu_custom_call" | custom-call | tf_op jit(solution)/shard_map/pallas_call | solution.py:284
  16.8 2.7 %collective-permute-start.5 = (bf16[272,128]{1,0:T(8,128)(2,1)S(1)}, bf16[272,128]{1,0:T(8,128)(2,1)S(1)}, u32[]{:S(2)}, u32[]{:S(2)}) collective-permute-start(bf16[272,128]{1,0:T(8,128)(2,1)S(1)} %get-tuple-element.34), channel_id=1, source_target_pairs={{0,2},{1,3},{2,0},{3,1},{4,6},{5,7},{6,4},{7,5},{8,10},{9,11},{10,... | collective-permute-start | bytes 208904 | tf_op jit(solution)/shard_map/ppermute | solution.py:295
  19.4 1.3 %collective-permute-start.6 = (bf16[272,128]{1,0:T(8,128)(2,1)S(1)}, bf16[272,128]{1,0:T(8,128)(2,1)S(1)}, u32[]{:S(2)}, u32[]{:S(2)}) collective-permute-start(bf16[272,128]{1,0:T(8,128)(2,1)S(1)} %get-tuple-element.35), channel_id=1, source_target_pairs={{0,3},{1,2},{2,1},{3,0},{4,7},{5,6},{6,5},{7,4},{8,11},{9,10},{10,... | collective-permute-start | bytes 208904 | tf_op jit(solution)/shard_map/ppermute | solution.py:295
  20.8 0.2 collective-permute-start.7
  21.0 3.7 %collective-permute-done.5.refs_1_ = bf16[272,128]{1,0:T(8,128)(2,1)S(1)} collective-permute-done((bf16[272,128]{1,0:T(8,128)(2,1)S(1)}, bf16[272,128]{1,0:T(8,128)(2,1)S(1)}, u32[]{:S(2)}, u32[]{:S(2)}) %collective-permute-start.5) | collective-permute-done | bytes 69664 | tf_op jit(solution)/shard_map/ppermute | solution.py:295
  24.7 1.2 %collective-permute-done.6.refs_2_ = bf16[272,128]{1,0:T(8,128)(2,1)S(1)} collective-permute-done((bf16[272,128]{1,0:T(8,128)(2,1)S(1)}, bf16[272,128]{1,0:T(8,128)(2,1)S(1)}, u32[]{:S(2)}, u32[]{:S(2)}) %collective-permute-start.6) | collective-permute-done | bytes 69664 | tf_op jit(solution)/shard_map/ppermute | solution.py:295
  25.9 0.5 %collective-permute-done.7.refs_3_ = bf16[272,128]{1,0:T(8,128)(2,1)S(1)} collective-permute-done((bf16[272,128]{1,0:T(8,128)(2,1)S(1)}, bf16[272,128]{1,0:T(8,128)(2,1)S(1)}, u32[]{:S(2)}, u32[]{:S(2)}) %collective-permute-start.7) | collective-permute-done | bytes 69664 | tf_op jit(solution)/shard_map/ppermute | solution.py:295
  26.4 0.9 %shard_map.42 = f32[8,64,128]{2,1,0:T(8,128)} custom-call(s32[1]{0:T(128)} %bitcast.core_ref, f32[272,128]{1,0:T(8,128)S(1)} %get-tuple-element.33.refs_0_, bf16[272,128]{1,0:T(8,128)(2,1)S(1)} %collective-permute-done.5.refs_1_, bf16[272,128]{1,0:T(8,128)(2,1)S(1)} %collective-permute-done.6.refs_2_, bf16[272,128]{1,0:T(8,128)(2,1)S(1)} %collective-permute-done.7.refs_3_), custom_call_target="tpu_custom_call" | custom-call | tf_op jit(solution)/shard_map/pallas_call | solution.py:296
  (3 shorter events, 0.0 us)
Async XLA Ops:
  0.0 1.1 %copy-start = (bf16[8,2,16,3,512]{4,2,3,1,0:T(8,128)(2,1)S(1)}, bf16[8,2,16,3,512]{4,2,3,1,0:T(8,128)(2,1)}, u32[]{:S(2)}) copy-start(bf16[8,2,16,3,512]{4,2,3,1,0:T(8,128)(2,1)} %param.3) | copy-start | bytes 2359300
  1.2 9.7 %collective-permute-start.1 = (bf16[2,2,3,16,512]{4,3,2,1,0:T(8,128)(2,1)S(1)}, bf16[2,2,3,16,512]{4,3,2,1,0:T(8,128)(2,1)S(1)}, u32[]{:S(2)}, u32[]{:S(2)}) collective-permute-start(bf16[2,2,3,16,512]{4,3,2,1,0:T(8,128)(2,1)S(1)} %get-tuple-element.25), channel_id=1, source_target_pairs={{0,24},{4,28},{8,16},{12,20},{16,8},{20,12},{24,0},{28,4},{1,25},{... | collective-permute-start | bytes 589832 | tf_op jit(solution)/shard_map/ppermute | solution.py:229
  5.1 9.1 %collective-permute-start.2 = (bf16[2,2,3,16,512]{4,3,2,1,0:T(8,128)(2,1)S(1)}, bf16[2,2,3,16,512]{4,3,2,1,0:T(8,128)(2,1)S(1)}, u32[]{:S(2)}, u32[]{:S(2)}) collective-permute-start(bf16[2,2,3,16,512]{4,3,2,1,0:T(8,128)(2,1)S(1)} %get-tuple-element.26), channel_id=1, source_target_pairs={{0,16},{4,20},{8,24},{12,28},{16,0},{20,4},{24,8},{28,12},{1,17},{... | collective-permute-start | bytes 589832 | tf_op jit(solution)/shard_map/ppermute | solution.py:229
  5.7 8.9 %collective-permute-start.3 = (bf16[2,2,3,16,512]{4,3,2,1,0:T(8,128)(2,1)S(1)}, bf16[2,2,3,16,512]{4,3,2,1,0:T(8,128)(2,1)S(1)}, u32[]{:S(2)}, u32[]{:S(2)}) collective-permute-start(bf16[2,2,3,16,512]{4,3,2,1,0:T(8,128)(2,1)S(1)} %get-tuple-element.27), channel_id=1, source_target_pairs={{0,8},{4,12},{8,0},{12,4},{16,24},{20,28},{24,16},{28,20},{1,9},{5... | collective-permute-start | bytes 589832 | tf_op jit(solution)/shard_map/ppermute | solution.py:229
  5.8 1.3 %collective-permute-start = (bf16[2,3,16,512]{3,2,1,0:T(8,128)(2,1)S(1)}, bf16[2,3,16,512]{3,2,1,0:T(8,128)(2,1)S(1)}, u32[]{:S(2)}, u32[]{:S(2)}) collective-permute-start(bf16[2,3,16,512]{3,2,1,0:T(8,128)(2,1)S(1)} %get-tuple-element.22), channel_id=1, source_target_pairs={{0,4},{4,0},{8,12},{12,8},{16,20},{20,16},{24,28},{28,24},{1,5},{5... | collective-permute-start | bytes 294920 | tf_op jit(solution)/shard_map/ppermute | solution.py:229
  7.1 1.1 %copy-start.1 = (bf16[1,2,128,3,512]{4,2,3,1,0:T(8,128)(2,1)S(1)}, bf16[1,2,128,3,512]{4,2,3,1,0:T(8,128)(2,1)}, u32[]{:S(2)}) copy-start(bf16[1,2,128,3,512]{4,2,3,1,0:T(8,128)(2,1)} %param.4) | copy-start | bytes 2359300
  14.6 1.6 %collective-permute-start.4 = (bf16[3,2,3,16,512]{4,3,2,1,0:T(8,128)(2,1)S(1)}, bf16[3,2,3,16,512]{4,3,2,1,0:T(8,128)(2,1)S(1)}, u32[]{:S(2)}, u32[]{:S(2)}) collective-permute-start(bf16[3,2,3,16,512]{4,3,2,1,0:T(8,128)(2,1)S(1)} %shard_map.40), channel_id=1, source_target_pairs={{0,4},{4,0},{8,12},{12,8},{16,20},{20,16},{24,28},{28,24},{1,5},{5... | collective-permute-start | bytes 884744 | tf_op jit(solution)/shard_map/ppermute | solution.py:229
  16.8 8.0 %collective-permute-start.5 = (bf16[272,128]{1,0:T(8,128)(2,1)S(1)}, bf16[272,128]{1,0:T(8,128)(2,1)S(1)}, u32[]{:S(2)}, u32[]{:S(2)}) collective-permute-start(bf16[272,128]{1,0:T(8,128)(2,1)S(1)} %get-tuple-element.34), channel_id=1, source_target_pairs={{0,2},{1,3},{2,0},{3,1},{4,6},{5,7},{6,4},{7,5},{8,10},{9,11},{10,... | collective-permute-start | bytes 208904 | tf_op jit(solution)/shard_map/ppermute | solution.py:295
  19.4 6.5 %collective-permute-start.6 = (bf16[272,128]{1,0:T(8,128)(2,1)S(1)}, bf16[272,128]{1,0:T(8,128)(2,1)S(1)}, u32[]{:S(2)}, u32[]{:S(2)}) collective-permute-start(bf16[272,128]{1,0:T(8,128)(2,1)S(1)} %get-tuple-element.35), channel_id=1, source_target_pairs={{0,3},{1,2},{2,1},{3,0},{4,7},{5,6},{6,5},{7,4},{8,11},{9,10},{10,... | collective-permute-start | bytes 208904 | tf_op jit(solution)/shard_map/ppermute | solution.py:295
  20.8 5.6 %collective-permute-start.7 = (bf16[272,128]{1,0:T(8,128)(2,1)S(1)}, bf16[272,128]{1,0:T(8,128)(2,1)S(1)}, u32[]{:S(2)}, u32[]{:S(2)}) collective-permute-start(bf16[272,128]{1,0:T(8,128)(2,1)S(1)} %get-tuple-element.36), channel_id=1, source_target_pairs={{0,1},{1,0},{2,3},{3,2},{4,5},{5,4},{6,7},{7,6},{8,9},{9,8},{10,11... | collective-permute-start | bytes 208904 | tf_op jit(solution)/shard_map/ppermute | solution.py:295

commit v5 on v4

--- a/solution.py
+++ b/solution.py
@@ -123,42 +123,49 @@
         out_ref[n] = slab_ref[1 - core_ref[0]]
 
 
-def stay_kernel(trivial, core_ref, tab_ref, r_ref, *refs):
-    slabs = len(refs) - 4
-    slab_refs, out_ref, w_refs = refs[:slabs], refs[slabs], refs[slabs + 1 :]
-    tiles, rows, cols = out_ref.shape[1:]
-    v_refs = [slab_ref.at[core_ref[0]] for slab_ref in slab_refs]
+def sums_kernel(trivial, half, core_ref, tab_ref, r_ref, *refs):
+    given = len(refs) - 1 - r_ref.shape[0]
+    out_ref, w_refs = refs[given], refs[given + 1 :]
+    count, tiles, rows, cols = out_ref.shape
+    if half == 0:
+        v_refs = [slab_ref.at[core_ref[0]] for slab_ref in refs[:given]]
+    else:
+        v_refs = [refs[0].at[n] for n in range(count)]
     total, squares = project_rows(trivial, v_refs, tab_ref, lambda colour: r_ref[colour], w_refs)
-    for n in range(slabs):
+    for n in range(count):
         for g in range(len(trivial)):
-            low = (g * slabs + n) * rows
+            low = (g * count + n) * rows
             for part in range(2):
                 out_ref[n, 2 * g + part] = total[low : low + rows, part * cols : (part + 1) * cols]
-        out_ref[n, tiles - 1] = square_tile(squares[n], 0)
-
-
-def rows_kernel(trivial, order, where_ref, tab_ref, r_ref, own_ref, sibling_ref, stay_ref, swapped_ref, *refs):
-    owners = stay_ref.shape[0] + 1
-    out_refs, acc_ref, w_refs = refs[:owners], refs[owners], refs[owners + 1 :]
+        out_ref[n, tiles - 1] = square_tile(squares[n], half)
+
+
+def rows_kernel(trivial, order, where_ref, tab_ref, r_ref, *refs):
+    own_ref, sibling_ref, stay_ref, came_ref, last_stay_ref, last_v_ref = refs[:6]
+    owners = len(order) + 1
+    early = stay_ref.shape[0]
+    late = owners - 1 - early
+    out_refs, acc_ref, w_refs = refs[6 : 6 + owners], refs[6 + owners], refs[7 + owners :]
     tiles, rows, cols = own_ref.shape
-    v_refs = [swapped_ref.at[n] for n in range(owners - 1)]
+    v_refs = [last_v_ref.at[n] for n in range(late)]
     total, squares = project_rows(trivial, v_refs, tab_ref, lambda colour: r_ref[colour], w_refs)
-    last = 2 * rows * (tiles - 1)
-    for tile in range(tiles - 1):
-        at = 2 * rows * tile
-        acc_ref[0, at : at + rows] = own_ref[tile]
-        acc_ref[0, at + rows : at + 2 * rows] = sibling_ref[tile]
-    acc_ref[0, last:] = own_ref[tiles - 1] + sibling_ref[tiles - 1]
-    for n, k in enumerate(order):
-        for g in range(len(trivial)):
-            low = (g * (owners - 1) + n) * rows
-            for part in range(2):
-                at = 2 * rows * (2 * g + part)
-                acc_ref[k, at : at + rows] = stay_ref[n, 2 * g + part]
-                acc_ref[k, at + rows : at + 2 * rows] = total[
-                    low : low + rows, part * cols : (part + 1) * cols
-                ]
-        acc_ref[k, last:] = stay_ref[n, tiles - 1] + square_tile(squares[n], 1)
+    halves = [(0, [own_ref[n] for n in range(tiles)], [sibling_ref[n] for n in range(tiles)])]
+    for n, k in enumerate(order[:early]):
+        halves.append((k, [stay_ref[n, i] for i in range(tiles)], [came_ref[n, i] for i in range(tiles)]))
+    for n, k in enumerate(order[early:]):
+        right = [
+            total[(g * late + n) * rows : (g * late + n + 1) * rows, part * cols : (part + 1) * cols]
+            for g in range(len(trivial))
+            for part in range(2)
+        ]
+        right.append(square_tile(squares[n], 1))
+        halves.append((k, [last_stay_ref[n, i] for i in range(tiles)], right))
+    for k, left, right in halves:
+        for tile in range(tiles - 1):
+            at = 2 * rows * tile
+            acc_ref[k, at : at + rows] = left[tile]
+            acc_ref[k, at + rows : at + 2 * rows] = right[tile]
+        acc_ref[k, 2 * rows * (tiles - 1) :] = left[tiles - 1] + right[tiles - 1]
     for q, out_ref in enumerate(out_refs):
         out_ref[...] = acc_ref[jnp.bitwise_xor(where_ref[0], q)].astype(out_ref.dtype)
 
@@ -244,7 +251,7 @@
         cost_estimate=small,
         compiler_params=params,
     )(vectors)
-    order = (3, 2, 1)
+    order, cut = (2, 1, 3), 2
     slabs = [swapped(slabs[k - 1], 2 * k) for k in order]
     sibling = swapped(sibling, 1)
 
@@ -261,35 +268,42 @@
 
     where = jnp.bitwise_xor(me // 2, z).astype(jnp.int32).reshape(1)
     core = (me % 2).astype(jnp.int32).reshape(1)
-    own_sums, slabs = lax.optimization_barrier((own_sums, slabs))
-    part = jax.ShapeDtypeStruct((space - 1,) + slabs[0].shape[1:], slabs[0].dtype)
-    leaving = pl.pallas_call(
-        part_kernel,
-        out_shape=part,
-        in_specs=scalar() + in_vmem(len(slabs)),
-        out_specs=in_vmem(1)[0],
-        cost_estimate=small,
-        compiler_params=params,
-    )(core, *slabs)
-    came = swapped(leaving, 1)
-    stay_sums = pl.pallas_call(
-        functools.partial(stay_kernel, trivial),
-        out_shape=jax.ShapeDtypeStruct((space - 1, tiles, rows, cols), jnp.float32),
-        in_specs=scalar() + in_vmem(2 + len(slabs)),
-        out_specs=in_vmem(1)[0],
-        scratch_shapes=w_scratch(len(slabs)),
-        cost_estimate=small,
-        compiler_params=params,
-    )(core, table, right, *slabs)
+    def part_of(slabs):
+        leaving = pl.pallas_call(
+            part_kernel,
+            out_shape=one(len(slabs)),
+            in_specs=scalar() + in_vmem(len(slabs)),
+            out_specs=in_vmem(1)[0],
+            cost_estimate=small,
+            compiler_params=params,
+        )(core, *slabs)
+        return swapped(leaving, 1)
+
+    def sums_of(half, count, *pieces):
+        return pl.pallas_call(
+            functools.partial(sums_kernel, trivial, half),
+            out_shape=jax.ShapeDtypeStruct((count, tiles, rows, cols), jnp.float32),
+            in_specs=scalar() + in_vmem(2 + len(pieces)),
+            out_specs=in_vmem(1)[0],
+            scratch_shapes=w_scratch(count),
+            cost_estimate=small,
+            compiler_params=params,
+        )(core, table, right, *pieces)
+
+    own_sums, early = lax.optimization_barrier((own_sums, slabs[:cut]))
+    stay_sums = sums_of(0, len(early), *early)
+    came_sums = sums_of(1, len(early), part_of(early))
+    stay_sums, late = lax.optimization_barrier((stay_sums, slabs[cut:]))
+    last_sums = sums_of(0, len(late), *late)
     own, *others = pl.pallas_call(
         functools.partial(rows_kernel, trivial, order),
         out_shape=[payload(jnp.float32)] + [payload(jnp.bfloat16)] * (space - 1),
-        in_specs=scalar() + in_vmem(6),
+        in_specs=scalar() + in_vmem(8),
         out_specs=in_vmem(space),
-        scratch_shapes=[pltpu.VMEM((space,) + payload(jnp.float32).shape, jnp.float32)] + w_scratch(space - 1),
+        scratch_shapes=[pltpu.VMEM((space,) + payload(jnp.float32).shape, jnp.float32)] + w_scratch(len(late)),
         cost_estimate=small,
         compiler_params=params,
-    )(where, table, right, own_sums, sibling_sums, stay_sums, came)
+    )(where, table, right, own_sums, sibling_sums, stay_sums, came_sums, last_sums, part_of(late))
     parts = [own]
     for q in (2, 3, 1):
         parts.append(lax.ppermute(others[q - 1], "space", [(i, i ^ q) for i in range(space)]))

time: 27.5 us -> 27.2 us (0.989)
  waiting for transfers between devices: 12.8 us -> 11.7 us
  Pallas kernels: 2.55 us -> 3.1 us
    ppermute x5 -> x6, waiting for transfers between devices: 7.35 us -> 6.36 us  [swapped(): return lax.ppermute(mine, 'tm', [(i, i ^ r) for i in range(tm)])]
    pallas_call x2 -> x5, Pallas kernels: 0.52 us -> 1.17 us  [the longest x3 1.15 us: sums_of(): pl.pallas_call(functools.partial(sums_kernel, trivial, half), out_shape=j...]
    ppermute x5 -> x6, starting transfers between devices: 4.68 us -> 4.72 us  [swapped(): return lax.ppermute(mine, 'tm', [(i, i ^ r) for i in range(tm)])]
  transfers between devices with their start and end apart: 8 -> 9, of which waited for: 8 -> 8; matrix products, arithmetic and copies ran while one was open for 3% -> 3% of each run, Pallas kernels for 4% -> 7%
where the time goes in v5:
time: 27.2 us; the launch traced here: 26.9 us
  waiting for transfers between devices  11.7 us (43%)
  starting transfers between devices  9.1 us (33%)
  Pallas kernels  3.1 us (11%)
  local copies, waits for them, and re-layouts  2.98 us (11%)
    ppermute x6, waiting for transfers between devices, swapped(): return lax.ppermute(mine, 'tm', [(i, i ^ r) for i in range(tm)])  6.36 us
    ppermute x3, waiting for transfers between devices, per_device_permutes(): lax.ppermute(others[q - 1], 'space', [(i, i ^ q) for i in range(space)])  5.29 us
    ppermute x6, starting transfers between devices, swapped(): return lax.ppermute(mine, 'tm', [(i, i ^ r) for i in range(tm)])  4.72 us
    ppermute x3, starting transfers between devices, per_device_permutes(): lax.ppermute(others[q - 1], 'space', [(i, i ^ q) for i in range(space)])  4.38 us
    unnamed x4, local copies, waits for them, and re-layouts  2.27 us
    pallas_call x3, Pallas kernels, sums_of(): pl.pallas_call(functools.partial(sums_kernel, trivial, half), out_shape=j...  1.15 us
    pallas_call x1, Pallas kernels, per_device_permutes(): pl.pallas_call(functools.partial(finish_kernel, group), out_shape=jax.Sha...  0.86 us
    squeeze x1, local copies, waits for them, and re-layouts, per_device_permutes(): table = lax.dynamic_index_in_dim(jnp.asarray(tables), z, 0, keepdims=False)  0.72 us
  transfers between devices with their start and end apart: 9, of which 8 were waited for; matrix products, arithmetic and copies ran while one was open for 3% of the time, Pallas kernels for 7%

profile of v5, /device:TPU:0, one launch (start us, length us, event | category | flops | bytes accessed | tf_op | source)
XLA Modules:
  0.0 26.9 jit_solution(11655718996395032751)
XLA Ops:
  0.0 1.1 %copy-done = bf16[8,2,16,3,512]{4,2,3,1,0:T(8,128)(2,1)S(1)} copy-done((bf16[8,2,16,3,512]{4,2,3,1,0:T(8,128)(2,1)S(1)}, bf16[8,2,16,3,512]{4,2,3,1,0:T(8,128)(2,1)}, u32[]{:S(2)}) %copy-start) | copy-done | bytes 786456
  1.2 3.0 %collective-permute-start.1 = (bf16[2,2,3,16,512]{4,3,2,1,0:T(8,128)(2,1)S(1)}, bf16[2,2,3,16,512]{4,3,2,1,0:T(8,128)(2,1)S(1)}, u32[]{:S(2)}, u32[]{:S(2)}) collective-permute-start(bf16[2,2,3,16,512]{4,3,2,1,0:T(8,128)(2,1)S(1)} %get-tuple-element.26), channel_id=1, source_target_pairs={{0,16},{4,20},{8,24},{12,28},{16,0},{20,4},{24,8},{28,12},{1,17},{... | collective-permute-start | bytes 589832 | tf_op jit(solution)/shard_map/ppermute | solution.py:236
  4.2 1.5 %collective-permute-start.2 = (bf16[2,2,3,16,512]{4,3,2,1,0:T(8,128)(2,1)S(1)}, bf16[2,2,3,16,512]{4,3,2,1,0:T(8,128)(2,1)S(1)}, u32[]{:S(2)}, u32[]{:S(2)}) collective-permute-start(bf16[2,2,3,16,512]{4,3,2,1,0:T(8,128)(2,1)S(1)} %get-tuple-element.27), channel_id=1, source_target_pairs={{0,8},{4,12},{8,0},{12,4},{16,24},{20,28},{24,16},{28,20},{1,9},{5... | collective-permute-start | bytes 589832 | tf_op jit(solution)/shard_map/ppermute | solution.py:236
  5.8 0.7 %dynamic-slice_bitcast_fusion.tab_ref = f32[8,512]{1,0:T(8,128)S(1)} fusion(f32[4,8,512]{2,1,0:T(8,128)} %constant.40.clone, s32[]{:T(128)S(6)} %select_n.17), kind=kLoop, calls=%fused_computation | loop fusion | bytes 32772 | tf_op jit(solution)/shard_map/jit(dynamic_index_in_dim)/squeeze | solution.py:229
  6.5 0.5 %collective-permute-done.refs_1_ = bf16[2,3,16,512]{3,2,1,0:T(8,128)(2,1)S(1)} collective-permute-done((bf16[2,3,16,512]{3,2,1,0:T(8,128)(2,1)S(1)}, bf16[2,3,16,512]{3,2,1,0:T(8,128)(2,1)S(1)}, u32[]{:S(2)}, u32[]{:S(2)}) %collective-permute-start) | collective-permute-done | bytes 98336 | tf_op jit(solution)/shard_map/ppermute | solution.py:236
  7.0 1.1 %copy-done.1 = bf16[1,2,128,3,512]{4,2,3,1,0:T(8,128)(2,1)S(1)} copy-done((bf16[1,2,128,3,512]{4,2,3,1,0:T(8,128)(2,1)S(1)}, bf16[1,2,128,3,512]{4,2,3,1,0:T(8,128)(2,1)}, u32[]{:S(2)}) %copy-start.1) | copy-done | bytes 786456
  8.2 0.6 %shard_map.38 = (bf16[3,1024,256]{2,1,0:T(8,128)(2,1)S(1)}, f32[9,16,128]{2,1,0:T(8,128)S(1)}, f32[9,16,128]{2,1,0:T(8,128)S(1)}) custom-call(f32[8,512]{1,0:T(8,128)S(1)} %dynamic-slice_bitcast_fusion.tab_ref, bf16[2,3,128,512]{3,2,1,0:T(8,128)(2,1)S(1)} %bitcast.12, bf16[2,3,16,512]{3,2,1,0:T(8,128)(2,1)S(1)} %get-tuple-element.22.refs_0_, ...), custom_call_target="tpu_custom_call" | custom-call | tf_op jit(solution)/shard_map/pallas_call | solution.py:258
  8.8 0.4 %collective-permute-done.1.refs_0_ = bf16[2,2,3,16,512]{4,3,2,1,0:T(8,128)(2,1)S(1)} collective-permute-done((bf16[2,2,3,16,512]{4,3,2,1,0:T(8,128)(2,1)S(1)}, bf16[2,2,3,16,512]{4,3,2,1,0:T(8,128)(2,1)S(1)}, u32[]{:S(2)}, u32[]{:S(2)}) %collective-permute-start.1) | collective-permute-done | bytes 196640 | tf_op jit(solution)/shard_map/ppermute | solution.py:236
  9.1 2.9 %collective-permute-done.2.refs_1_ = bf16[2,2,3,16,512]{4,3,2,1,0:T(8,128)(2,1)S(1)} collective-permute-done((bf16[2,2,3,16,512]{4,3,2,1,0:T(8,128)(2,1)S(1)}, bf16[2,2,3,16,512]{4,3,2,1,0:T(8,128)(2,1)S(1)}, u32[]{:S(2)}, u32[]{:S(2)}) %collective-permute-start.2) | collective-permute-done | bytes 196640 | tf_op jit(solution)/shard_map/ppermute | solution.py:236
  12.1 0.1 collective-permute-start.4
  12.1 0.4 %shard_map.39.refs_2_ = f32[2,9,16,128]{3,2,1,0:T(8,128)S(1)} custom-call(s32[1]{0:T(128)} %bitcast.core_ref, f32[8,512]{1,0:T(8,128)S(1)} %dynamic-slice_bitcast_fusion.tab_ref, bf16[3,1024,256]{2,1,0:T(8,128)(2,1)S(1)} %get-tuple-element.24.r_ref, bf16[2,2,3,16,512]{4,3,2,1,0:T(8,128)(2,1)S(1)} %collective-permute-done.1.refs_0_, ...), custom_call_target="tpu_custom_call" | custom-call | tf_op jit(solution)/shard_map/pallas_call | solution.py:283
  12.5 2.1 %collective-permute-done.3.refs_0_ = bf16[2,2,3,16,512]{4,3,2,1,0:T(8,128)(2,1)S(1)} collective-permute-done((bf16[2,2,3,16,512]{4,3,2,1,0:T(8,128)(2,1)S(1)}, bf16[2,2,3,16,512]{4,3,2,1,0:T(8,128)(2,1)S(1)}, u32[]{:S(2)}, u32[]{:S(2)}) %collective-permute-start.3) | collective-permute-done | bytes 196640 | tf_op jit(solution)/shard_map/ppermute | solution.py:236
  14.6 0.1 collective-permute-start.5
  14.7 0.4 %shard_map.42.refs_4_ = f32[1,9,16,128]{3,2,1,0:T(8,128)S(1)} custom-call(s32[1]{0:T(128)} %bitcast.core_ref, f32[8,512]{1,0:T(8,128)S(1)} %dynamic-slice_bitcast_fusion.tab_ref, bf16[3,1024,256]{2,1,0:T(8,128)(2,1)S(1)} %get-tuple-element.24.r_ref, bf16[2,2,3,16,512]{4,3,2,1,0:T(8,128)(2,1)S(1)} %collective-permute-done.3.refs_0_), custom_call_target="tpu_custom_call" | custom-call | tf_op jit(solution)/shard_map/pallas_call | solution.py:283
  15.1 0.4 %shard_map.41.refs_3_ = f32[2,9,16,128]{3,2,1,0:T(8,128)S(1)} custom-call(s32[1]{0:T(128)} %bitcast.core_ref, f32[8,512]{1,0:T(8,128)S(1)} %dynamic-slice_bitcast_fusion.tab_ref, bf16[3,1024,256]{2,1,0:T(8,128)(2,1)S(1)} %get-tuple-element.24.r_ref, bf16[2,2,3,16,512]{4,3,2,1,0:T(8,128)(2,1)S(1)} %collective-permute-done.4.refs_0_), custom_call_target="tpu_custom_call" | custom-call | tf_op jit(solution)/shard_map/pallas_call | solution.py:283
  15.5 0.5 %collective-permute-done.5.refs_5_ = bf16[1,2,3,16,512]{4,3,2,1,0:T(8,128)(2,1)S(1)} collective-permute-done((bf16[1,2,3,16,512]{4,3,2,1,0:T(8,128)(2,1)S(1)}, bf16[1,2,3,16,512]{4,3,2,1,0:T(8,128)(2,1)S(1)}, u32[]{:S(2)}, u32[]{:S(2)}) %collective-permute-start.5) | collective-permute-done | bytes 98336 | tf_op jit(solution)/shard_map/ppermute | solution.py:236
  16.0 0.4 %shard_map.44 = (f32[272,128]{1,0:T(8,128)S(1)}, bf16[272,128]{1,0:T(8,128)(2,1)S(1)}, bf16[272,128]{1,0:T(8,128)(2,1)S(1)}, bf16[272,128]{1,0:T(8,128)(2,1)S(1)}) custom-call(s32[1]{0:T(128)} %bitcast.1.where_ref, f32[8,512]{1,0:T(8,128)S(1)} %dynamic-slice_bitcast_fusion.tab_ref, bf16[3,1024,256]{2,1,0:T(8,128)(2,1)S(1)} %get-tuple-element.24.r_ref, ...), custom_call_target="tpu_custom_call" | custom-call | tf_op jit(solution)/shard_map/pallas_call | solution.py:298
  16.4 2.8 %collective-permute-start.6 = (bf16[272,128]{1,0:T(8,128)(2,1)S(1)}, bf16[272,128]{1,0:T(8,128)(2,1)S(1)}, u32[]{:S(2)}, u32[]{:S(2)}) collective-permute-start(bf16[272,128]{1,0:T(8,128)(2,1)S(1)} %get-tuple-element.36), channel_id=1, source_target_pairs={{0,2},{1,3},{2,0},{3,1},{4,6},{5,7},{6,4},{7,5},{8,10},{9,11},{10,... | collective-permute-start | bytes 208904 | tf_op jit(solution)/shard_map/ppermute | solution.py:309
  19.2 1.4 %collective-permute-start.7 = (bf16[272,128]{1,0:T(8,128)(2,1)S(1)}, bf16[272,128]{1,0:T(8,128)(2,1)S(1)}, u32[]{:S(2)}, u32[]{:S(2)}) collective-permute-start(bf16[272,128]{1,0:T(8,128)(2,1)S(1)} %get-tuple-element.37), channel_id=1, source_target_pairs={{0,3},{1,2},{2,1},{3,0},{4,7},{5,6},{6,5},{7,4},{8,11},{9,10},{10,... | collective-permute-start | bytes 208904 | tf_op jit(solution)/shard_map/ppermute | solution.py:309
  20.5 0.2 collective-permute-start.8
  20.8 2.7 %collective-permute-done.6.refs_1_ = bf16[272,128]{1,0:T(8,128)(2,1)S(1)} collective-permute-done((bf16[272,128]{1,0:T(8,128)(2,1)S(1)}, bf16[272,128]{1,0:T(8,128)(2,1)S(1)}, u32[]{:S(2)}, u32[]{:S(2)}) %collective-permute-start.6) | collective-permute-done | bytes 69664 | tf_op jit(solution)/shard_map/ppermute | solution.py:309
  23.4 2.3 %collective-permute-done.7.refs_2_ = bf16[272,128]{1,0:T(8,128)(2,1)S(1)} collective-permute-done((bf16[272,128]{1,0:T(8,128)(2,1)S(1)}, bf16[272,128]{1,0:T(8,128)(2,1)S(1)}, u32[]{:S(2)}, u32[]{:S(2)}) %collective-permute-start.7) | collective-permute-done | bytes 69664 | tf_op jit(solution)/shard_map/ppermute | solution.py:309
  25.7 0.3 %collective-permute-done.8.refs_3_ = bf16[272,128]{1,0:T(8,128)(2,1)S(1)} collective-permute-done((bf16[272,128]{1,0:T(8,128)(2,1)S(1)}, bf16[272,128]{1,0:T(8,128)(2,1)S(1)}, u32[]{:S(2)}, u32[]{:S(2)}) %collective-permute-start.8) | collective-permute-done | bytes 69664 | tf_op jit(solution)/shard_map/ppermute | solution.py:309
  26.1 0.9 %shard_map.45 = f32[8,64,128]{2,1,0:T(8,128)} custom-call(s32[1]{0:T(128)} %bitcast.core_ref, f32[272,128]{1,0:T(8,128)S(1)} %get-tuple-element.35.refs_0_, bf16[272,128]{1,0:T(8,128)(2,1)S(1)} %collective-permute-done.6.refs_1_, bf16[272,128]{1,0:T(8,128)(2,1)S(1)} %collective-permute-done.7.refs_2_, bf16[272,128]{1,0:T(8,128)(2,1)S(1)} %collective-permute-done.8.refs_3_), custom_call_target="tpu_custom_call" | custom-call | tf_op jit(solution)/shard_map/pallas_call | solution.py:310
  (8 shorter events, 0.1 us)
Async XLA Ops:
  0.0 1.1 %copy-start = (bf16[8,2,16,3,512]{4,2,3,1,0:T(8,128)(2,1)S(1)}, bf16[8,2,16,3,512]{4,2,3,1,0:T(8,128)(2,1)}, u32[]{:S(2)}) copy-start(bf16[8,2,16,3,512]{4,2,3,1,0:T(8,128)(2,1)} %param.3) | copy-start | bytes 2359300
  1.2 7.9 %collective-permute-start.1 = (bf16[2,2,3,16,512]{4,3,2,1,0:T(8,128)(2,1)S(1)}, bf16[2,2,3,16,512]{4,3,2,1,0:T(8,128)(2,1)S(1)}, u32[]{:S(2)}, u32[]{:S(2)}) collective-permute-start(bf16[2,2,3,16,512]{4,3,2,1,0:T(8,128)(2,1)S(1)} %get-tuple-element.26), channel_id=1, source_target_pairs={{0,16},{4,20},{8,24},{12,28},{16,0},{20,4},{24,8},{28,12},{1,17},{... | collective-permute-start | bytes 589832 | tf_op jit(solution)/shard_map/ppermute | solution.py:236
  4.2 7.8 %collective-permute-start.2 = (bf16[2,2,3,16,512]{4,3,2,1,0:T(8,128)(2,1)S(1)}, bf16[2,2,3,16,512]{4,3,2,1,0:T(8,128)(2,1)S(1)}, u32[]{:S(2)}, u32[]{:S(2)}) collective-permute-start(bf16[2,2,3,16,512]{4,3,2,1,0:T(8,128)(2,1)S(1)} %get-tuple-element.27), channel_id=1, source_target_pairs={{0,8},{4,12},{8,0},{12,4},{16,24},{20,28},{24,16},{28,20},{1,9},{5... | collective-permute-start | bytes 589832 | tf_op jit(solution)/shard_map/ppermute | solution.py:236
  5.7 1.3 %collective-permute-start = (bf16[2,3,16,512]{3,2,1,0:T(8,128)(2,1)S(1)}, bf16[2,3,16,512]{3,2,1,0:T(8,128)(2,1)S(1)}, u32[]{:S(2)}, u32[]{:S(2)}) collective-permute-start(bf16[2,3,16,512]{3,2,1,0:T(8,128)(2,1)S(1)} %get-tuple-element.23), channel_id=1, source_target_pairs={{0,4},{4,0},{8,12},{12,8},{16,20},{20,16},{24,28},{28,24},{1,5},{5... | collective-permute-start | bytes 294920 | tf_op jit(solution)/shard_map/ppermute | solution.py:236
  5.7 8.9 %collective-permute-start.3 = (bf16[2,2,3,16,512]{4,3,2,1,0:T(8,128)(2,1)S(1)}, bf16[2,2,3,16,512]{4,3,2,1,0:T(8,128)(2,1)S(1)}, u32[]{:S(2)}, u32[]{:S(2)}) collective-permute-start(bf16[2,2,3,16,512]{4,3,2,1,0:T(8,128)(2,1)S(1)} %get-tuple-element.32), channel_id=1, source_target_pairs={{0,24},{4,28},{8,16},{12,20},{16,8},{20,12},{24,0},{28,4},{1,25},{... | collective-permute-start | bytes 589832 | tf_op jit(solution)/shard_map/ppermute | solution.py:236
  7.0 1.1 %copy-start.1 = (bf16[1,2,128,3,512]{4,2,3,1,0:T(8,128)(2,1)S(1)}, bf16[1,2,128,3,512]{4,2,3,1,0:T(8,128)(2,1)}, u32[]{:S(2)}) copy-start(bf16[1,2,128,3,512]{4,2,3,1,0:T(8,128)(2,1)} %param.4) | copy-start | bytes 2359300
  12.1 3.0 %collective-permute-start.4 = (bf16[2,2,3,16,512]{4,3,2,1,0:T(8,128)(2,1)S(1)}, bf16[2,2,3,16,512]{4,3,2,1,0:T(8,128)(2,1)S(1)}, u32[]{:S(2)}, u32[]{:S(2)}) collective-permute-start(bf16[2,2,3,16,512]{4,3,2,1,0:T(8,128)(2,1)S(1)} %shard_map.40), channel_id=1, source_target_pairs={{0,4},{4,0},{8,12},{12,8},{16,20},{20,16},{24,28},{28,24},{1,5},{5... | collective-permute-start | bytes 589832 | tf_op jit(solution)/shard_map/ppermute | solution.py:236
  14.6 1.4 %collective-permute-start.5 = (bf16[1,2,3,16,512]{4,3,2,1,0:T(8,128)(2,1)S(1)}, bf16[1,2,3,16,512]{4,3,2,1,0:T(8,128)(2,1)S(1)}, u32[]{:S(2)}, u32[]{:S(2)}) collective-permute-start(bf16[1,2,3,16,512]{4,3,2,1,0:T(8,128)(2,1)S(1)} %shard_map.43), channel_id=1, source_target_pairs={{0,4},{4,0},{8,12},{12,8},{16,20},{20,16},{24,28},{28,24},{1,5},{5... | collective-permute-start | bytes 294920 | tf_op jit(solution)/shard_map/ppermute | solution.py:236
  16.4 7.1 %collective-permute-start.6 = (bf16[272,128]{1,0:T(8,128)(2,1)S(1)}, bf16[272,128]{1,0:T(8,128)(2,1)S(1)}, u32[]{:S(2)}, u32[]{:S(2)}) collective-permute-start(bf16[272,128]{1,0:T(8,128)(2,1)S(1)} %get-tuple-element.36), channel_id=1, source_target_pairs={{0,2},{1,3},{2,0},{3,1},{4,6},{5,7},{6,4},{7,5},{8,10},{9,11},{10,... | collective-permute-start | bytes 208904 | tf_op jit(solution)/shard_map/ppermute | solution.py:309
  19.2 6.5 %collective-permute-start.7 = (bf16[272,128]{1,0:T(8,128)(2,1)S(1)}, bf16[272,128]{1,0:T(8,128)(2,1)S(1)}, u32[]{:S(2)}, u32[]{:S(2)}) collective-permute-start(bf16[272,128]{1,0:T(8,128)(2,1)S(1)} %get-tuple-element.37), channel_id=1, source_target_pairs={{0,3},{1,2},{2,1},{3,0},{4,7},{5,6},{6,5},{7,4},{8,11},{9,10},{10,... | collective-permute-start | bytes 208904 | tf_op jit(solution)/shard_map/ppermute | solution.py:309
  20.5 5.5 %collective-permute-start.8 = (bf16[272,128]{1,0:T(8,128)(2,1)S(1)}, bf16[272,128]{1,0:T(8,128)(2,1)S(1)}, u32[]{:S(2)}, u32[]{:S(2)}) collective-permute-start(bf16[272,128]{1,0:T(8,128)(2,1)S(1)} %get-tuple-element.38), channel_id=1, source_target_pairs={{0,1},{1,0},{2,3},{3,2},{4,5},{5,4},{6,7},{7,6},{8,9},{9,8},{10,11... | collective-permute-start | bytes 208904 | tf_op jit(solution)/shard_map/ppermute | solution.py:309

commit v6 on v5

--- a/solution.py
+++ b/solution.py
@@ -172,9 +172,9 @@
 
 def finish_kernel(group, core_ref, *refs):
     count = len(group)
-    parts, out_ref, done_ref, sems = refs[:-3], refs[-3], refs[-2], refs[-1]
+    parts, out_ref = refs[:-1], refs[-1]
     groups = max(group) + 1
-    rows = done_ref.shape[1] // 4
+    rows = out_ref.shape[1] // 4
     last = 4 * rows * groups
 
     def summed(at, size):
@@ -189,27 +189,19 @@
     mine = (lane == place) | (lane == place + 2 * rows)
     squares = jnp.sum(jnp.where(mine, both, 0.0), axis=1, keepdims=True)
     inverse = lax.rsqrt(squares + epsilon_norm)
-    copies = []
     for g in range(groups):
         for part in range(2):
             value = summed(2 * rows * (2 * g + part), 2 * rows) * inverse
             for other in range(2):
                 first = pl.multiple_of(jnp.bitwise_xor(core_ref[0], other) * (2 * rows), 2 * rows)
-                done_ref[g, pl.ds(first + part, rows, stride=2), :] = value[other * rows : (other + 1) * rows]
-        for m in range(count):
-            if group[m] == g:
-                copies.append(pltpu.make_async_copy(done_ref.at[g], out_ref.at[m], sems.at[m]))
-                copies[-1].start()
-    for copy in copies:
-        copy.wait()
+                half = value[other * rows : (other + 1) * rows]
+                for m in range(count):
+                    if group[m] == g:
+                        out_ref[m, pl.ds(first + part, rows, stride=2), :] = half
 
 
 def in_vmem(count):
     return [pl.BlockSpec(memory_space=pltpu.VMEM)] * count
-
-
-def anywhere(count):
-    return [pl.BlockSpec(memory_space=pl.ANY)] * count
 
 
 def scalar():
@@ -311,11 +303,7 @@
         functools.partial(finish_kernel, group),
         out_shape=jax.ShapeDtypeStruct((len(group), 2 * rows * 2, cols), jnp.float32),
         in_specs=scalar() + in_vmem(len(parts)),
-        out_specs=anywhere(1)[0],
-        scratch_shapes=[
-            pltpu.VMEM((groups, 2 * rows * 2, cols), jnp.float32),
-            pltpu.SemaphoreType.DMA((len(group),)),
-        ],
+        out_specs=in_vmem(1)[0],
         cost_estimate=small,
         compiler_params=params,
     )(core, *parts)

time: 27.2 us -> 27.1 us (level)
  no operation moved by 1% of the time
where the time goes in v6:
time: 27.1 us; the launch traced here: 26.9 us
  waiting for transfers between devices  11.7 us (43%)
  starting transfers between devices  9.1 us (34%)
  Pallas kernels  3.05 us (11%)
  local copies, waits for them, and re-layouts  2.98 us (11%)
    ppermute x6, waiting for transfers between devices, swapped(): return lax.ppermute(mine, 'tm', [(i, i ^ r) for i in range(tm)])  6.36 us
    ppermute x3, waiting for transfers between devices, per_device_permutes(): lax.ppermute(others[q - 1], 'space', [(i, i ^ q) for i in range(space)])  5.29 us
    ppermute x6, starting transfers between devices, swapped(): return lax.ppermute(mine, 'tm', [(i, i ^ r) for i in range(tm)])  4.72 us
    ppermute x3, starting transfers between devices, per_device_permutes(): lax.ppermute(others[q - 1], 'space', [(i, i ^ q) for i in range(space)])  4.38 us
    unnamed x4, local copies, waits for them, and re-layouts  2.27 us
    pallas_call x3, Pallas kernels, sums_of(): pl.pallas_call(functools.partial(sums_kernel, trivial, half), out_shape=j...  1.15 us
    pallas_call x1, Pallas kernels, per_device_permutes(): pl.pallas_call(functools.partial(finish_kernel, group), out_shape=jax.Sha...  0.81 us
    squeeze x1, local copies, waits for them, and re-layouts, per_device_permutes(): table = lax.dynamic_index_in_dim(jnp.asarray(tables), z, 0, keepdims=False)  0.72 us
  transfers between devices with their start and end apart: 9, of which 8 were waited for; matrix products, arithmetic and copies ran while one was open for 3% of the time, Pallas kernels for 7%

profile of v6, /device:TPU:0, one launch (start us, length us, event | category | flops | bytes accessed | tf_op | source)
XLA Modules:
  0.0 26.9 jit_solution(1152514721794056977)
XLA Ops:
  0.0 1.1 %copy-done = bf16[8,2,16,3,512]{4,2,3,1,0:T(8,128)(2,1)S(1)} copy-done((bf16[8,2,16,3,512]{4,2,3,1,0:T(8,128)(2,1)S(1)}, bf16[8,2,16,3,512]{4,2,3,1,0:T(8,128)(2,1)}, u32[]{:S(2)}) %copy-start) | copy-done | bytes 786456
  1.2 3.0 %collective-permute-start.1 = (bf16[2,2,3,16,512]{4,3,2,1,0:T(8,128)(2,1)S(1)}, bf16[2,2,3,16,512]{4,3,2,1,0:T(8,128)(2,1)S(1)}, u32[]{:S(2)}, u32[]{:S(2)}) collective-permute-start(bf16[2,2,3,16,512]{4,3,2,1,0:T(8,128)(2,1)S(1)} %get-tuple-element.26), channel_id=1, source_target_pairs={{0,16},{4,20},{8,24},{12,28},{16,0},{20,4},{24,8},{28,12},{1,17},{... | collective-permute-start | bytes 589832 | tf_op jit(solution)/shard_map/ppermute | solution.py:228
  4.2 1.5 %collective-permute-start.2 = (bf16[2,2,3,16,512]{4,3,2,1,0:T(8,128)(2,1)S(1)}, bf16[2,2,3,16,512]{4,3,2,1,0:T(8,128)(2,1)S(1)}, u32[]{:S(2)}, u32[]{:S(2)}) collective-permute-start(bf16[2,2,3,16,512]{4,3,2,1,0:T(8,128)(2,1)S(1)} %get-tuple-element.27), channel_id=1, source_target_pairs={{0,8},{4,12},{8,0},{12,4},{16,24},{20,28},{24,16},{28,20},{1,9},{5... | collective-permute-start | bytes 589832 | tf_op jit(solution)/shard_map/ppermute | solution.py:228
  5.8 0.7 %dynamic-slice_bitcast_fusion.tab_ref = f32[8,512]{1,0:T(8,128)S(1)} fusion(f32[4,8,512]{2,1,0:T(8,128)} %constant.40.clone, s32[]{:T(128)S(6)} %select_n.17), kind=kLoop, calls=%fused_computation | loop fusion | bytes 32772 | tf_op jit(solution)/shard_map/jit(dynamic_index_in_dim)/squeeze | solution.py:221
  6.5 0.5 %collective-permute-done.refs_1_ = bf16[2,3,16,512]{3,2,1,0:T(8,128)(2,1)S(1)} collective-permute-done((bf16[2,3,16,512]{3,2,1,0:T(8,128)(2,1)S(1)}, bf16[2,3,16,512]{3,2,1,0:T(8,128)(2,1)S(1)}, u32[]{:S(2)}, u32[]{:S(2)}) %collective-permute-start) | collective-permute-done | bytes 98336 | tf_op jit(solution)/shard_map/ppermute | solution.py:228
  7.0 1.1 %copy-done.1 = bf16[1,2,128,3,512]{4,2,3,1,0:T(8,128)(2,1)S(1)} copy-done((bf16[1,2,128,3,512]{4,2,3,1,0:T(8,128)(2,1)S(1)}, bf16[1,2,128,3,512]{4,2,3,1,0:T(8,128)(2,1)}, u32[]{:S(2)}) %copy-start.1) | copy-done | bytes 786456
  8.2 0.6 %shard_map.38 = (bf16[3,1024,256]{2,1,0:T(8,128)(2,1)S(1)}, f32[9,16,128]{2,1,0:T(8,128)S(1)}, f32[9,16,128]{2,1,0:T(8,128)S(1)}) custom-call(f32[8,512]{1,0:T(8,128)S(1)} %dynamic-slice_bitcast_fusion.tab_ref, bf16[2,3,128,512]{3,2,1,0:T(8,128)(2,1)S(1)} %bitcast.12, bf16[2,3,16,512]{3,2,1,0:T(8,128)(2,1)S(1)} %get-tuple-element.22.refs_0_, ...), custom_call_target="tpu_custom_call" | custom-call | tf_op jit(solution)/shard_map/pallas_call | solution.py:250
  8.8 0.4 %collective-permute-done.1.refs_0_ = bf16[2,2,3,16,512]{4,3,2,1,0:T(8,128)(2,1)S(1)} collective-permute-done((bf16[2,2,3,16,512]{4,3,2,1,0:T(8,128)(2,1)S(1)}, bf16[2,2,3,16,512]{4,3,2,1,0:T(8,128)(2,1)S(1)}, u32[]{:S(2)}, u32[]{:S(2)}) %collective-permute-start.1) | collective-permute-done | bytes 196640 | tf_op jit(solution)/shard_map/ppermute | solution.py:228
  9.1 2.9 %collective-permute-done.2.refs_1_ = bf16[2,2,3,16,512]{4,3,2,1,0:T(8,128)(2,1)S(1)} collective-permute-done((bf16[2,2,3,16,512]{4,3,2,1,0:T(8,128)(2,1)S(1)}, bf16[2,2,3,16,512]{4,3,2,1,0:T(8,128)(2,1)S(1)}, u32[]{:S(2)}, u32[]{:S(2)}) %collective-permute-start.2) | collective-permute-done | bytes 196640 | tf_op jit(solution)/shard_map/ppermute | solution.py:228
  12.1 0.1 collective-permute-start.4
  12.1 0.4 %shard_map.39.refs_2_ = f32[2,9,16,128]{3,2,1,0:T(8,128)S(1)} custom-call(s32[1]{0:T(128)} %bitcast.core_ref, f32[8,512]{1,0:T(8,128)S(1)} %dynamic-slice_bitcast_fusion.tab_ref, bf16[3,1024,256]{2,1,0:T(8,128)(2,1)S(1)} %get-tuple-element.24.r_ref, bf16[2,2,3,16,512]{4,3,2,1,0:T(8,128)(2,1)S(1)} %collective-permute-done.1.refs_0_, ...), custom_call_target="tpu_custom_call" | custom-call | tf_op jit(solution)/shard_map/pallas_call | solution.py:275
  12.5 2.1 %collective-permute-done.3.refs_0_ = bf16[2,2,3,16,512]{4,3,2,1,0:T(8,128)(2,1)S(1)} collective-permute-done((bf16[2,2,3,16,512]{4,3,2,1,0:T(8,128)(2,1)S(1)}, bf16[2,2,3,16,512]{4,3,2,1,0:T(8,128)(2,1)S(1)}, u32[]{:S(2)}, u32[]{:S(2)}) %collective-permute-start.3) | collective-permute-done | bytes 196640 | tf_op jit(solution)/shard_map/ppermute | solution.py:228
  14.6 0.1 collective-permute-start.5
  14.7 0.4 %shard_map.42.refs_4_ = f32[1,9,16,128]{3,2,1,0:T(8,128)S(1)} custom-call(s32[1]{0:T(128)} %bitcast.core_ref, f32[8,512]{1,0:T(8,128)S(1)} %dynamic-slice_bitcast_fusion.tab_ref, bf16[3,1024,256]{2,1,0:T(8,128)(2,1)S(1)} %get-tuple-element.24.r_ref, bf16[2,2,3,16,512]{4,3,2,1,0:T(8,128)(2,1)S(1)} %collective-permute-done.3.refs_0_), custom_call_target="tpu_custom_call" | custom-call | tf_op jit(solution)/shard_map/pallas_call | solution.py:275
  15.1 0.4 %shard_map.41.refs_3_ = f32[2,9,16,128]{3,2,1,0:T(8,128)S(1)} custom-call(s32[1]{0:T(128)} %bitcast.core_ref, f32[8,512]{1,0:T(8,128)S(1)} %dynamic-slice_bitcast_fusion.tab_ref, bf16[3,1024,256]{2,1,0:T(8,128)(2,1)S(1)} %get-tuple-element.24.r_ref, bf16[2,2,3,16,512]{4,3,2,1,0:T(8,128)(2,1)S(1)} %collective-permute-done.4.refs_0_), custom_call_target="tpu_custom_call" | custom-call | tf_op jit(solution)/shard_map/pallas_call | solution.py:275
  15.5 0.5 %collective-permute-done.5.refs_5_ = bf16[1,2,3,16,512]{4,3,2,1,0:T(8,128)(2,1)S(1)} collective-permute-done((bf16[1,2,3,16,512]{4,3,2,1,0:T(8,128)(2,1)S(1)}, bf16[1,2,3,16,512]{4,3,2,1,0:T(8,128)(2,1)S(1)}, u32[]{:S(2)}, u32[]{:S(2)}) %collective-permute-start.5) | collective-permute-done | bytes 98336 | tf_op jit(solution)/shard_map/ppermute | solution.py:228
  16.0 0.4 %shard_map.44 = (f32[272,128]{1,0:T(8,128)S(1)}, bf16[272,128]{1,0:T(8,128)(2,1)S(1)}, bf16[272,128]{1,0:T(8,128)(2,1)S(1)}, bf16[272,128]{1,0:T(8,128)(2,1)S(1)}) custom-call(s32[1]{0:T(128)} %bitcast.1.where_ref, f32[8,512]{1,0:T(8,128)S(1)} %dynamic-slice_bitcast_fusion.tab_ref, bf16[3,1024,256]{2,1,0:T(8,128)(2,1)S(1)} %get-tuple-element.24.r_ref, ...), custom_call_target="tpu_custom_call" | custom-call | tf_op jit(solution)/shard_map/pallas_call | solution.py:290
  16.4 2.8 %collective-permute-start.6 = (bf16[272,128]{1,0:T(8,128)(2,1)S(1)}, bf16[272,128]{1,0:T(8,128)(2,1)S(1)}, u32[]{:S(2)}, u32[]{:S(2)}) collective-permute-start(bf16[272,128]{1,0:T(8,128)(2,1)S(1)} %get-tuple-element.36), channel_id=1, source_target_pairs={{0,2},{1,3},{2,0},{3,1},{4,6},{5,7},{6,4},{7,5},{8,10},{9,11},{10,... | collective-permute-start | bytes 208904 | tf_op jit(solution)/shard_map/ppermute | solution.py:301
  19.2 1.4 %collective-permute-start.7 = (bf16[272,128]{1,0:T(8,128)(2,1)S(1)}, bf16[272,128]{1,0:T(8,128)(2,1)S(1)}, u32[]{:S(2)}, u32[]{:S(2)}) collective-permute-start(bf16[272,128]{1,0:T(8,128)(2,1)S(1)} %get-tuple-element.37), channel_id=1, source_target_pairs={{0,3},{1,2},{2,1},{3,0},{4,7},{5,6},{6,5},{7,4},{8,11},{9,10},{10,... | collective-permute-start | bytes 208904 | tf_op jit(solution)/shard_map/ppermute | solution.py:301
  20.5 0.2 collective-permute-start.8
  20.8 2.7 %collective-permute-done.6.refs_1_ = bf16[272,128]{1,0:T(8,128)(2,1)S(1)} collective-permute-done((bf16[272,128]{1,0:T(8,128)(2,1)S(1)}, bf16[272,128]{1,0:T(8,128)(2,1)S(1)}, u32[]{:S(2)}, u32[]{:S(2)}) %collective-permute-start.6) | collective-permute-done | bytes 69664 | tf_op jit(solution)/shard_map/ppermute | solution.py:301
  23.4 2.3 %collective-permute-done.7.refs_2_ = bf16[272,128]{1,0:T(8,128)(2,1)S(1)} collective-permute-done((bf16[272,128]{1,0:T(8,128)(2,1)S(1)}, bf16[272,128]{1,0:T(8,128)(2,1)S(1)}, u32[]{:S(2)}, u32[]{:S(2)}) %collective-permute-start.7) | collective-permute-done | bytes 69664 | tf_op jit(solution)/shard_map/ppermute | solution.py:301
  25.7 0.3 %collective-permute-done.8.refs_3_ = bf16[272,128]{1,0:T(8,128)(2,1)S(1)} collective-permute-done((bf16[272,128]{1,0:T(8,128)(2,1)S(1)}, bf16[272,128]{1,0:T(8,128)(2,1)S(1)}, u32[]{:S(2)}, u32[]{:S(2)}) %collective-permute-start.8) | collective-permute-done | bytes 69664 | tf_op jit(solution)/shard_map/ppermute | solution.py:301
  26.1 0.8 %shard_map.45 = f32[8,64,128]{2,1,0:T(8,128)} custom-call(s32[1]{0:T(128)} %bitcast.core_ref, f32[272,128]{1,0:T(8,128)S(1)} %get-tuple-element.35.refs_0_, bf16[272,128]{1,0:T(8,128)(2,1)S(1)} %collective-permute-done.6.refs_1_, bf16[272,128]{1,0:T(8,128)(2,1)S(1)} %collective-permute-done.7.refs_2_, bf16[272,128]{1,0:T(8,128)(2,1)S(1)} %collective-permute-done.8.refs_3_), custom_call_target="tpu_custom_call" | custom-call | tf_op jit(solution)/shard_map/pallas_call | solution.py:302
  (8 shorter events, 0.1 us)
Async XLA Ops:
  0.0 1.1 %copy-start = (bf16[8,2,16,3,512]{4,2,3,1,0:T(8,128)(2,1)S(1)}, bf16[8,2,16,3,512]{4,2,3,1,0:T(8,128)(2,1)}, u32[]{:S(2)}) copy-start(bf16[8,2,16,3,512]{4,2,3,1,0:T(8,128)(2,1)} %param.3) | copy-start | bytes 2359300
  1.2 7.9 %collective-permute-start.1 = (bf16[2,2,3,16,512]{4,3,2,1,0:T(8,128)(2,1)S(1)}, bf16[2,2,3,16,512]{4,3,2,1,0:T(8,128)(2,1)S(1)}, u32[]{:S(2)}, u32[]{:S(2)}) collective-permute-start(bf16[2,2,3,16,512]{4,3,2,1,0:T(8,128)(2,1)S(1)} %get-tuple-element.26), channel_id=1, source_target_pairs={{0,16},{4,20},{8,24},{12,28},{16,0},{20,4},{24,8},{28,12},{1,17},{... | collective-permute-start | bytes 589832 | tf_op jit(solution)/shard_map/ppermute | solution.py:228
  4.2 7.8 %collective-permute-start.2 = (bf16[2,2,3,16,512]{4,3,2,1,0:T(8,128)(2,1)S(1)}, bf16[2,2,3,16,512]{4,3,2,1,0:T(8,128)(2,1)S(1)}, u32[]{:S(2)}, u32[]{:S(2)}) collective-permute-start(bf16[2,2,3,16,512]{4,3,2,1,0:T(8,128)(2,1)S(1)} %get-tuple-element.27), channel_id=1, source_target_pairs={{0,8},{4,12},{8,0},{12,4},{16,24},{20,28},{24,16},{28,20},{1,9},{5... | collective-permute-start | bytes 589832 | tf_op jit(solution)/shard_map/ppermute | solution.py:228
  5.7 1.3 %collective-permute-start = (bf16[2,3,16,512]{3,2,1,0:T(8,128)(2,1)S(1)}, bf16[2,3,16,512]{3,2,1,0:T(8,128)(2,1)S(1)}, u32[]{:S(2)}, u32[]{:S(2)}) collective-permute-start(bf16[2,3,16,512]{3,2,1,0:T(8,128)(2,1)S(1)} %get-tuple-element.23), channel_id=1, source_target_pairs={{0,4},{4,0},{8,12},{12,8},{16,20},{20,16},{24,28},{28,24},{1,5},{5... | collective-permute-start | bytes 294920 | tf_op jit(solution)/shard_map/ppermute | solution.py:228
  5.7 8.9 %collective-permute-start.3 = (bf16[2,2,3,16,512]{4,3,2,1,0:T(8,128)(2,1)S(1)}, bf16[2,2,3,16,512]{4,3,2,1,0:T(8,128)(2,1)S(1)}, u32[]{:S(2)}, u32[]{:S(2)}) collective-permute-start(bf16[2,2,3,16,512]{4,3,2,1,0:T(8,128)(2,1)S(1)} %get-tuple-element.32), channel_id=1, source_target_pairs={{0,24},{4,28},{8,16},{12,20},{16,8},{20,12},{24,0},{28,4},{1,25},{... | collective-permute-start | bytes 589832 | tf_op jit(solution)/shard_map/ppermute | solution.py:228
  7.0 1.1 %copy-start.1 = (bf16[1,2,128,3,512]{4,2,3,1,0:T(8,128)(2,1)S(1)}, bf16[1,2,128,3,512]{4,2,3,1,0:T(8,128)(2,1)}, u32[]{:S(2)}) copy-start(bf16[1,2,128,3,512]{4,2,3,1,0:T(8,128)(2,1)} %param.4) | copy-start | bytes 2359300
  12.1 3.0 %collective-permute-start.4 = (bf16[2,2,3,16,512]{4,3,2,1,0:T(8,128)(2,1)S(1)}, bf16[2,2,3,16,512]{4,3,2,1,0:T(8,128)(2,1)S(1)}, u32[]{:S(2)}, u32[]{:S(2)}) collective-permute-start(bf16[2,2,3,16,512]{4,3,2,1,0:T(8,128)(2,1)S(1)} %shard_map.40), channel_id=1, source_target_pairs={{0,4},{4,0},{8,12},{12,8},{16,20},{20,16},{24,28},{28,24},{1,5},{5... | collective-permute-start | bytes 589832 | tf_op jit(solution)/shard_map/ppermute | solution.py:228
  14.6 1.4 %collective-permute-start.5 = (bf16[1,2,3,16,512]{4,3,2,1,0:T(8,128)(2,1)S(1)}, bf16[1,2,3,16,512]{4,3,2,1,0:T(8,128)(2,1)S(1)}, u32[]{:S(2)}, u32[]{:S(2)}) collective-permute-start(bf16[1,2,3,16,512]{4,3,2,1,0:T(8,128)(2,1)S(1)} %shard_map.43), channel_id=1, source_target_pairs={{0,4},{4,0},{8,12},{12,8},{16,20},{20,16},{24,28},{28,24},{1,5},{5... | collective-permute-start | bytes 294920 | tf_op jit(solution)/shard_map/ppermute | solution.py:228
  16.4 7.1 %collective-permute-start.6 = (bf16[272,128]{1,0:T(8,128)(2,1)S(1)}, bf16[272,128]{1,0:T(8,128)(2,1)S(1)}, u32[]{:S(2)}, u32[]{:S(2)}) collective-permute-start(bf16[272,128]{1,0:T(8,128)(2,1)S(1)} %get-tuple-element.36), channel_id=1, source_target_pairs={{0,2},{1,3},{2,0},{3,1},{4,6},{5,7},{6,4},{7,5},{8,10},{9,11},{10,... | collective-permute-start | bytes 208904 | tf_op jit(solution)/shard_map/ppermute | solution.py:301
  19.2 6.5 %collective-permute-start.7 = (bf16[272,128]{1,0:T(8,128)(2,1)S(1)}, bf16[272,128]{1,0:T(8,128)(2,1)S(1)}, u32[]{:S(2)}, u32[]{:S(2)}) collective-permute-start(bf16[272,128]{1,0:T(8,128)(2,1)S(1)} %get-tuple-element.37), channel_id=1, source_target_pairs={{0,3},{1,2},{2,1},{3,0},{4,7},{5,6},{6,5},{7,4},{8,11},{9,10},{10,... | collective-permute-start | bytes 208904 | tf_op jit(solution)/shard_map/ppermute | solution.py:301
  20.5 5.5 %collective-permute-start.8 = (bf16[272,128]{1,0:T(8,128)(2,1)S(1)}, bf16[272,128]{1,0:T(8,128)(2,1)S(1)}, u32[]{:S(2)}, u32[]{:S(2)}) collective-permute-start(bf16[272,128]{1,0:T(8,128)(2,1)S(1)} %get-tuple-element.38), channel_id=1, source_target_pairs={{0,1},{1,0},{2,3},{3,2},{4,5},{5,4},{6,7},{7,6},{8,9},{9,8},{10,11... | collective-permute-start | bytes 208904 | tf_op jit(solution)/shard_map/ppermute | solution.py:301

commit v7 on v6

--- a/solution.py
+++ b/solution.py
@@ -170,6 +170,13 @@
         out_ref[...] = acc_ref[jnp.bitwise_xor(where_ref[0], q)].astype(out_ref.dtype)
 
 
+def add_kernel(*refs):
+    total = refs[0][...]
+    for ref in refs[1:-1]:
+        total = total + ref[...].astype(jnp.float32)
+    refs[-1][...] = total
+
+
 def finish_kernel(group, core_ref, *refs):
     count = len(group)
     parts, out_ref = refs[:-1], refs[-1]
@@ -299,6 +306,15 @@
     parts = [own]
     for q in (2, 3, 1):
         parts.append(lax.ppermute(others[q - 1], "space", [(i, i ^ q) for i in range(space)]))
+    early_sum = pl.pallas_call(
+        add_kernel,
+        out_shape=payload(jnp.float32),
+        in_specs=in_vmem(len(parts) - 1),
+        out_specs=in_vmem(1)[0],
+        cost_estimate=small,
+        compiler_params=params,
+    )(*parts[:-1])
+    parts = [early_sum, parts[-1]]
     out = pl.pallas_call(
         functools.partial(finish_kernel, group),
         out_shape=jax.ShapeDtypeStruct((len(group), 2 * rows * 2, cols), jnp.float32),

time: 27.1 us -> 27.1 us (level)
  no operation moved by 1% of the time
where the time goes in v7:
time: 27.1 us; the launch traced here: 26.9 us
  waiting for transfers between devices  11.6 us (43%)
  starting transfers between devices  9.1 us (34%)
  Pallas kernels  3.07 us (11%)
  local copies, waits for them, and re-layouts  2.98 us (11%)
    ppermute x6, waiting for transfers between devices, swapped(): return lax.ppermute(mine, 'tm', [(i, i ^ r) for i in range(tm)])  6.36 us
    ppermute x3, waiting for transfers between devices, per_device_permutes(): lax.ppermute(others[q - 1], 'space', [(i, i ^ q) for i in range(space)])  5.26 us
    ppermute x6, starting transfers between devices, swapped(): return lax.ppermute(mine, 'tm', [(i, i ^ r) for i in range(tm)])  4.72 us
    ppermute x3, starting transfers between devices, per_device_permutes(): lax.ppermute(others[q - 1], 'space', [(i, i ^ q) for i in range(space)])  4.38 us
    unnamed x4, local copies, waits for them, and re-layouts  2.27 us
    pallas_call x3, Pallas kernels, sums_of(): pl.pallas_call(functools.partial(sums_kernel, trivial, half), out_shape=j...  1.15 us
    pallas_call x1, Pallas kernels, per_device_permutes(): pl.pallas_call(functools.partial(finish_kernel, group), out_shape=jax.Sha...  0.81 us
    squeeze x1, local copies, waits for them, and re-layouts, per_device_permutes(): table = lax.dynamic_index_in_dim(jnp.asarray(tables), z, 0, keepdims=False)  0.72 us
  transfers between devices with their start and end apart: 9, of which 8 were waited for; matrix products, arithmetic and copies ran while one was open for 3% of the time, Pallas kernels for 7%

profile of v7, /device:TPU:0, one launch (start us, length us, event | category | flops | bytes accessed | tf_op | source)
XLA Modules:
  0.0 26.9 jit_solution(16181237146586170418)
XLA Ops:
  0.0 1.1 %copy-done = bf16[8,2,16,3,512]{4,2,3,1,0:T(8,128)(2,1)S(1)} copy-done((bf16[8,2,16,3,512]{4,2,3,1,0:T(8,128)(2,1)S(1)}, bf16[8,2,16,3,512]{4,2,3,1,0:T(8,128)(2,1)}, u32[]{:S(2)}) %copy-start) | copy-done | bytes 786456
  1.2 3.0 %collective-permute-start.1 = (bf16[2,2,3,16,512]{4,3,2,1,0:T(8,128)(2,1)S(1)}, bf16[2,2,3,16,512]{4,3,2,1,0:T(8,128)(2,1)S(1)}, u32[]{:S(2)}, u32[]{:S(2)}) collective-permute-start(bf16[2,2,3,16,512]{4,3,2,1,0:T(8,128)(2,1)S(1)} %get-tuple-element.26), channel_id=1, source_target_pairs={{0,16},{4,20},{8,24},{12,28},{16,0},{20,4},{24,8},{28,12},{1,17},{... | collective-permute-start | bytes 589832 | tf_op jit(solution)/shard_map/ppermute | solution.py:235
  4.2 1.5 %collective-permute-start.2 = (bf16[2,2,3,16,512]{4,3,2,1,0:T(8,128)(2,1)S(1)}, bf16[2,2,3,16,512]{4,3,2,1,0:T(8,128)(2,1)S(1)}, u32[]{:S(2)}, u32[]{:S(2)}) collective-permute-start(bf16[2,2,3,16,512]{4,3,2,1,0:T(8,128)(2,1)S(1)} %get-tuple-element.27), channel_id=1, source_target_pairs={{0,8},{4,12},{8,0},{12,4},{16,24},{20,28},{24,16},{28,20},{1,9},{5... | collective-permute-start | bytes 589832 | tf_op jit(solution)/shard_map/ppermute | solution.py:235
  5.8 0.7 %dynamic-slice_bitcast_fusion.tab_ref = f32[8,512]{1,0:T(8,128)S(1)} fusion(f32[4,8,512]{2,1,0:T(8,128)} %constant.40.clone, s32[]{:T(128)S(6)} %select_n.17), kind=kLoop, calls=%fused_computation | loop fusion | bytes 32772 | tf_op jit(solution)/shard_map/jit(dynamic_index_in_dim)/squeeze | solution.py:228
  6.5 0.5 %collective-permute-done.refs_1_ = bf16[2,3,16,512]{3,2,1,0:T(8,128)(2,1)S(1)} collective-permute-done((bf16[2,3,16,512]{3,2,1,0:T(8,128)(2,1)S(1)}, bf16[2,3,16,512]{3,2,1,0:T(8,128)(2,1)S(1)}, u32[]{:S(2)}, u32[]{:S(2)}) %collective-permute-start) | collective-permute-done | bytes 98336 | tf_op jit(solution)/shard_map/ppermute | solution.py:235
  7.0 1.1 %copy-done.1 = bf16[1,2,128,3,512]{4,2,3,1,0:T(8,128)(2,1)S(1)} copy-done((bf16[1,2,128,3,512]{4,2,3,1,0:T(8,128)(2,1)S(1)}, bf16[1,2,128,3,512]{4,2,3,1,0:T(8,128)(2,1)}, u32[]{:S(2)}) %copy-start.1) | copy-done | bytes 786456
  8.2 0.6 %shard_map.38 = (bf16[3,1024,256]{2,1,0:T(8,128)(2,1)S(1)}, f32[9,16,128]{2,1,0:T(8,128)S(1)}, f32[9,16,128]{2,1,0:T(8,128)S(1)}) custom-call(f32[8,512]{1,0:T(8,128)S(1)} %dynamic-slice_bitcast_fusion.tab_ref, bf16[2,3,128,512]{3,2,1,0:T(8,128)(2,1)S(1)} %bitcast.12, bf16[2,3,16,512]{3,2,1,0:T(8,128)(2,1)S(1)} %get-tuple-element.22.refs_0_, ...), custom_call_target="tpu_custom_call" | custom-call | tf_op jit(solution)/shard_map/pallas_call | solution.py:257
  8.8 0.4 %collective-permute-done.1.refs_0_ = bf16[2,2,3,16,512]{4,3,2,1,0:T(8,128)(2,1)S(1)} collective-permute-done((bf16[2,2,3,16,512]{4,3,2,1,0:T(8,128)(2,1)S(1)}, bf16[2,2,3,16,512]{4,3,2,1,0:T(8,128)(2,1)S(1)}, u32[]{:S(2)}, u32[]{:S(2)}) %collective-permute-start.1) | collective-permute-done | bytes 196640 | tf_op jit(solution)/shard_map/ppermute | solution.py:235
  9.1 2.9 %collective-permute-done.2.refs_1_ = bf16[2,2,3,16,512]{4,3,2,1,0:T(8,128)(2,1)S(1)} collective-permute-done((bf16[2,2,3,16,512]{4,3,2,1,0:T(8,128)(2,1)S(1)}, bf16[2,2,3,16,512]{4,3,2,1,0:T(8,128)(2,1)S(1)}, u32[]{:S(2)}, u32[]{:S(2)}) %collective-permute-start.2) | collective-permute-done | bytes 196640 | tf_op jit(solution)/shard_map/ppermute | solution.py:235
  12.1 0.1 collective-permute-start.4
  12.1 0.4 %shard_map.39.refs_2_ = f32[2,9,16,128]{3,2,1,0:T(8,128)S(1)} custom-call(s32[1]{0:T(128)} %bitcast.core_ref, f32[8,512]{1,0:T(8,128)S(1)} %dynamic-slice_bitcast_fusion.tab_ref, bf16[3,1024,256]{2,1,0:T(8,128)(2,1)S(1)} %get-tuple-element.24.r_ref, bf16[2,2,3,16,512]{4,3,2,1,0:T(8,128)(2,1)S(1)} %collective-permute-done.1.refs_0_, ...), custom_call_target="tpu_custom_call" | custom-call | tf_op jit(solution)/shard_map/pallas_call | solution.py:282
  12.5 2.1 %collective-permute-done.3.refs_0_ = bf16[2,2,3,16,512]{4,3,2,1,0:T(8,128)(2,1)S(1)} collective-permute-done((bf16[2,2,3,16,512]{4,3,2,1,0:T(8,128)(2,1)S(1)}, bf16[2,2,3,16,512]{4,3,2,1,0:T(8,128)(2,1)S(1)}, u32[]{:S(2)}, u32[]{:S(2)}) %collective-permute-start.3) | collective-permute-done | bytes 196640 | tf_op jit(solution)/shard_map/ppermute | solution.py:235
  14.6 0.1 collective-permute-start.5
  14.7 0.4 %shard_map.42.refs_4_ = f32[1,9,16,128]{3,2,1,0:T(8,128)S(1)} custom-call(s32[1]{0:T(128)} %bitcast.core_ref, f32[8,512]{1,0:T(8,128)S(1)} %dynamic-slice_bitcast_fusion.tab_ref, bf16[3,1024,256]{2,1,0:T(8,128)(2,1)S(1)} %get-tuple-element.24.r_ref, bf16[2,2,3,16,512]{4,3,2,1,0:T(8,128)(2,1)S(1)} %collective-permute-done.3.refs_0_), custom_call_target="tpu_custom_call" | custom-call | tf_op jit(solution)/shard_map/pallas_call | solution.py:282
  15.1 0.4 %shard_map.41.refs_3_ = f32[2,9,16,128]{3,2,1,0:T(8,128)S(1)} custom-call(s32[1]{0:T(128)} %bitcast.core_ref, f32[8,512]{1,0:T(8,128)S(1)} %dynamic-slice_bitcast_fusion.tab_ref, bf16[3,1024,256]{2,1,0:T(8,128)(2,1)S(1)} %get-tuple-element.24.r_ref, bf16[2,2,3,16,512]{4,3,2,1,0:T(8,128)(2,1)S(1)} %collective-permute-done.4.refs_0_), custom_call_target="tpu_custom_call" | custom-call | tf_op jit(solution)/shard_map/pallas_call | solution.py:282
  15.5 0.5 %collective-permute-done.5.refs_5_ = bf16[1,2,3,16,512]{4,3,2,1,0:T(8,128)(2,1)S(1)} collective-permute-done((bf16[1,2,3,16,512]{4,3,2,1,0:T(8,128)(2,1)S(1)}, bf16[1,2,3,16,512]{4,3,2,1,0:T(8,128)(2,1)S(1)}, u32[]{:S(2)}, u32[]{:S(2)}) %collective-permute-start.5) | collective-permute-done | bytes 98336 | tf_op jit(solution)/shard_map/ppermute | solution.py:235
  16.0 0.4 %shard_map.44 = (f32[272,128]{1,0:T(8,128)S(1)}, bf16[272,128]{1,0:T(8,128)(2,1)S(1)}, bf16[272,128]{1,0:T(8,128)(2,1)S(1)}, bf16[272,128]{1,0:T(8,128)(2,1)S(1)}) custom-call(s32[1]{0:T(128)} %bitcast.1.where_ref, f32[8,512]{1,0:T(8,128)S(1)} %dynamic-slice_bitcast_fusion.tab_ref, bf16[3,1024,256]{2,1,0:T(8,128)(2,1)S(1)} %get-tuple-element.24.r_ref, ...), custom_call_target="tpu_custom_call" | custom-call | tf_op jit(solution)/shard_map/pallas_call | solution.py:297
  16.4 2.8 %collective-permute-start.6 = (bf16[272,128]{1,0:T(8,128)(2,1)S(1)}, bf16[272,128]{1,0:T(8,128)(2,1)S(1)}, u32[]{:S(2)}, u32[]{:S(2)}) collective-permute-start(bf16[272,128]{1,0:T(8,128)(2,1)S(1)} %get-tuple-element.36), channel_id=1, source_target_pairs={{0,2},{1,3},{2,0},{3,1},{4,6},{5,7},{6,4},{7,5},{8,10},{9,11},{10,... | collective-permute-start | bytes 208904 | tf_op jit(solution)/shard_map/ppermute | solution.py:308
  19.2 1.4 %collective-permute-start.7 = (bf16[272,128]{1,0:T(8,128)(2,1)S(1)}, bf16[272,128]{1,0:T(8,128)(2,1)S(1)}, u32[]{:S(2)}, u32[]{:S(2)}) collective-permute-start(bf16[272,128]{1,0:T(8,128)(2,1)S(1)} %get-tuple-element.37), channel_id=1, source_target_pairs={{0,3},{1,2},{2,1},{3,0},{4,7},{5,6},{6,5},{7,4},{8,11},{9,10},{10,... | collective-permute-start | bytes 208904 | tf_op jit(solution)/shard_map/ppermute | solution.py:308
  20.5 0.2 collective-permute-start.8
  20.8 2.7 %collective-permute-done.6.refs_1_ = bf16[272,128]{1,0:T(8,128)(2,1)S(1)} collective-permute-done((bf16[272,128]{1,0:T(8,128)(2,1)S(1)}, bf16[272,128]{1,0:T(8,128)(2,1)S(1)}, u32[]{:S(2)}, u32[]{:S(2)}) %collective-permute-start.6) | collective-permute-done | bytes 69664 | tf_op jit(solution)/shard_map/ppermute | solution.py:308
  23.4 2.3 %collective-permute-done.7.refs_2_ = bf16[272,128]{1,0:T(8,128)(2,1)S(1)} collective-permute-done((bf16[272,128]{1,0:T(8,128)(2,1)S(1)}, bf16[272,128]{1,0:T(8,128)(2,1)S(1)}, u32[]{:S(2)}, u32[]{:S(2)}) %collective-permute-start.7) | collective-permute-done | bytes 69664 | tf_op jit(solution)/shard_map/ppermute | solution.py:308
  25.8 0.3 %collective-permute-done.8.refs_1_ = bf16[272,128]{1,0:T(8,128)(2,1)S(1)} collective-permute-done((bf16[272,128]{1,0:T(8,128)(2,1)S(1)}, bf16[272,128]{1,0:T(8,128)(2,1)S(1)}, u32[]{:S(2)}, u32[]{:S(2)}) %collective-permute-start.8) | collective-permute-done | bytes 69664 | tf_op jit(solution)/shard_map/ppermute | solution.py:308
  26.1 0.8 %shard_map.46 = f32[8,64,128]{2,1,0:T(8,128)} custom-call(s32[1]{0:T(128)} %bitcast.core_ref, f32[272,128]{1,0:T(8,128)S(1)} %shard_map.45.refs_0_, bf16[272,128]{1,0:T(8,128)(2,1)S(1)} %collective-permute-done.8.refs_1_), custom_call_target="tpu_custom_call" | custom-call | tf_op jit(solution)/shard_map/pallas_call | solution.py:318
  (9 shorter events, 0.2 us)
Async XLA Ops:
  0.0 1.1 %copy-start = (bf16[8,2,16,3,512]{4,2,3,1,0:T(8,128)(2,1)S(1)}, bf16[8,2,16,3,512]{4,2,3,1,0:T(8,128)(2,1)}, u32[]{:S(2)}) copy-start(bf16[8,2,16,3,512]{4,2,3,1,0:T(8,128)(2,1)} %param.3) | copy-start | bytes 2359300
  1.2 7.9 %collective-permute-start.1 = (bf16[2,2,3,16,512]{4,3,2,1,0:T(8,128)(2,1)S(1)}, bf16[2,2,3,16,512]{4,3,2,1,0:T(8,128)(2,1)S(1)}, u32[]{:S(2)}, u32[]{:S(2)}) collective-permute-start(bf16[2,2,3,16,512]{4,3,2,1,0:T(8,128)(2,1)S(1)} %get-tuple-element.26), channel_id=1, source_target_pairs={{0,16},{4,20},{8,24},{12,28},{16,0},{20,4},{24,8},{28,12},{1,17},{... | collective-permute-start | bytes 589832 | tf_op jit(solution)/shard_map/ppermute | solution.py:235
  4.2 7.8 %collective-permute-start.2 = (bf16[2,2,3,16,512]{4,3,2,1,0:T(8,128)(2,1)S(1)}, bf16[2,2,3,16,512]{4,3,2,1,0:T(8,128)(2,1)S(1)}, u32[]{:S(2)}, u32[]{:S(2)}) collective-permute-start(bf16[2,2,3,16,512]{4,3,2,1,0:T(8,128)(2,1)S(1)} %get-tuple-element.27), channel_id=1, source_target_pairs={{0,8},{4,12},{8,0},{12,4},{16,24},{20,28},{24,16},{28,20},{1,9},{5... | collective-permute-start | bytes 589832 | tf_op jit(solution)/shard_map/ppermute | solution.py:235
  5.7 1.3 %collective-permute-start = (bf16[2,3,16,512]{3,2,1,0:T(8,128)(2,1)S(1)}, bf16[2,3,16,512]{3,2,1,0:T(8,128)(2,1)S(1)}, u32[]{:S(2)}, u32[]{:S(2)}) collective-permute-start(bf16[2,3,16,512]{3,2,1,0:T(8,128)(2,1)S(1)} %get-tuple-element.23), channel_id=1, source_target_pairs={{0,4},{4,0},{8,12},{12,8},{16,20},{20,16},{24,28},{28,24},{1,5},{5... | collective-permute-start | bytes 294920 | tf_op jit(solution)/shard_map/ppermute | solution.py:235
  5.7 8.9 %collective-permute-start.3 = (bf16[2,2,3,16,512]{4,3,2,1,0:T(8,128)(2,1)S(1)}, bf16[2,2,3,16,512]{4,3,2,1,0:T(8,128)(2,1)S(1)}, u32[]{:S(2)}, u32[]{:S(2)}) collective-permute-start(bf16[2,2,3,16,512]{4,3,2,1,0:T(8,128)(2,1)S(1)} %get-tuple-element.32), channel_id=1, source_target_pairs={{0,24},{4,28},{8,16},{12,20},{16,8},{20,12},{24,0},{28,4},{1,25},{... | collective-permute-start | bytes 589832 | tf_op jit(solution)/shard_map/ppermute | solution.py:235
  7.0 1.1 %copy-start.1 = (bf16[1,2,128,3,512]{4,2,3,1,0:T(8,128)(2,1)S(1)}, bf16[1,2,128,3,512]{4,2,3,1,0:T(8,128)(2,1)}, u32[]{:S(2)}) copy-start(bf16[1,2,128,3,512]{4,2,3,1,0:T(8,128)(2,1)} %param.4) | copy-start | bytes 2359300
  12.1 3.0 %collective-permute-start.4 = (bf16[2,2,3,16,512]{4,3,2,1,0:T(8,128)(2,1)S(1)}, bf16[2,2,3,16,512]{4,3,2,1,0:T(8,128)(2,1)S(1)}, u32[]{:S(2)}, u32[]{:S(2)}) collective-permute-start(bf16[2,2,3,16,512]{4,3,2,1,0:T(8,128)(2,1)S(1)} %shard_map.40), channel_id=1, source_target_pairs={{0,4},{4,0},{8,12},{12,8},{16,20},{20,16},{24,28},{28,24},{1,5},{5... | collective-permute-start | bytes 589832 | tf_op jit(solution)/shard_map/ppermute | solution.py:235
  14.6 1.4 %collective-permute-start.5 = (bf16[1,2,3,16,512]{4,3,2,1,0:T(8,128)(2,1)S(1)}, bf16[1,2,3,16,512]{4,3,2,1,0:T(8,128)(2,1)S(1)}, u32[]{:S(2)}, u32[]{:S(2)}) collective-permute-start(bf16[1,2,3,16,512]{4,3,2,1,0:T(8,128)(2,1)S(1)} %shard_map.43), channel_id=1, source_target_pairs={{0,4},{4,0},{8,12},{12,8},{16,20},{20,16},{24,28},{28,24},{1,5},{5... | collective-permute-start | bytes 294920 | tf_op jit(solution)/shard_map/ppermute | solution.py:235
  16.4 7.1 %collective-permute-start.6 = (bf16[272,128]{1,0:T(8,128)(2,1)S(1)}, bf16[272,128]{1,0:T(8,128)(2,1)S(1)}, u32[]{:S(2)}, u32[]{:S(2)}) collective-permute-start(bf16[272,128]{1,0:T(8,128)(2,1)S(1)} %get-tuple-element.36), channel_id=1, source_target_pairs={{0,2},{1,3},{2,0},{3,1},{4,6},{5,7},{6,4},{7,5},{8,10},{9,11},{10,... | collective-permute-start | bytes 208904 | tf_op jit(solution)/shard_map/ppermute | solution.py:308
  19.2 6.5 %collective-permute-start.7 = (bf16[272,128]{1,0:T(8,128)(2,1)S(1)}, bf16[272,128]{1,0:T(8,128)(2,1)S(1)}, u32[]{:S(2)}, u32[]{:S(2)}) collective-permute-start(bf16[272,128]{1,0:T(8,128)(2,1)S(1)} %get-tuple-element.37), channel_id=1, source_target_pairs={{0,3},{1,2},{2,1},{3,0},{4,7},{5,6},{6,5},{7,4},{8,11},{9,10},{10,... | collective-permute-start | bytes 208904 | tf_op jit(solution)/shard_map/ppermute | solution.py:308
  20.5 5.5 %collective-permute-start.8 = (bf16[272,128]{1,0:T(8,128)(2,1)S(1)}, bf16[272,128]{1,0:T(8,128)(2,1)S(1)}, u32[]{:S(2)}, u32[]{:S(2)}) collective-permute-start(bf16[272,128]{1,0:T(8,128)(2,1)S(1)} %get-tuple-element.38), channel_id=1, source_target_pairs={{0,1},{1,0},{2,3},{3,2},{4,5},{5,4},{6,7},{7,6},{8,9},{9,8},{10,11... | collective-permute-start | bytes 208904 | tf_op jit(solution)/shard_map/ppermute | solution.py:308
